TPU v7x, 256 devices: a whole 4x4x8 slice. The times are simulated.
256 devices in a mesh: band: 32 (over z_hi, x, y), dom: 8 (over z_lo, core).
Axes of the slice: x: 4, y: 4, z: 8 (z_hi: 2, z_lo: 4; z = z_hi * 4 + z_lo), core: 2. Of those that a mesh axis runs over, the one named last changes fastest.
Arguments:
- states: bfloat16 [256, 48, 24, 128], P('band', 'dom'), may hold values from -8 to 8
- potential: float32 [48, 24, 128], P('dom'), may hold values from -2 to 0
- owners: int32 [2], replicated, may hold values from 0 to 31, as said below
Outputs:
- projected: bfloat16 [256, 48, 24, 128], P('band', 'dom')
Inputs may be any that keep to these rules, and one draw needn't show every extreme that they name: `owners`: 2 distinct band indices; the last band index is always among them.
All inputs are finite; a program needn't handle non-finite values.
Results may differ from a plain program's by a relative error of at most 0.0074.
Values may be sent and summed in bfloat16 or wider, within the bound.
No kernel may reach another device: no remote copies, remote signals or barrier semaphores. Data moves between devices by JAX's collectives and lax.ppermute only.
A program may use at most 192 MiB of HBM per device.

v0:
```python
import jax
import jax.numpy as jnp
from jax import lax
from jax.sharding import PartitionSpec as P

ROUNDS = 2


stencil_weights = (
    -5369.0 / 1800.0,
    12.0 / 7.0,
    -15.0 / 56.0,
    10.0 / 189.0,
    -1.0 / 112.0,
    2.0 / 1925.0,
    -1.0 / 16632.0,
)
filter_center = 6.0
filter_halfwidth = 5.0


def padded_2(cells, sides, width):
    for axis, dim in sides:
        count = lax.axis_size(axis)
        head = lax.slice_in_dim(cells, 0, width, axis=dim)
        tail = lax.slice_in_dim(cells, cells.shape[dim] - width, cells.shape[dim], axis=dim)
        cells = jnp.concatenate(
            [
                lax.ppermute(tail, axis, [(i, (i + 1) % count) for i in range(count)]),
                cells,
                lax.ppermute(head, axis, [((i + 1) % count, i) for i in range(count)]),
            ],
            axis=dim,
        )
    return cells


def spread_2(x, axis, root):
    mine = lax.axis_index(axis) == root
    return lax.psum(jnp.where(mine, x, jnp.zeros_like(x)), axis)


def hamiltonian(padded, potential):
    planes = padded.shape[1] - 12
    center = padded[:, 6 : 6 + planes]
    laplace = 3.0 * stencil_weights[0] * center
    for offset in range(1, 7):
        laplace = laplace + stencil_weights[offset] * (
            padded[:, 6 + offset : 6 + offset + planes]
            + padded[:, 6 - offset : 6 - offset + planes]
        )
    for axis_number in (2, 3):
        for offset in range(1, 7):
            laplace = laplace + stencil_weights[offset] * (
                jnp.roll(center, offset, axis=axis_number)
                + jnp.roll(center, -offset, axis=axis_number)
            )
    return -0.5 * laplace + potential * center


def filter_states(block, potential):
    padded = padded_2(block, (("dom", 1),), 6).astype(jnp.float32)
    center = block.astype(jnp.float32)
    first = ((hamiltonian(padded, potential) - filter_center * center) / filter_halfwidth).astype(
        jnp.bfloat16
    )
    padded_first = padded_2(first, (("dom", 1),), 6).astype(jnp.float32)
    first_wide = lax.optimization_barrier(first).astype(jnp.float32)
    second = (
        2.0 * (hamiltonian(padded_first, potential) - filter_center * first_wide) / filter_halfwidth
        - center
    )
    return second.astype(jnp.bfloat16)


def on_device(states, potential, owners):
    count = states.shape[0]
    weight = 1.0 / float(states.shape[1] * lax.axis_size("dom") * states.shape[2] * states.shape[3])
    resident = filter_states(states, potential)
    spread = [spread_2(resident, "band", owners[turn_index]) for turn_index in range(ROUNDS)]
    block_zero = spread[0].reshape(count, -1)
    block_one = spread[1].reshape(count, -1)
    flat_states = resident.reshape(count, -1)
    block_zero_wide = block_zero.astype(jnp.float32)
    block_one_wide = block_one.astype(jnp.float32)
    contract = (((1,), (1,)), ((), ()))
    part_one = lax.dot_general(
        block_zero, flat_states, contract, preferred_element_type=jnp.float32
    )
    coef_one = weight * lax.psum(part_one, "dom")
    after_one = flat_states.astype(jnp.float32) - jnp.dot(
        coef_one.T, block_zero_wide, precision=lax.Precision.HIGHEST
    )
    part_two = lax.dot_general(block_one_wide, after_one, contract, precision=lax.Precision.HIGHEST)
    coef_two = weight * lax.psum(part_two, "dom")
    result = after_one - jnp.dot(coef_two.T, block_one_wide, precision=lax.Precision.HIGHEST)
    return result.astype(jnp.bfloat16).reshape(states.shape)


def solution(mesh):
    return jax.shard_map(
        on_device,
        mesh=mesh,
        in_specs=(P("band", "dom", None, None), P("dom", None, None), P()),
        out_specs=P("band", "dom", None, None),
        check_vma=False,
    )
```

profile of v0, /device:TPU:1, one launch (start us, length us, event | category | flops | bytes accessed | tf_op | source)
XLA Modules:
  0.0 514.4 jit_solution(12774175899071616326)
XLA Ops:
  6.5 3.2 collective-permute-start.1
  9.8 4.4 collective-permute-done.1
  14.4 1.1 maximum_convert_fusion
  15.4 0.7 fusion.117
  16.1 0.7 fusion.119
  16.8 0.7 fusion.121
  17.6 0.8 fusion.123
  18.3 0.8 fusion.125
  22.3 0.9 copy-done
  23.2 0.7 maximum_convert_fusion.5
  23.8 5.5 %fusion.3 = bf16[8,6,24,128]{3,2,1,0:T(8,128)(2,1)S(1)} fusion(bf16[8,6,24,128]{3,2,1,0:T(8,128)(2,1)S(1)} %copy-done, f32[8,6,24,6]{3,2,1,0:T(8,128)S(1)} %get-tuple-element.98, f32[8,6,24,122]{3,2,1,0:T(8,128)S(1)} %get-tuple-element.100, f32[8,6,24,122]{3,2,1,0:T(8,128)S(1)} %get-tuple-element.99, f32[8,6,24,6]{3,2,1,0:T(8,128)S(1)} %get-tuple-element.97, ...), kind=kLoop, calls=%fused_computation.10 | loop fusion | flops 12828672 | bytes 22487040 | tf_op jit(solution)/shard_map/convert_element_type | solution.py:64
  29.3 6.5 %collective-permute-start.3 = (bf16[8,6,24,128]{3,2,1,0:T(8,128)(2,1)S(1)}, bf16[8,6,24,128]{3,2,1,0:T(8,128)(2,1)S(1)}, u32[]{:S(2)}, u32[]{:S(2)}) collective-permute-start(bf16[8,6,24,128]{3,2,1,0:T(8,128)(2,1)S(1)} %fusion.3), channel_id=1, source_target_pairs={{1,0},{2,1},{3,2},{4,3},{5,4},{6,5},{7,6},{0,7},{9,8},{10,9},{11,1... | collective-permute-start | bytes 884744 | tf_op jit(solution)/shard_map/ppermute | solution.py:31
  35.8 0.6 fusion.139
  37.8 4.4 collective-permute-done.2
  42.3 0.7 fusion.94
  43.0 0.7 fusion.96
  43.7 0.7 fusion.98
  44.4 0.7 fusion.100
  45.2 0.8 fusion.102
  49.0 0.9 fusion.103
  49.9 0.6 maximum_convert_fusion.3
  50.6 5.6 %broadcast_select_fusion = (bf16[8,6,24,128]{3,2,1,0:T(8,128)(2,1)S(1)}, bf16[8,6,24,128]{3,2,1,0:T(8,128)(2,1)S(1)}) fusion(pred[]{:T(512)S(6)} %eq.7, bf16[8,6,24,128]{3,2,1,0:T(8,128)(2,1)S(1)} %copy-done, bf16[8,6,24,128]{3,2,1,0:T(8,128)(2,1)S(1)} %fusion.3, f32[6,24,128]{2,1,0:T(8,128)S(1)} %copy-done.2, f32[8,6,24,6]{3,2,1,0:T(8,128)S(1)} %get-tuple-element.52, ...), kind=kLoop, calls=%fused_computation.130 | loop fusion | flops 13271040 | bytes 23076864 | tf_op jit(solution)/shard_map/jit(_where)/select_n | solution.py:40
  56.2 0.8 copy.21
  57.0 0.7 broadcast_select_fusion.1
  57.8 399.4 %all-reduce.3.cloned.1.call-done = (bf16[8,6,24,128]{3,2,1,0:T(8,128)(2,1)}, bf16[8,18432]{1,0:T(8,128)(2,1)}) async-done(((bf16[8,6,24,128]{3,2,1,0:T(8,128)(2,1)}, bf16[8,18432]{1,0:T(8,128)(2,1)}), (bf16[8,6,24,128]{3,2,1,0:T(8,128)(2,1)}, bf16[8,18432]{1,0:T(8,128)(2,1)})) %all-reduce.3.cloned.1.call-update) | async-done | bytes 589840 | tf_op jit(solution)/shard_map/psum | solution.py:40
  457.2 1.3 convolution_bitcast_fusion
  458.5 32.0 %psum.29 = f32[8,8]{1,0:T(8,128)S(1)} all-reduce(f32[8,8]{1,0:T(8,128)S(1)} %convolution_bitcast_fusion), channel_id=1, replica_groups=mesh['band'=32,'dom'=8] {'dom'}, use_global_device_ids=true, to_apply=%region_1.2 | all-reduce | flops 64 | bytes 512 | tf_op jit(solution)/shard_map/psum | solution.py:90
  490.5 1.5 convolution_subtract_fusion.1
  492.0 0.7 fusion.140
  492.7 13.6 %psum.31 = f32[8,8]{1,0:T(8,128)S(1)} all-reduce(f32[8,8]{1,0:T(8,128)S(1)} %fusion.140), channel_id=1, replica_groups=mesh['band'=32,'dom'=8] {'dom'}, use_global_device_ids=true, to_apply=%region_3.4 | all-reduce | flops 64 | bytes 512 | tf_op jit(solution)/shard_map/psum | solution.py:95
  506.4 0.5 fusion
  506.8 0.8 copy.4
  (50 shorter events, 6.6 us)
Async XLA Ops:
  6.5 450.7 %all-reduce.3.cloned.1.call-start = ((), (), s32[]{:S(2)}) async-start(), calls=%async_computation | async-start | bytes 1179648 | tf_op jit(solution)/shard_map/psum | solution.py:40
  6.5 7.6 %collective-permute-start.1 = (bf16[8,6,24,128]{3,2,1,0:T(8,128)(2,1)}, bf16[8,6,24,128]{3,2,1,0:T(8,128)(2,1)S(1)}, u32[]{:S(2)}, u32[]{:S(2)}) collective-permute-start(bf16[8,6,24,128]{3,2,1,0:T(8,128)(2,1)} %param.3), channel_id=1, source_target_pairs={{1,0},{2,1},{3,2},{4,3},{5,4},{6,5},{7,6},{0,7},{9,8},{10,9},{11,1... | collective-permute-start | bytes 884744 | tf_op jit(solution)/shard_map/ppermute | solution.py:31
  9.8 4.6 collective-permute-start
  22.2 1.0 copy-start
  23.8 12.0 %copy-start.3 = (s32[2]{0:T(128)S(1)}, s32[2]{0:T(128)}, u32[]{:S(2)}) copy-start(s32[2]{0:T(128)} %param.5) | copy-start | bytes 28
  29.3 8.4 %collective-permute-start.3 = (bf16[8,6,24,128]{3,2,1,0:T(8,128)(2,1)S(1)}, bf16[8,6,24,128]{3,2,1,0:T(8,128)(2,1)S(1)}, u32[]{:S(2)}, u32[]{:S(2)}) collective-permute-start(bf16[8,6,24,128]{3,2,1,0:T(8,128)(2,1)S(1)} %fusion.3), channel_id=1, source_target_pairs={{1,0},{2,1},{3,2},{4,3},{5,4},{6,5},{7,6},{0,7},{9,8},{10,9},{11,1... | collective-permute-start | bytes 884744 | tf_op jit(solution)/shard_map/ppermute | solution.py:31
  35.8 6.4 %collective-permute-start.2 = (bf16[8,6,24,128]{3,2,1,0:T(8,128)(2,1)S(1)}, bf16[8,6,24,128]{3,2,1,0:T(8,128)(2,1)S(1)}, u32[]{:S(2)}, u32[]{:S(2)}) collective-permute-start(bf16[8,6,24,128]{3,2,1,0:T(8,128)(2,1)S(1)} %fusion.3), channel_id=1, source_target_pairs={{0,1},{1,2},{2,3},{3,4},{4,5},{5,6},{6,7},{7,0},{8,9},{9,10},{10,1... | collective-permute-start | bytes 884744 | tf_op jit(solution)/shard_map/ppermute | solution.py:29
  49.0 1.6 copy-start.2
  457.2 34.8 %copy-start.1 = (bf16[8,18432]{1,0:T(8,128)(2,1)S(1)}, bf16[8,18432]{1,0:T(8,128)(2,1)}, u32[]{:S(2)}) copy-start(bf16[8,18432]{1,0:T(8,128)(2,1)} %get-tuple-element.6) | copy-start | bytes 884740
Sparse Core Ops, SparseCore 0:
  57.9 399.2 all-reduce.2
where the time goes:
time: 515 us; the launch traced here: 514 us
  waiting for transfers between devices  408 us (79%)
  blocking collectives  45.6 us (9%)
  local copies, waits for them, and re-layouts  17.4 us (3%)
  between operations  14.9 us (3%)
  other arithmetic  14.4 us (3%)
  starting transfers between devices  9.71 us (2%)
    psum x1, waiting for transfers between devices, spread_2(): return lax.psum(jnp.where(mine, x, jnp.zeros_like(x)), axis)  399 us
    psum x1, blocking collectives, on_device(): coef_one = weight * lax.psum(part_one, 'dom')  32 us
    slice x46, local copies, waits for them, and re-layouts, hamiltonian(): jnp.roll(center, offset, axis=axis_number)  14.3 us
    psum x1, blocking collectives, on_device(): coef_two = weight * lax.psum(part_two, 'dom')  13.6 us
  transfers between devices with their start and end apart: 5, of which 4 were waited for; matrix products, arithmetic and copies ran while one was open for 0% of the time, Pallas kernels for 0%

commit v1 on v0

v1 whole, which is shorter than its diff:
```python
import functools

import jax
import jax.numpy as jnp
import numpy as np
from jax import lax
from jax.experimental import pallas as pl
from jax.experimental.pallas import tpu as pltpu
from jax.sharding import PartitionSpec as P

ROUNDS = 2
PLANE = 16

stencil_weights = (
    -5369.0 / 1800.0,
    12.0 / 7.0,
    -15.0 / 56.0,
    10.0 / 189.0,
    -1.0 / 112.0,
    2.0 / 1925.0,
    -1.0 / 16632.0,
)
filter_center = 6.0
filter_halfwidth = 5.0
bf16 = jnp.bfloat16
f32 = jnp.float32


def halves(matrix):
    matrix = matrix.astype(np.float32)
    high = matrix.astype(bf16)
    low = (matrix - high.astype(np.float32)).astype(bf16)
    return high, low


def stencil_matrices(planes, ny, nx):
    scale = -0.5 / filter_halfwidth
    rows = planes * ny
    left = np.zeros((rows, 3 * rows), np.float64)
    for p in range(planes):
        for y in range(ny):
            for k in range(1, 7):
                for sign in (k, -k):
                    left[p * ny + y, (planes + p + sign) * ny + y] += scale * stencil_weights[k]
                    left[p * ny + y, (planes + p) * ny + (y + sign) % ny] += scale * stencil_weights[k]
    right = np.zeros((nx, nx), np.float64)
    for x in range(nx):
        for k in range(1, 7):
            for sign in (k, -k):
                right[(x + sign) % nx, x] += scale * stencil_weights[k]
    return np.concatenate(halves(left), axis=0), np.concatenate(halves(right), axis=1)


def apply_filter(before, center, after, potential, left, right):
    count, rows, nx = center.shape
    slabs = [jnp.concatenate([before[s], center[s], after[s]], axis=0) for s in range(count)]
    along_zy = jnp.dot(left, jnp.concatenate(slabs, axis=1), preferred_element_type=f32)
    along_zy = along_zy[:rows] + along_zy[rows:]
    along_x = jnp.dot(center.reshape(count * rows, nx), right, preferred_element_type=f32)
    along_x = (along_x[:, :nx] + along_x[:, nx:]).reshape(count, rows, nx)
    diagonal = (-1.5 * stencil_weights[0] - filter_center) / filter_halfwidth + potential * (1.0 / filter_halfwidth)
    return [
        along_zy[:, s * nx : (s + 1) * nx] + along_x[s] + diagonal * center[s].astype(f32) for s in range(count)
    ]


def first_kernel(before, center, after, potential, left, right, out):
    result = apply_filter(before[...], center[...], after[...], potential[...], left[...], right[...])
    for s, value in enumerate(result):
        out[s] = value.astype(bf16)


def second_kernel(before, center, after, states, potential, left, right, out):
    result = apply_filter(before[...], center[...], after[...], potential[...], left[...], right[...])
    for s, value in enumerate(result):
        out[s] = (2.0 * value - states[s].astype(f32)).astype(bf16)


def select_kernel(owners, pieces, out):
    for turn in range(ROUNDS):
        out[turn] = pieces[lax.rem(owners[turn], PLANE)]


def spread_kernel(owners, place, mine, other, out):
    for turn in range(ROUNDS):
        here = lax.div(owners[turn], PLANE) == place[0]
        value = jnp.where(here, mine[turn], other[turn])
        for target in range(PLANE):
            out[target, turn] = value


def total(value):
    return functools.reduce(lambda a, b: a + b, [value[r : r + 8] for r in range(0, value.shape[0], 8)])


def gram_kernel(gathered, resident, out):
    count, rows, nx = resident.shape
    half = gathered.shape[2]
    out[...] = jnp.zeros_like(out)

    def block(turn, s):
        return jnp.concatenate([gathered[2 * s, turn], gathered[2 * s + 1, turn]], axis=0).astype(f32)

    lines = []
    for turn, other in ((0, None), (1, None), (1, 0)):
        for i in range(count):
            mine = block(turn, i)
            entries = []
            for j in range(count):
                against = resident[j].astype(f32) if other is None else block(other, j)
                entries.append(jnp.sum(total(mine * against), axis=0, keepdims=True))
            lines.append(jnp.concatenate(entries, axis=0))
    for i, line in enumerate(lines):
        out[i] = jnp.sum(line, axis=1, keepdims=True) + jnp.zeros_like(line)


def project_kernel(weight, gram, gathered, resident, out):
    count, rows, nx = resident.shape
    one = [gram[i] * weight for i in range(count)]
    cross = [gram[2 * count + i] for i in range(count)]
    two = []
    for i in range(count):
        value = gram[count + i]
        for k in range(count):
            value = value - cross[i][k : k + 1, :] * one[k]
        two.append(value * weight)
    half = rows // 2
    for part in range(2):
        for j in range(count):
            value = resident[j].astype(f32)[part * half : (part + 1) * half]
            for i in range(count):
                value = value - one[i][j : j + 1] * gathered[2 * i + part, 0].astype(f32)
            for i in range(count):
                value = value - two[i][j : j + 1] * gathered[2 * i + part, 1].astype(f32)
            out[j, part * half : (part + 1) * half] = value.astype(bf16)


vmem = pl.BlockSpec(memory_space=pltpu.VMEM)
smem = pl.BlockSpec(memory_space=pltpu.SMEM)
params = pltpu.CompilerParams(vmem_limit_bytes=48 * 1024 * 1024)


def call(kernel, shape, dtype, specs, *operands, name):
    return pl.pallas_call(
        kernel,
        out_shape=jax.ShapeDtypeStruct(shape, dtype),
        in_specs=specs,
        out_specs=vmem,
        compiler_params=params,
        name=name,
    )(*operands)


def neighbours(cells):
    count = lax.axis_size("dom")
    ahead = [(i, (i + 1) % count) for i in range(count)]
    return lax.ppermute(cells, "dom", ahead), lax.ppermute(cells, "dom", [(b, a) for a, b in ahead])


def on_device(states, potential, owners):
    count, planes, ny, nx = states.shape
    rows = planes * ny
    weight = 1.0 / float(planes * lax.axis_size("dom") * ny * nx)
    bands = lax.axis_size("band")
    groups = [list(range(start, start + PLANE)) for start in range(0, bands, PLANE)]
    place = (lax.axis_index("band") // PLANE).astype(jnp.int32).reshape(1)
    left, right = stencil_matrices(planes, ny, nx)
    left, right = jnp.asarray(left), jnp.asarray(right)
    states = states.reshape(count, rows, nx)
    potential = potential.reshape(rows, nx)

    before, after = neighbours(states)
    first = call(
        first_kernel, states.shape, bf16, [vmem] * 6, before, states, after, potential, left, right, name="first"
    )
    before, after = neighbours(first)
    resident = call(
        second_kernel, states.shape, bf16, [vmem] * 7, before, first, after, states, potential, left, right,
        name="second",
    )
    half = count * rows // PLANE
    pieces = lax.all_to_all(resident.reshape(PLANE, half, nx), "band", 0, 0, axis_index_groups=groups)
    mine = call(select_kernel, (ROUNDS, half, nx), bf16, [smem, vmem], owners, pieces, name="select")
    other = lax.ppermute(mine, "band", [(i, (i + PLANE) % bands) for i in range(bands)])
    copies = call(
        spread_kernel, (PLANE, ROUNDS, half, nx), bf16, [smem, smem, vmem, vmem], owners, place, mine, other,
        name="spread",
    )
    gathered = lax.all_to_all(copies, "band", 0, 0, axis_index_groups=groups)
    gram = call(gram_kernel, (3 * count, count, nx), f32, [vmem, vmem], gathered, resident, name="gram")
    gram = lax.psum(gram[:, :, 0], "dom")
    gram = jnp.broadcast_to(gram[:, :, None], (3 * count, count, nx))
    result = call(
        functools.partial(project_kernel, weight), states.shape, bf16, [vmem] * 3, gram, gathered, resident,
        name="project",
    )
    return result.reshape(count, planes, ny, nx)


def solution(mesh):
    return jax.shard_map(
        on_device,
        mesh=mesh,
        in_specs=(P("band", "dom", None, None), P("dom", None, None), P()),
        out_specs=P("band", "dom", None, None),
        check_vma=False,
    )
```

time: 515 us -> 83.6 us (0.16)
  waiting for transfers between devices: 408 us -> 14.7 us
  between operations: 14.9 us -> 0.06 us
  other arithmetic: 14.4 us -> 0 us
  local copies, waits for them, and re-layouts: 17.4 us -> 3.94 us
  Pallas kernels: 0 us -> 5.39 us
    psum x1 -> x0, waiting for transfers between devices: 399 us -> none  [spread_2(): return lax.psum(jnp.where(mine, x, jnp.zeros_like(x)), axis)]
    all_to_all x0 -> x2, blocking collectives: none -> 26.7 us  [the longest x1 14.3 us: on_device(): lax.all_to_all(resident.reshape(PLANE, half, nx), 'band', 0, 0, axis_inde...]
    psum x2 -> x1, blocking collectives: 45.6 us -> 19.7 us  [on_device(): gram = lax.psum(gram[:, :, 0], 'dom')]
    slice x47 -> x1, local copies, waits for them, and re-layouts: 15 us -> 0.12 us  [on_device(): gram = lax.psum(gram[:, :, 0], 'dom')]
    convert_element_type x3 -> x0, other arithmetic: 6.72 us -> none  [the longest x1 5.51 us: filter_states(): ((hamiltonian(padded, potential) - filter_center * center) / filter_halfw...]
    select_n x2 -> x0, other arithmetic: 6.36 us -> none  [spread_2(): return lax.psum(jnp.where(mine, x, jnp.zeros_like(x)), axis)]
    ppermute x4 -> x5, waiting for transfers between devices: 8.96 us -> 14.7 us  [the longest x2 5.6 us: neighbours(): lax.ppermute(cells, 'dom', [(b, a) for a, b in ahead])]
    pallas_call x0 -> x6, Pallas kernels: none -> 5.39 us  [call(): pl.pallas_call(kernel, out_shape=jax.ShapeDtypeStruct(shape, dtype), in_s...]
  transfers between devices with their start and end apart: 5 -> 5, of which waited for: 4 -> 5; matrix products, arithmetic and copies ran while one was open for 0% -> 0% of each run, Pallas kernels for 0% -> 0%
where the time goes in v1:
time: 83.6 us; the launch traced here: 83.3 us
  blocking collectives  46.5 us (56%)
  waiting for transfers between devices  14.7 us (18%)
  starting transfers between devices  12.7 us (15%)
  Pallas kernels  5.39 us (6%)
  local copies, waits for them, and re-layouts  3.94 us (5%)
    psum x1, blocking collectives, on_device(): gram = lax.psum(gram[:, :, 0], 'dom')  19.7 us
    all_to_all x1, blocking collectives, on_device(): lax.all_to_all(resident.reshape(PLANE, half, nx), 'band', 0, 0, axis_inde...  14.3 us
    all_to_all x1, blocking collectives, on_device(): gathered = lax.all_to_all(copies, 'band', 0, 0, axis_index_groups=groups)  12.5 us
    ppermute x2, starting transfers between devices, neighbours(): lax.ppermute(cells, 'dom', [(b, a) for a, b in ahead])  9.7 us
    ppermute x2, waiting for transfers between devices, neighbours(): lax.ppermute(cells, 'dom', [(b, a) for a, b in ahead])  5.6 us
    pallas_call x6, Pallas kernels, call(): pl.pallas_call(kernel, out_shape=jax.ShapeDtypeStruct(shape, dtype), in_s...  5.39 us
    ppermute x2, waiting for transfers between devices, neighbours(): lax.ppermute(cells, 'dom', ahead)  5.33 us
    ppermute x1, waiting for transfers between devices, on_device(): lax.ppermute(mine, 'band', [(i, (i + PLANE) % bands) for i in range(bands)])  3.8 us
  transfers between devices with their start and end apart: 5, of which 5 were waited for; matrix products, arithmetic and copies ran while one was open for 0% of the time, Pallas kernels for 0%

profile of v1, /device:TPU:1, one launch (start us, length us, event | category | flops | bytes accessed | tf_op | source)
XLA Modules:
  0.0 83.3 jit_solution(7612629516574889298)
XLA Ops:
  0.0 3.2 %collective-permute-start.1 = (bf16[8,144,128]{2,1,0:T(8,128)(2,1)}, bf16[8,144,128]{2,1,0:T(8,128)(2,1)S(1)}, u32[]{:S(2)}, u32[]{:S(2)}) collective-permute-start(bf16[8,144,128]{2,1,0:T(8,128)(2,1)} %bitcast.8), channel_id=1, source_target_pairs={{1,0},{2,1},{3,2},{4,3},{5,4},{6,5},{7,6},{0,7},{9,8},{10,9},{11,1... | collective-permute-start | bytes 884744 | tf_op jit(solution)/shard_map/ppermute | solution.py:157
  3.2 0.0 collective-permute-start
  3.2 4.4 %collective-permute-done.1.after = bf16[8,144,128]{2,1,0:T(8,128)(2,1)S(1)} collective-permute-done((bf16[8,144,128]{2,1,0:T(8,128)(2,1)}, bf16[8,144,128]{2,1,0:T(8,128)(2,1)S(1)}, u32[]{:S(2)}, u32[]{:S(2)}) %collective-permute-start.1) | collective-permute-done | bytes 294944 | tf_op jit(solution)/shard_map/ppermute | solution.py:157
  7.6 0.2 collective-permute-done.before
  7.8 0.0 copy-start
  7.8 1.0 %copy-done = bf16[8,6,24,128]{3,2,1,0:T(8,128)(2,1)S(1)} copy-done((bf16[8,6,24,128]{3,2,1,0:T(8,128)(2,1)S(1)}, bf16[8,6,24,128]{3,2,1,0:T(8,128)(2,1)}, u32[]{:S(2)}) %copy-start) | copy-done | bytes 294936
  8.8 0.0 copy-start.2
  8.8 1.0 %copy-done.2 = bf16[288,432]{1,0:T(8,128)(2,1)S(1)} copy-done((bf16[288,432]{1,0:T(8,128)(2,1)S(1)}, bf16[288,432]{1,0:T(8,128)(2,1)}, u32[]{:S(2)}) %copy-start.2) | copy-done | bytes 248856
  9.7 0.9 %copy-done.4 = f32[6,24,128]{2,1,0:T(8,128)S(1)} copy-done((f32[6,24,128]{2,1,0:T(8,128)S(1)}, f32[6,24,128]{2,1,0:T(8,128)}, u32[]{:S(2)}) %copy-start.4) | copy-done | bytes 73752
  10.6 0.8 %copy-done.5 = bf16[128,256]{1,0:T(8,128)(2,1)S(1)} copy-done((bf16[128,256]{1,0:T(8,128)(2,1)S(1)}, bf16[128,256]{1,0:T(8,128)(2,1)}, u32[]{:S(2)}) %copy-start.5) | copy-done | bytes 65560
  11.5 0.6 first.1.center
  12.1 6.5 %collective-permute-start.3 = (bf16[8,144,128]{2,1,0:T(8,128)(2,1)S(1)}, bf16[8,144,128]{2,1,0:T(8,128)(2,1)S(1)}, u32[]{:S(2)}, u32[]{:S(2)}) collective-permute-start(bf16[8,144,128]{2,1,0:T(8,128)(2,1)S(1)} %first.1.center), channel_id=1, source_target_pairs={{1,0},{2,1},{3,2},{4,3},{5,4},{6,5},{7,6},{0,7},{9,8},{10,9},{11,1... | collective-permute-start | bytes 884744 | tf_op jit(solution)/shard_map/ppermute | solution.py:157
  18.6 0.0 collective-permute-start.2
  18.6 1.2 %collective-permute-done.3.after = bf16[8,144,128]{2,1,0:T(8,128)(2,1)S(1)} collective-permute-done((bf16[8,144,128]{2,1,0:T(8,128)(2,1)S(1)}, bf16[8,144,128]{2,1,0:T(8,128)(2,1)S(1)}, u32[]{:S(2)}, u32[]{:S(2)}) %collective-permute-start.3) | collective-permute-done | bytes 294944 | tf_op jit(solution)/shard_map/ppermute | solution.py:157
  19.8 5.2 %collective-permute-done.2.before = bf16[8,144,128]{2,1,0:T(8,128)(2,1)S(1)} collective-permute-done((bf16[8,144,128]{2,1,0:T(8,128)(2,1)S(1)}, bf16[8,144,128]{2,1,0:T(8,128)(2,1)S(1)}, u32[]{:S(2)}, u32[]{:S(2)}) %collective-permute-start.2) | collective-permute-done | bytes 294944 | tf_op jit(solution)/shard_map/ppermute | solution.py:157
  24.9 0.0 copy-done.1
  24.9 0.0 copy-done.3
  24.9 0.6 second.1.resident
  25.6 0.0 copy-start.6
  25.6 14.3 %all_to_all.10.pieces = bf16[16,72,128]{2,1,0:T(8,128)(2,1)S(1)} all-to-all(bf16[16,72,128]{2,1,0:T(8,128)(2,1)S(1)} %bitcast.7), channel_id=1, replica_groups={{0,8,16,24,32,40,48,56,64,72,80,88,96,104,112,120},{128,136,144,152,160..., dimensions={0} | all-to-all | bytes 589824 | tf_op jit(solution)/shard_map/all_to_all | solution.py:182
  39.9 0.0 copy-done.6
  39.9 0.6 select.5.mine
  40.4 3.0 %collective-permute-start.4 = (bf16[2,72,128]{2,1,0:T(8,128)(2,1)S(1)}, bf16[2,72,128]{2,1,0:T(8,128)(2,1)S(1)}, u32[]{:S(2)}, u32[]{:S(2)}) collective-permute-start(bf16[2,72,128]{2,1,0:T(8,128)(2,1)S(1)} %select.5.mine), channel_id=1, source_target_pairs={{0,128},{8,136},{16,144},{24,152},{32,160},{40,168},{48,176},{56,1... | collective-permute-start | bytes 110600 | tf_op jit(solution)/shard_map/ppermute | solution.py:184
  43.4 3.8 %collective-permute-done.4.other = bf16[2,72,128]{2,1,0:T(8,128)(2,1)S(1)} collective-permute-done((bf16[2,72,128]{2,1,0:T(8,128)(2,1)S(1)}, bf16[2,72,128]{2,1,0:T(8,128)(2,1)S(1)}, u32[]{:S(2)}, u32[]{:S(2)}) %collective-permute-start.4) | collective-permute-done | bytes 36896 | tf_op jit(solution)/shard_map/ppermute | solution.py:184
  47.2 0.6 spread.1
  47.9 12.5 %all_to_all.11.gathered = bf16[16,2,72,128]{3,2,1,0:T(8,128)(2,1)S(1)} all-to-all(bf16[16,2,72,128]{3,2,1,0:T(8,128)(2,1)S(1)} %spread.1), channel_id=1, replica_groups={{0,8,16,24,32,40,48,56,64,72,80,88,96,104,112,120},{128,136,144,152,160..., dimensions={0} | all-to-all | bytes 1179648 | tf_op jit(solution)/shard_map/all_to_all | solution.py:189
  60.3 1.2 %gram.1 = f32[24,8,128]{2,1,0:T(8,128)S(1)} custom-call(bf16[16,2,72,128]{3,2,1,0:T(8,128)(2,1)S(1)} %all_to_all.11.gathered, bf16[8,144,128]{2,1,0:T(8,128)(2,1)S(1)} %second.1.resident), custom_call_target="tpu_custom_call" | custom-call | tf_op jit(solution)/shard_map/gram/pallas_call | solution.py:144
  61.5 0.1 copy.6
  61.7 19.7 %psum.7 = f32[24,8]{0,1:T(8,128)S(1)} all-reduce(f32[24,8]{0,1:T(8,128)S(1)} %bitcast.15), channel_id=1, replica_groups=mesh['band'=32,'dom'=8] {'dom'}, use_global_device_ids=true, to_apply=%region_0.1 | all-reduce | flops 192 | bytes 1536 | tf_op jit(solution)/shard_map/psum | solution.py:191
  81.4 0.1 copy.7
  81.5 0.1 broadcast_in_dim.2.gram
  81.6 1.7 %project.1 = bf16[8,144,128]{2,1,0:T(8,128)(2,1)} custom-call(f32[24,8,128]{2,1,0:T(8,128)S(1)} %broadcast_in_dim.2.gram, bf16[16,2,72,128]{3,2,1,0:T(8,128)(2,1)S(1)} %all_to_all.11.gathered, bf16[8,144,128]{2,1,0:T(8,128)(2,1)S(1)} %second.1.resident), custom_call_target="tpu_custom_call" | custom-call | tf_op jit(solution)/shard_map/project/pallas_call | solution.py:144
  (4 shorter events, 0.0 us)
Async XLA Ops:
  0.0 7.6 %collective-permute-start.1 = (bf16[8,144,128]{2,1,0:T(8,128)(2,1)}, bf16[8,144,128]{2,1,0:T(8,128)(2,1)S(1)}, u32[]{:S(2)}, u32[]{:S(2)}) collective-permute-start(bf16[8,144,128]{2,1,0:T(8,128)(2,1)} %bitcast.8), channel_id=1, source_target_pairs={{1,0},{2,1},{3,2},{4,3},{5,4},{6,5},{7,6},{0,7},{9,8},{10,9},{11,1... | collective-permute-start | bytes 884744 | tf_op jit(solution)/shard_map/ppermute | solution.py:157
  3.2 4.6 %collective-permute-start = (bf16[8,144,128]{2,1,0:T(8,128)(2,1)}, bf16[8,144,128]{2,1,0:T(8,128)(2,1)S(1)}, u32[]{:S(2)}, u32[]{:S(2)}) collective-permute-start(bf16[8,144,128]{2,1,0:T(8,128)(2,1)} %bitcast.9), channel_id=1, source_target_pairs={{0,1},{1,2},{2,3},{3,4},{4,5},{5,6},{6,7},{7,0},{8,9},{9,10},{10,1... | collective-permute-start | bytes 884744 | tf_op jit(solution)/shard_map/ppermute | solution.py:157
  7.8 1.0 %copy-start = (bf16[8,6,24,128]{3,2,1,0:T(8,128)(2,1)S(1)}, bf16[8,6,24,128]{3,2,1,0:T(8,128)(2,1)}, u32[]{:S(2)}) copy-start(bf16[8,6,24,128]{3,2,1,0:T(8,128)(2,1)} %param.5) | copy-start | bytes 884740
  8.8 1.0 %copy-start.2 = (bf16[288,432]{1,0:T(8,128)(2,1)S(1)}, bf16[288,432]{1,0:T(8,128)(2,1)}, u32[]{:S(2)}) copy-start(bf16[288,432]{1,0:T(8,128)(2,1)} %constant.26.clone.left) | copy-start | bytes 746500
  9.7 0.9 %copy-start.4 = (f32[6,24,128]{2,1,0:T(8,128)S(1)}, f32[6,24,128]{2,1,0:T(8,128)}, u32[]{:S(2)}) copy-start(f32[6,24,128]{2,1,0:T(8,128)} %param.6) | copy-start | bytes 221188
  10.6 0.8 %copy-start.5 = (bf16[128,256]{1,0:T(8,128)(2,1)S(1)}, bf16[128,256]{1,0:T(8,128)(2,1)}, u32[]{:S(2)}) copy-start(bf16[128,256]{1,0:T(8,128)(2,1)} %constant.27.clone.right) | copy-start | bytes 196612
  11.5 13.5 %copy-start.1 = (bf16[8,6,24,128]{3,2,1,0:T(8,128)(2,1)S(1)}, bf16[8,6,24,128]{3,2,1,0:T(8,128)(2,1)}, u32[]{:S(2)}) copy-start(bf16[8,6,24,128]{3,2,1,0:T(8,128)(2,1)} %param.5) | copy-start | bytes 884740
  11.5 13.5 %copy-start.3 = (bf16[288,432]{1,0:T(8,128)(2,1)S(1)}, bf16[288,432]{1,0:T(8,128)(2,1)}, u32[]{:S(2)}) copy-start(bf16[288,432]{1,0:T(8,128)(2,1)} %constant.26.clone.left) | copy-start | bytes 746500
  12.1 7.7 %collective-permute-start.3 = (bf16[8,144,128]{2,1,0:T(8,128)(2,1)S(1)}, bf16[8,144,128]{2,1,0:T(8,128)(2,1)S(1)}, u32[]{:S(2)}, u32[]{:S(2)}) collective-permute-start(bf16[8,144,128]{2,1,0:T(8,128)(2,1)S(1)} %first.1.center), channel_id=1, source_target_pairs={{1,0},{2,1},{3,2},{4,3},{5,4},{6,5},{7,6},{0,7},{9,8},{10,9},{11,1... | collective-permute-start | bytes 884744 | tf_op jit(solution)/shard_map/ppermute | solution.py:157
  18.6 6.4 %collective-permute-start.2 = (bf16[8,144,128]{2,1,0:T(8,128)(2,1)S(1)}, bf16[8,144,128]{2,1,0:T(8,128)(2,1)S(1)}, u32[]{:S(2)}, u32[]{:S(2)}) collective-permute-start(bf16[8,144,128]{2,1,0:T(8,128)(2,1)S(1)} %first.1.center), channel_id=1, source_target_pairs={{0,1},{1,2},{2,3},{3,4},{4,5},{5,6},{6,7},{7,0},{8,9},{9,10},{10,1... | collective-permute-start | bytes 884744 | tf_op jit(solution)/shard_map/ppermute | solution.py:157
  25.6 14.3 %copy-start.6 = (s32[2]{0:T(128)S(1)}, s32[2]{0:T(128)}, u32[]{:S(2)}) copy-start(s32[2]{0:T(128)} %owners.3) | copy-start | bytes 28
  40.4 6.8 %collective-permute-start.4 = (bf16[2,72,128]{2,1,0:T(8,128)(2,1)S(1)}, bf16[2,72,128]{2,1,0:T(8,128)(2,1)S(1)}, u32[]{:S(2)}, u32[]{:S(2)}) collective-permute-start(bf16[2,72,128]{2,1,0:T(8,128)(2,1)S(1)} %select.5.mine), channel_id=1, source_target_pairs={{0,128},{8,136},{16,144},{24,152},{32,160},{40,168},{48,176},{56,1... | collective-permute-start | bytes 110600 | tf_op jit(solution)/shard_map/ppermute | solution.py:184

commit v2 on v1

v2 whole, which is shorter than its diff:
```python
import functools

import jax
import jax.numpy as jnp
import numpy as np
from jax import lax
from jax.experimental import pallas as pl
from jax.experimental.pallas import tpu as pltpu
from jax.sharding import PartitionSpec as P

ROUNDS = 2
PLANE = 16
GROUP = 8

stencil_weights = (
    -5369.0 / 1800.0,
    12.0 / 7.0,
    -15.0 / 56.0,
    10.0 / 189.0,
    -1.0 / 112.0,
    2.0 / 1925.0,
    -1.0 / 16632.0,
)
filter_center = 6.0
filter_halfwidth = 5.0
bf16 = jnp.bfloat16
f32 = jnp.float32


def halves(matrix):
    matrix = matrix.astype(np.float32)
    high = matrix.astype(bf16)
    low = (matrix - high.astype(np.float32)).astype(bf16)
    return high, low


def stencil_matrices(planes, ny, nx):
    scale = -0.5 / filter_halfwidth
    rows = planes * ny
    left = np.zeros((rows, 3 * rows), np.float64)
    for p in range(planes):
        for y in range(ny):
            for k in range(1, 7):
                for sign in (k, -k):
                    left[p * ny + y, (planes + p + sign) * ny + y] += scale * stencil_weights[k]
                    left[p * ny + y, (planes + p) * ny + (y + sign) % ny] += scale * stencil_weights[k]
    along_x = np.zeros((nx, nx), np.float64)
    for x in range(nx):
        for k in range(1, 7):
            for sign in (k, -k):
                along_x[(x + sign) % nx, x] += scale * stencil_weights[k]
    inside = np.concatenate(halves(left[:, rows : 2 * rows]), axis=0)
    beside = np.concatenate(halves(np.concatenate([left[:, :rows], left[:, 2 * rows :]], axis=1)), axis=0)
    return tuple(jnp.asarray(m) for m in (inside, beside, np.concatenate(halves(along_x), axis=1)))


def diagonal_of(potential):
    return (-1.5 * stencil_weights[0] - filter_center) / filter_halfwidth + potential * (1.0 / filter_halfwidth)


def inner_part(center, diagonals, inside, along_x):
    count, rows, nx = center.shape
    zy = jnp.dot(inside, jnp.concatenate([center[s] for s in range(count)], axis=1), preferred_element_type=f32)
    zy = zy[:rows] + zy[rows:]
    x = jnp.dot(center.reshape(count * rows, nx), along_x, preferred_element_type=f32)
    x = (x[:, :nx] + x[:, nx:]).reshape(count, rows, nx)
    return [zy[:, s * nx : (s + 1) * nx] + x[s] + diagonals[s] * center[s].astype(f32) for s in range(count)]


def outer_part(before, after, beside):
    count, rows, nx = before.shape
    slabs = [jnp.concatenate([before[s], after[s]], axis=0) for s in range(count)]
    zy = jnp.dot(beside, jnp.concatenate(slabs, axis=1), preferred_element_type=f32)
    zy = zy[:rows] + zy[rows:]
    return [zy[:, s * nx : (s + 1) * nx] for s in range(count)]


def inner_kernel(center, potential, inside, along_x, out):
    for s, value in enumerate(inner_part(center[...], [diagonal_of(potential[...])] * center.shape[0], inside[...], along_x[...])):
        out[s] = value


def first_kernel(before, after, inner, beside, out):
    for s, value in enumerate(outer_part(before[...], after[...], beside[...])):
        out[s] = (inner[s] + value).astype(bf16)


def second_kernel(before, after, inner, states, beside, out):
    for s, value in enumerate(outer_part(before[...], after[...], beside[...])):
        out[s] = (2.0 * (inner[s] + value) - states[s].astype(f32)).astype(bf16)


def owner_kernel(slab_a, slab_b, slab_c, slab_d, slab_e, pot_b, pot_c, pot_d, inside, beside, along_x, out):
    inside, beside, along_x = inside[...], beside[...], along_x[...]
    middle = jnp.stack([slab_b[...], slab_c[...], slab_d[...]])
    first = []
    before = jnp.stack([slab_a[...], slab_b[...], slab_c[...]])
    after = jnp.stack([slab_c[...], slab_d[...], slab_e[...]])
    outer = outer_part(before, after, beside)
    diagonals = [diagonal_of(p[...]) for p in (pot_b, pot_c, pot_d)]
    inner = inner_part(middle, diagonals, inside, along_x)
    first = [(i + o).astype(bf16)[None] for i, o in zip(inner, outer)]
    value = inner_part(first[1], diagonals[1:2], inside, along_x)[0] + outer_part(first[0], first[2], beside)[0]
    block = (2.0 * value - slab_c[...].astype(f32)).astype(bf16)
    for target in range(PLANE):
        out[target] = block


def by_rows(blocks):
    return jnp.concatenate(
        [jnp.concatenate([b[r : r + GROUP] for r in range(0, b.shape[0], GROUP)], axis=1) for b in blocks], axis=0
    ).astype(bf16)


def same_row(shape):
    row = lax.broadcasted_iota(jnp.int32, shape, 0) % GROUP
    return row == lax.broadcasted_iota(jnp.int32, shape, 1) % GROUP


def gram_kernel(gathered, resident, out, rows_out):
    count = resident.shape[0]
    blocks = []
    for turn in range(ROUNDS):
        for s in range(count):
            blocks.append(gathered[turn * count + s].astype(f32))
    owned = by_rows(blocks)
    against = jnp.concatenate(
        [by_rows([resident[j].astype(f32) for j in range(count)]), owned[: count * GROUP]], axis=0
    )
    products = lax.dot_general(owned, against, (((1,), (1,)), ((), ())), preferred_element_type=f32)
    products = jnp.where(same_row(products.shape), products, 0.0)
    out[...] = jnp.sum(products.reshape(ROUNDS * count, GROUP, products.shape[1]), axis=1)
    rows_out[...] = owned


def project_kernel(weight, gram, owned, resident, out):
    count, rows, nx = resident.shape
    lanes = gram.shape[1]
    group = lax.broadcasted_iota(jnp.int32, (lanes, lanes), 0) // GROUP
    same_group = jnp.where(group == lax.broadcasted_iota(jnp.int32, (lanes, lanes), 1) // GROUP, 1.0, 0.0)
    sums = jnp.dot(gram[...], same_group, precision=lax.Precision.HIGHEST, preferred_element_type=f32)
    one = sums[:count] * weight
    two = sums[count:]
    for k in range(count):
        lane = (count + k) * GROUP
        two = two - sums[count:, lane : lane + 1] * one[k : k + 1]
    coef = jnp.concatenate([one, two * weight], axis=0)
    spread = jnp.broadcast_to(coef[:, None, :], (ROUNDS * count, GROUP, lanes)).reshape(lanes, lanes)
    spread = jnp.where(same_row(spread.shape), spread, 0.0).T[: count * GROUP]
    high = spread.astype(bf16)
    low = (spread - high.astype(f32)).astype(bf16)
    taken = jnp.dot(jnp.concatenate([high, low], axis=0), owned[...], preferred_element_type=f32)
    taken = taken[: count * GROUP] + taken[count * GROUP :]
    for j in range(count):
        mine = taken[j * GROUP : (j + 1) * GROUP]
        mine = jnp.concatenate([mine[:, b * nx : (b + 1) * nx] for b in range(rows // GROUP)], axis=0)
        out[j] = (resident[j].astype(f32) - mine).astype(bf16)


vmem = pl.BlockSpec(memory_space=pltpu.VMEM)
smem = pl.BlockSpec(memory_space=pltpu.SMEM)
params = pltpu.CompilerParams(vmem_limit_bytes=40 * 1024 * 1024)


def call(kernel, out_shape, specs, *operands, name):
    return pl.pallas_call(
        kernel,
        out_shape=out_shape,
        in_specs=specs,
        out_specs=jax.tree.map(lambda _: vmem, out_shape),
        compiler_params=params,
        name=name,
    )(*operands)


def on_device(states, potential, owners):
    count, planes, ny, nx = states.shape
    rows = planes * ny
    doms, bands = lax.axis_size("dom"), lax.axis_size("band")
    weight = 1.0 / float(planes * doms * ny * nx)
    band = lax.axis_index("band")
    inside, beside, along_x = stencil_matrices(planes, ny, nx)
    states = states.reshape(count, rows, nx)
    potential = potential.reshape(rows, nx)
    block = jax.ShapeDtypeStruct(states.shape, bf16)
    wide = jax.ShapeDtypeStruct(states.shape, f32)
    cells = (rows, nx)
    groups = [list(range(start, start + PLANE)) for start in range(0, bands, PLANE)]

    def both_ways(values):
        ring = [(i, (i + 1) % doms) for i in range(doms)]
        return lax.ppermute(values, "dom", ring), lax.ppermute(values, "dom", [(b, a) for a, b in ring])

    def along_z(values, step):
        pairs = []
        for b in range(bands):
            for d in range(doms):
                place = (b // PLANE * doms + d + step) % (bands // PLANE * doms)
                pairs.append((b * doms + d, (place // doms * PLANE + b % PLANE) * doms + place % doms))
        return lax.ppermute(values, ("band", "dom"), pairs)

    owner = lax.dynamic_index_in_dim(owners, band % PLANE // count, 0, keepdims=False)
    twice = jnp.broadcast_to(states[None], (ROUNDS,) + states.shape).reshape((PLANE,) + cells)
    pieces = lax.all_to_all(twice, "band", 0, 0, axis_index_groups=groups)
    before, after = both_ways(states)
    inner = call(inner_kernel, wide, [vmem] * 4, states, potential, inside, along_x, name="first_inner")
    first = call(first_kernel, block, [vmem] * 4, before, after, inner, beside, name="first")
    pieces, first = lax.optimization_barrier((pieces, first))
    mine = lax.dynamic_index_in_dim(pieces, owner % PLANE, 0, keepdims=False)
    mine = jnp.where(owner // PLANE == band // PLANE, mine, jnp.zeros_like(mine))
    raw = mine + lax.ppermute(mine, "band", [(i, (i + PLANE) % bands) for i in range(bands)])
    near = [along_z(raw, step) for step in (1, -1, 2, -2)]
    pot_before, pot_after = along_z(potential, 1), along_z(potential, -1)

    before, after = both_ways(first)
    inner = call(inner_kernel, wide, [vmem] * 4, first, potential, inside, along_x, name="second_inner")
    resident = call(second_kernel, block, [vmem] * 5, before, after, inner, states, beside, name="second")

    copies = call(
        owner_kernel, jax.ShapeDtypeStruct((PLANE,) + cells, bf16), [vmem] * 11,
        near[2], near[0], raw, near[1], near[3], pot_before, potential, pot_after, inside, beside, along_x,
        name="owner",
    )
    gathered = lax.all_to_all(copies, "band", 0, 0, axis_index_groups=groups)
    gram, owned = call(
        gram_kernel,
        (
            jax.ShapeDtypeStruct((ROUNDS * count, ROUNDS * count * GROUP), f32),
            jax.ShapeDtypeStruct((ROUNDS * count * GROUP, rows // GROUP * nx), bf16),
        ),
        [vmem] * 2, gathered, resident, name="gram",
    )
    gram = gram + lax.ppermute(gram, "dom", [(i, i ^ 1) for i in range(doms)])
    gram = gram + sum(lax.ppermute(gram, "dom", [(i, i ^ s) for i in range(doms)]) for s in range(2, doms, 2))
    result = call(
        functools.partial(project_kernel, weight), block, [vmem] * 3, gram, owned, resident, name="project"
    )
    return result.reshape(count, planes, ny, nx)


def solution(mesh):
    return jax.shard_map(
        on_device,
        mesh=mesh,
        in_specs=(P("band", "dom", None, None), P("dom", None, None), P()),
        out_specs=P("band", "dom", None, None),
        check_vma=False,
    )
```

time: 83.6 us -> 69 us (0.83)
  blocking collectives: 46.5 us -> 0 us
  starting transfers between devices: 12.7 us -> 39.3 us
  waiting for transfers between devices: 14.7 us -> 18.9 us
  between operations: 0.06 us -> 2.78 us
  local copies, waits for them, and re-layouts: 3.94 us -> 2.49 us
    all_to_all x2 -> x0, blocking collectives: 26.7 us -> none  [the longest x1 14.3 us: on_device(): lax.all_to_all(resident.reshape(PLANE, half, nx), 'band', 0, 0, axis_inde...]
    psum x1 -> x0, blocking collectives: 19.7 us -> none  [on_device(): gram = lax.psum(gram[:, :, 0], 'dom')]
    all_to_all x0 -> x2, starting transfers between devices: none -> 13.1 us  [the longest x1 7.73 us: on_device(): pieces = lax.all_to_all(twice, 'band', 0, 0, axis_index_groups=groups)]
    ppermute x4 -> x14, starting transfers between devices: 9.71 us -> 19.1 us  [the longest x6 8.89 us: along_z(): return lax.ppermute(values, ('band', 'dom'), pairs)]
    all_to_all x0 -> x2, waiting for transfers between devices: none -> 4.12 us  [the longest x1 3.24 us: on_device(): pieces = lax.all_to_all(twice, 'band', 0, 0, axis_index_groups=groups)]
    ppermute x1, starting transfers between devices: 3.01 us -> 6.99 us  [on_device(): lax.ppermute(mine, 'band', [(i, (i + PLANE) % bands) for i in range(bands)])]
    ppermute x4 -> x14, waiting for transfers between devices: 10.9 us -> 14.8 us  [the longest x2 8.27 us: both_ways(): lax.ppermute(values, 'dom', [(b, a) for a, b in ring])]
    ppermute x1, waiting for transfers between devices: 3.8 us -> 0.01 us  [on_device(): lax.ppermute(mine, 'band', [(i, (i + PLANE) % bands) for i in range(bands)])]
  transfers between devices with their start and end apart: 5 -> 17, of which waited for: 5 -> 10; matrix products, arithmetic and copies ran while one was open for 0% -> 1% of each run, Pallas kernels for 0% -> 3%
where the time goes in v2:
time: 69 us; the launch traced here: 68.7 us
  starting transfers between devices  39.3 us (57%)
  waiting for transfers between devices  18.9 us (27%)
  Pallas kernels  5.21 us (8%)
  between operations  2.78 us (4%)
  local copies, waits for them, and re-layouts  2.49 us (4%)
    ppermute x6, starting transfers between devices, along_z(): return lax.ppermute(values, ('band', 'dom'), pairs)  8.89 us
    ppermute x2, waiting for transfers between devices, both_ways(): lax.ppermute(values, 'dom', [(b, a) for a, b in ring])  8.27 us
    all_to_all x1, starting transfers between devices, on_device(): pieces = lax.all_to_all(twice, 'band', 0, 0, axis_index_groups=groups)  7.73 us
    ppermute x1, starting transfers between devices, on_device(): lax.ppermute(mine, 'band', [(i, (i + PLANE) % bands) for i in range(bands)])  6.99 us
    all_to_all x1, starting transfers between devices, on_device(): gathered = lax.all_to_all(copies, 'band', 0, 0, axis_index_groups=groups)  5.42 us
    pallas_call x7, Pallas kernels, call(): pl.pallas_call(kernel, out_shape=out_shape, in_specs=specs, out_specs=jax...  5.21 us
    ppermute x6, waiting for transfers between devices, along_z(): return lax.ppermute(values, ('band', 'dom'), pairs)  4.27 us
    ppermute x3, starting transfers between devices, on_device(): lax.ppermute(gram, 'dom', [(i, i ^ s) for i in range(doms)])  3.55 us
  transfers between devices with their start and end apart: 17, of which 10 were waited for; matrix products, arithmetic and copies ran while one was open for 1% of the time, Pallas kernels for 3%

profile of v2, /device:TPU:1, one launch (start us, length us, event | category | flops | bytes accessed | tf_op | source)
XLA Modules:
  0.0 68.7 jit_solution(13010738340963081382)
XLA Ops:
  0.0 1.9 %broadcast_in_dim.11 = bf16[2,8,144,128]{3,2,1,0:T(8,128)(2,1)} broadcast(bf16[8,144,128]{2,1,0:T(8,128)(2,1)} %bitcast.9), dimensions={1,2,3} | broadcast | bytes 884736 | tf_op jit(solution)/shard_map/broadcast_in_dim | solution.py:203
  1.9 7.7 %all-to-all-start = ((bf16[16,144,128]{2,1,0:T(8,128)(2,1)}), bf16[16,144,128]{2,1,0:T(8,128)(2,1)S(1)}, u32[]{:S(2)}, u32[]{:S(2)}) async-start(bf16[16,144,128]{2,1,0:T(8,128)(2,1)} %bitcast.2), calls=%async_computation | async-start | bytes 1179648 | tf_op jit(solution)/shard_map/all_to_all | solution.py:204
  9.6 1.0 %collective-permute-start.1 = (bf16[8,144,128]{2,1,0:T(8,128)(2,1)S(1)}, bf16[8,144,128]{2,1,0:T(8,128)(2,1)S(1)}, u32[]{:S(2)}, u32[]{:S(2)}) collective-permute-start(bf16[8,144,128]{2,1,0:T(8,128)(2,1)S(1)} %bitcast.10), channel_id=1, source_target_pairs={{1,0},{2,1},{3,2},{4,3},{5,4},{6,5},{7,6},{0,7},{9,8},{10,9},{11,1... | collective-permute-start | bytes 884744 | tf_op jit(solution)/shard_map/ppermute | solution.py:192
  10.7 1.6 %collective-permute-start = (bf16[8,144,128]{2,1,0:T(8,128)(2,1)S(1)}, bf16[8,144,128]{2,1,0:T(8,128)(2,1)S(1)}, u32[]{:S(2)}, u32[]{:S(2)}) collective-permute-start(bf16[8,144,128]{2,1,0:T(8,128)(2,1)S(1)} %bitcast.11), channel_id=1, source_target_pairs={{0,1},{1,2},{2,3},{3,4},{4,5},{5,6},{6,7},{7,0},{8,9},{9,10},{10,1... | collective-permute-start | bytes 884744 | tf_op jit(solution)/shard_map/ppermute | solution.py:192
  12.3 0.6 dynamic_slice.8
  15.6 0.5 first_inner.1.inner
  16.0 0.9 %collective-permute-done.1.after = bf16[8,144,128]{2,1,0:T(8,128)(2,1)S(1)} collective-permute-done((bf16[8,144,128]{2,1,0:T(8,128)(2,1)S(1)}, bf16[8,144,128]{2,1,0:T(8,128)(2,1)S(1)}, u32[]{:S(2)}, u32[]{:S(2)}) %collective-permute-start.1) | collective-permute-done | bytes 294944 | tf_op jit(solution)/shard_map/ppermute | solution.py:192
  16.9 0.5 first.1.center
  17.4 3.2 %all-to-all-done = bf16[16,144,128]{2,1,0:T(8,128)(2,1)S(1)} async-done(((bf16[16,144,128]{2,1,0:T(8,128)(2,1)}), bf16[16,144,128]{2,1,0:T(8,128)(2,1)S(1)}, u32[]{:S(2)}, u32[]{:S(2)}) %all-to-all-start) | async-done | bytes 589856 | tf_op jit(solution)/shard_map/all_to_all | solution.py:204
  20.6 7.0 %collective-permute-start.2 = (bf16[144,128]{1,0:T(8,128)(2,1)S(1)}, bf16[144,128]{1,0:T(8,128)(2,1)S(1)}, u32[]{:S(2)}, u32[]{:S(2)}) collective-permute-start(bf16[144,128]{1,0:T(8,128)(2,1)S(1)} %select_bitcast_fusion), channel_id=1, source_target_pairs={{0,128},{8,136},{16,144},{24,152},{32,160},{40,168},{48,176},{56,1... | collective-permute-start | bytes 110600 | tf_op jit(solution)/shard_map/ppermute | solution.py:211
  27.6 2.1 %collective-permute-start.8 = (f32[144,128]{1,0:T(8,128)S(1)}, f32[144,128]{1,0:T(8,128)S(1)}, u32[]{:S(2)}, u32[]{:S(2)}) collective-permute-start(f32[144,128]{1,0:T(8,128)S(1)} %bitcast.15), channel_id=1, source_target_pairs={{0,135},{1,0},{2,1},{3,2},{4,3},{5,4},{6,5},{7,6},{8,143},{9,8},{1... | collective-permute-start | bytes 221192 | tf_op jit(solution)/shard_map/ppermute | solution.py:200
  29.8 0.6 collective-permute-start.7
  30.4 3.2 %collective-permute-start.6 = (bf16[144,128]{1,0:T(8,128)(2,1)S(1)}, bf16[144,128]{1,0:T(8,128)(2,1)S(1)}, u32[]{:S(2)}, u32[]{:S(2)}) collective-permute-start(bf16[144,128]{1,0:T(8,128)(2,1)S(1)} %fusion.slab_c), channel_id=1, source_target_pairs={{0,134},{1,135},{2,0},{3,1},{4,2},{5,3},{6,4},{7,5},{8,142},{9,143... | collective-permute-start | bytes 110600 | tf_op jit(solution)/shard_map/ppermute | solution.py:200
  33.6 2.9 %collective-permute-start.5 = (bf16[144,128]{1,0:T(8,128)(2,1)S(1)}, bf16[144,128]{1,0:T(8,128)(2,1)S(1)}, u32[]{:S(2)}, u32[]{:S(2)}) collective-permute-start(bf16[144,128]{1,0:T(8,128)(2,1)S(1)} %fusion.slab_c), channel_id=1, source_target_pairs={{0,135},{1,0},{2,1},{3,2},{4,3},{5,4},{6,5},{7,6},{8,143},{9,8},{1... | collective-permute-start | bytes 110600 | tf_op jit(solution)/shard_map/ppermute | solution.py:200
  36.6 0.8 %collective-permute-done.5.slab_d = bf16[144,128]{1,0:T(8,128)(2,1)S(1)} collective-permute-done((bf16[144,128]{1,0:T(8,128)(2,1)S(1)}, bf16[144,128]{1,0:T(8,128)(2,1)S(1)}, u32[]{:S(2)}, u32[]{:S(2)}) %collective-permute-start.5) | collective-permute-done | bytes 36896 | tf_op jit(solution)/shard_map/ppermute | solution.py:200
  37.4 0.3 collective-permute-done.4.slab_b
  37.7 3.1 %collective-permute-done.3.slab_a = bf16[144,128]{1,0:T(8,128)(2,1)S(1)} collective-permute-done((bf16[144,128]{1,0:T(8,128)(2,1)S(1)}, bf16[144,128]{1,0:T(8,128)(2,1)S(1)}, u32[]{:S(2)}, u32[]{:S(2)}) %collective-permute-start.3) | collective-permute-done | bytes 36896 | tf_op jit(solution)/shard_map/ppermute | solution.py:200
  40.8 1.6 %owner.1 = bf16[16,144,128]{2,1,0:T(8,128)(2,1)} custom-call(bf16[144,128]{1,0:T(8,128)(2,1)S(1)} %collective-permute-done.3.slab_a, bf16[144,128]{1,0:T(8,128)(2,1)S(1)} %collective-permute-done.4.slab_b, bf16[144,128]{1,0:T(8,128)(2,1)S(1)} %fusion.slab_c, bf16[144,128]{1,0:T(8,128)(2,1)S(1)} %collective-permute-done.5.slab_d, ...), custom_call_target="tpu_custom_call" | custom-call | tf_op jit(solution)/shard_map/owner/pallas_call | solution.py:166
  42.4 5.4 %all-to-all-start.1 = ((bf16[16,144,128]{2,1,0:T(8,128)(2,1)}), bf16[16,144,128]{2,1,0:T(8,128)(2,1)S(1)}, u32[]{:S(2)}, u32[]{:S(2)}) async-start(bf16[16,144,128]{2,1,0:T(8,128)(2,1)} %owner.1), calls=%async_computation.1 | async-start | bytes 1179648 | tf_op jit(solution)/shard_map/all_to_all | solution.py:224
  48.1 1.5 %collective-permute-start.9 = (bf16[8,144,128]{2,1,0:T(8,128)(2,1)S(1)}, bf16[8,144,128]{2,1,0:T(8,128)(2,1)S(1)}, u32[]{:S(2)}, u32[]{:S(2)}) collective-permute-start(bf16[8,144,128]{2,1,0:T(8,128)(2,1)S(1)} %first.1.center), channel_id=1, source_target_pairs={{0,1},{1,2},{2,3},{3,4},{4,5},{5,6},{6,7},{7,0},{8,9},{9,10},{10,1... | collective-permute-start | bytes 884744 | tf_op jit(solution)/shard_map/ppermute | solution.py:192
  49.7 0.5 second_inner.1.inner
  50.1 7.4 %collective-permute-done.10.after = bf16[8,144,128]{2,1,0:T(8,128)(2,1)S(1)} collective-permute-done((bf16[8,144,128]{2,1,0:T(8,128)(2,1)S(1)}, bf16[8,144,128]{2,1,0:T(8,128)(2,1)S(1)}, u32[]{:S(2)}, u32[]{:S(2)}) %collective-permute-start.10) | collective-permute-done | bytes 294944 | tf_op jit(solution)/shard_map/ppermute | solution.py:192
  57.5 0.5 second.1.resident
  58.0 0.9 %all-to-all-done.1.gathered = bf16[16,144,128]{2,1,0:T(8,128)(2,1)S(1)} async-done(((bf16[16,144,128]{2,1,0:T(8,128)(2,1)}), bf16[16,144,128]{2,1,0:T(8,128)(2,1)S(1)}, u32[]{:S(2)}, u32[]{:S(2)}) %all-to-all-start.1) | async-done | bytes 589856 | tf_op jit(solution)/shard_map/all_to_all | solution.py:224
  58.9 0.3 gram.1
  59.2 2.2 %collective-permute-start.11 = (f32[16,128]{1,0:T(8,128)S(1)}, f32[16,128]{1,0:T(8,128)S(1)}, u32[]{:S(2)}, u32[]{:S(2)}) collective-permute-start(f32[16,128]{1,0:T(8,128)S(1)} %get-tuple-element.11), channel_id=1, source_target_pairs={{0,1},{1,0},{2,3},{3,2},{4,5},{5,4},{6,7},{7,6},{8,9},{9,8},{10,11... | collective-permute-start | bytes 24584 | tf_op jit(solution)/shard_map/ppermute | solution.py:233
  61.5 0.8 %collective-permute-done.11 = f32[16,128]{1,0:T(8,128)S(1)} collective-permute-done((f32[16,128]{1,0:T(8,128)S(1)}, f32[16,128]{1,0:T(8,128)S(1)}, u32[]{:S(2)}, u32[]{:S(2)}) %collective-permute-start.11) | collective-permute-done | bytes 8224 | tf_op jit(solution)/shard_map/ppermute | solution.py:233
  62.4 0.8 %collective-permute-start.13 = (f32[16,128]{1,0:T(8,128)S(1)}, f32[16,128]{1,0:T(8,128)S(1)}, u32[]{:S(2)}, u32[]{:S(2)}) collective-permute-start(f32[16,128]{1,0:T(8,128)S(1)} %add.38), channel_id=1, source_target_pairs={{0,4},{1,5},{2,6},{3,7},{4,0},{5,1},{6,2},{7,3},{8,12},{9,13},{10,... | collective-permute-start | bytes 24584 | tf_op jit(solution)/shard_map/ppermute | solution.py:234
  63.1 2.7 %collective-permute-start.12 = (f32[16,128]{1,0:T(8,128)S(1)}, f32[16,128]{1,0:T(8,128)S(1)}, u32[]{:S(2)}, u32[]{:S(2)}) collective-permute-start(f32[16,128]{1,0:T(8,128)S(1)} %add.38), channel_id=1, source_target_pairs={{0,2},{1,3},{2,0},{3,1},{4,6},{5,7},{6,4},{7,5},{8,10},{9,11},{10,... | collective-permute-start | bytes 24584 | tf_op jit(solution)/shard_map/ppermute | solution.py:234
  65.9 0.8 %collective-permute-done.14 = f32[16,128]{1,0:T(8,128)S(1)} collective-permute-done((f32[16,128]{1,0:T(8,128)S(1)}, f32[16,128]{1,0:T(8,128)S(1)}, u32[]{:S(2)}, u32[]{:S(2)}) %collective-permute-start.14) | collective-permute-done | bytes 8224 | tf_op jit(solution)/shard_map/ppermute | solution.py:234
  66.6 0.6 collective-permute-done.12
  67.3 1.4 %project.1 = bf16[8,144,128]{2,1,0:T(8,128)(2,1)} custom-call(f32[16,128]{1,0:T(8,128)S(1)} %add_add_fusion.gram, bf16[128,2304]{1,0:T(8,128)(2,1)S(1)} %get-tuple-element.12.owned, bf16[8,144,128]{2,1,0:T(8,128)(2,1)S(1)} %second.1.resident), custom_call_target="tpu_custom_call" | custom-call | tf_op jit(solution)/shard_map/project/pallas_call | solution.py:166
  (27 shorter events, 0.4 us)
Async XLA Ops:
  1.9 7.7 %copy-start = (bf16[8,6,24,128]{3,2,1,0:T(8,128)(2,1)S(1)}, bf16[8,6,24,128]{3,2,1,0:T(8,128)(2,1)}, u32[]{:S(2)}) copy-start(bf16[8,6,24,128]{3,2,1,0:T(8,128)(2,1)} %param.6) | copy-start | bytes 884740
  1.9 10.4 %copy-start.5 = (s32[2]{0:T(128)S(1)}, s32[2]{0:T(128)}, u32[]{:S(2)}) copy-start(s32[2]{0:T(128)} %param.8) | copy-start | bytes 28
  1.9 13.6 %copy-start.2 = (bf16[288,144]{1,0:T(8,128)(2,1)S(1)}, bf16[288,144]{1,0:T(8,128)(2,1)}, u32[]{:S(2)}) copy-start(bf16[288,144]{1,0:T(8,128)(2,1)} %constant.71.clone.inside) | copy-start | bytes 248836
  1.9 13.6 %copy-start.4 = (bf16[128,256]{1,0:T(8,128)(2,1)S(1)}, bf16[128,256]{1,0:T(8,128)(2,1)}, u32[]{:S(2)}) copy-start(bf16[128,256]{1,0:T(8,128)(2,1)} %constant.73.clone.along_x) | copy-start | bytes 196612
  1.9 18.7 %all-to-all-start = ((bf16[16,144,128]{2,1,0:T(8,128)(2,1)}), bf16[16,144,128]{2,1,0:T(8,128)(2,1)S(1)}, u32[]{:S(2)}, u32[]{:S(2)}) async-start(bf16[16,144,128]{2,1,0:T(8,128)(2,1)} %bitcast.2), calls=%async_computation | async-start | bytes 1179648 | tf_op jit(solution)/shard_map/all_to_all | solution.py:204
  9.6 5.9 %copy-start.3 = (f32[6,24,128]{2,1,0:T(8,128)S(1)}, f32[6,24,128]{2,1,0:T(8,128)}, u32[]{:S(2)}) copy-start(f32[6,24,128]{2,1,0:T(8,128)} %param.7) | copy-start | bytes 221188
  9.6 7.3 %collective-permute-start.1 = (bf16[8,144,128]{2,1,0:T(8,128)(2,1)S(1)}, bf16[8,144,128]{2,1,0:T(8,128)(2,1)S(1)}, u32[]{:S(2)}, u32[]{:S(2)}) collective-permute-start(bf16[8,144,128]{2,1,0:T(8,128)(2,1)S(1)} %bitcast.10), channel_id=1, source_target_pairs={{1,0},{2,1},{3,2},{4,3},{5,4},{6,5},{7,6},{0,7},{9,8},{10,9},{11,1... | collective-permute-start | bytes 884744 | tf_op jit(solution)/shard_map/ppermute | solution.py:192
  10.7 6.2 %collective-permute-start = (bf16[8,144,128]{2,1,0:T(8,128)(2,1)S(1)}, bf16[8,144,128]{2,1,0:T(8,128)(2,1)S(1)}, u32[]{:S(2)}, u32[]{:S(2)}) collective-permute-start(bf16[8,144,128]{2,1,0:T(8,128)(2,1)S(1)} %bitcast.11), channel_id=1, source_target_pairs={{0,1},{1,2},{2,3},{3,4},{4,5},{5,6},{6,7},{7,0},{8,9},{9,10},{10,1... | collective-permute-start | bytes 884744 | tf_op jit(solution)/shard_map/ppermute | solution.py:192
  15.5 1.4 %copy-start.1 = (bf16[288,288]{1,0:T(8,128)(2,1)S(1)}, bf16[288,288]{1,0:T(8,128)(2,1)}, u32[]{:S(2)}) copy-start(bf16[288,288]{1,0:T(8,128)(2,1)} %constant.72.clone.beside) | copy-start | bytes 497668
  20.6 9.8 %collective-permute-start.2 = (bf16[144,128]{1,0:T(8,128)(2,1)S(1)}, bf16[144,128]{1,0:T(8,128)(2,1)S(1)}, u32[]{:S(2)}, u32[]{:S(2)}) collective-permute-start(bf16[144,128]{1,0:T(8,128)(2,1)S(1)} %select_bitcast_fusion), channel_id=1, source_target_pairs={{0,128},{8,136},{16,144},{24,152},{32,160},{40,168},{48,176},{56,1... | collective-permute-start | bytes 110600 | tf_op jit(solution)/shard_map/ppermute | solution.py:211
  27.6 8.9 %collective-permute-start.8 = (f32[144,128]{1,0:T(8,128)S(1)}, f32[144,128]{1,0:T(8,128)S(1)}, u32[]{:S(2)}, u32[]{:S(2)}) collective-permute-start(f32[144,128]{1,0:T(8,128)S(1)} %bitcast.15), channel_id=1, source_target_pairs={{0,135},{1,0},{2,1},{3,2},{4,3},{5,4},{6,5},{7,6},{8,143},{9,8},{1... | collective-permute-start | bytes 221192 | tf_op jit(solution)/shard_map/ppermute | solution.py:200
  29.8 6.8 %collective-permute-start.7 = (f32[144,128]{1,0:T(8,128)S(1)}, f32[144,128]{1,0:T(8,128)S(1)}, u32[]{:S(2)}, u32[]{:S(2)}) collective-permute-start(f32[144,128]{1,0:T(8,128)S(1)} %bitcast.16), channel_id=1, source_target_pairs={{0,1},{1,2},{2,3},{3,4},{4,5},{5,6},{6,7},{7,128},{8,9},{9,10},{10... | collective-permute-start | bytes 221192 | tf_op jit(solution)/shard_map/ppermute | solution.py:200
  30.4 6.2 %collective-permute-start.6 = (bf16[144,128]{1,0:T(8,128)(2,1)S(1)}, bf16[144,128]{1,0:T(8,128)(2,1)S(1)}, u32[]{:S(2)}, u32[]{:S(2)}) collective-permute-start(bf16[144,128]{1,0:T(8,128)(2,1)S(1)} %fusion.slab_c), channel_id=1, source_target_pairs={{0,134},{1,135},{2,0},{3,1},{4,2},{5,3},{6,4},{7,5},{8,142},{9,143... | collective-permute-start | bytes 110600 | tf_op jit(solution)/shard_map/ppermute | solution.py:200
  33.6 3.8 %collective-permute-start.5 = (bf16[144,128]{1,0:T(8,128)(2,1)S(1)}, bf16[144,128]{1,0:T(8,128)(2,1)S(1)}, u32[]{:S(2)}, u32[]{:S(2)}) collective-permute-start(bf16[144,128]{1,0:T(8,128)(2,1)S(1)} %fusion.slab_c), channel_id=1, source_target_pairs={{0,135},{1,0},{2,1},{3,2},{4,3},{5,4},{6,5},{7,6},{8,143},{9,8},{1... | collective-permute-start | bytes 110600 | tf_op jit(solution)/shard_map/ppermute | solution.py:200
  36.5 1.2 %collective-permute-start.4 = (bf16[144,128]{1,0:T(8,128)(2,1)S(1)}, bf16[144,128]{1,0:T(8,128)(2,1)S(1)}, u32[]{:S(2)}, u32[]{:S(2)}) collective-permute-start(bf16[144,128]{1,0:T(8,128)(2,1)S(1)} %fusion.slab_c), channel_id=1, source_target_pairs={{0,1},{1,2},{2,3},{3,4},{4,5},{5,6},{6,7},{7,128},{8,9},{9,10},{10... | collective-permute-start | bytes 110600 | tf_op jit(solution)/shard_map/ppermute | solution.py:200
  36.5 4.3 %collective-permute-start.3 = (bf16[144,128]{1,0:T(8,128)(2,1)S(1)}, bf16[144,128]{1,0:T(8,128)(2,1)S(1)}, u32[]{:S(2)}, u32[]{:S(2)}) collective-permute-start(bf16[144,128]{1,0:T(8,128)(2,1)S(1)} %fusion.slab_c), channel_id=1, source_target_pairs={{0,2},{1,3},{2,4},{3,5},{4,6},{5,7},{6,128},{7,129},{8,10},{9,11},... | collective-permute-start | bytes 110600 | tf_op jit(solution)/shard_map/ppermute | solution.py:200
  42.4 16.5 %all-to-all-start.1 = ((bf16[16,144,128]{2,1,0:T(8,128)(2,1)}), bf16[16,144,128]{2,1,0:T(8,128)(2,1)S(1)}, u32[]{:S(2)}, u32[]{:S(2)}) async-start(bf16[16,144,128]{2,1,0:T(8,128)(2,1)} %owner.1), calls=%async_computation.1 | async-start | bytes 1179648 | tf_op jit(solution)/shard_map/all_to_all | solution.py:224
  47.8 9.7 %collective-permute-start.10 = (bf16[8,144,128]{2,1,0:T(8,128)(2,1)S(1)}, bf16[8,144,128]{2,1,0:T(8,128)(2,1)S(1)}, u32[]{:S(2)}, u32[]{:S(2)}) collective-permute-start(bf16[8,144,128]{2,1,0:T(8,128)(2,1)S(1)} %first.1.center), channel_id=1, source_target_pairs={{1,0},{2,1},{3,2},{4,3},{5,4},{6,5},{7,6},{0,7},{9,8},{10,9},{11,1... | collective-permute-start | bytes 884744 | tf_op jit(solution)/shard_map/ppermute | solution.py:192
  48.1 9.4 %collective-permute-start.9 = (bf16[8,144,128]{2,1,0:T(8,128)(2,1)S(1)}, bf16[8,144,128]{2,1,0:T(8,128)(2,1)S(1)}, u32[]{:S(2)}, u32[]{:S(2)}) collective-permute-start(bf16[8,144,128]{2,1,0:T(8,128)(2,1)S(1)} %first.1.center), channel_id=1, source_target_pairs={{0,1},{1,2},{2,3},{3,4},{4,5},{5,6},{6,7},{7,0},{8,9},{9,10},{10,1... | collective-permute-start | bytes 884744 | tf_op jit(solution)/shard_map/ppermute | solution.py:192
  59.2 3.1 %collective-permute-start.11 = (f32[16,128]{1,0:T(8,128)S(1)}, f32[16,128]{1,0:T(8,128)S(1)}, u32[]{:S(2)}, u32[]{:S(2)}) collective-permute-start(f32[16,128]{1,0:T(8,128)S(1)} %get-tuple-element.11), channel_id=1, source_target_pairs={{0,1},{1,0},{2,3},{3,2},{4,5},{5,4},{6,7},{7,6},{8,9},{9,8},{10,11... | collective-permute-start | bytes 24584 | tf_op jit(solution)/shard_map/ppermute | solution.py:233
  62.3 4.3 %collective-permute-start.14 = (f32[16,128]{1,0:T(8,128)S(1)}, f32[16,128]{1,0:T(8,128)S(1)}, u32[]{:S(2)}, u32[]{:S(2)}) collective-permute-start(f32[16,128]{1,0:T(8,128)S(1)} %add.38), channel_id=1, source_target_pairs={{0,6},{1,7},{2,4},{3,5},{4,2},{5,3},{6,0},{7,1},{8,14},{9,15},{10,... | collective-permute-start | bytes 24584 | tf_op jit(solution)/shard_map/ppermute | solution.py:234
  62.4 4.2 %collective-permute-start.13 = (f32[16,128]{1,0:T(8,128)S(1)}, f32[16,128]{1,0:T(8,128)S(1)}, u32[]{:S(2)}, u32[]{:S(2)}) collective-permute-start(f32[16,128]{1,0:T(8,128)S(1)} %add.38), channel_id=1, source_target_pairs={{0,4},{1,5},{2,6},{3,7},{4,0},{5,1},{6,2},{7,3},{8,12},{9,13},{10,... | collective-permute-start | bytes 24584 | tf_op jit(solution)/shard_map/ppermute | solution.py:234
  63.1 4.1 %collective-permute-start.12 = (f32[16,128]{1,0:T(8,128)S(1)}, f32[16,128]{1,0:T(8,128)S(1)}, u32[]{:S(2)}, u32[]{:S(2)}) collective-permute-start(f32[16,128]{1,0:T(8,128)S(1)} %add.38), channel_id=1, source_target_pairs={{0,2},{1,3},{2,0},{3,1},{4,6},{5,7},{6,4},{7,5},{8,10},{9,11},{10,... | collective-permute-start | bytes 24584 | tf_op jit(solution)/shard_map/ppermute | solution.py:234

commit v3 on v2

--- a/solution.py
+++ b/solution.py
@@ -73,6 +73,15 @@
     zy = jnp.dot(beside, jnp.concatenate(slabs, axis=1), preferred_element_type=f32)
     zy = zy[:rows] + zy[rows:]
     return [zy[:, s * nx : (s + 1) * nx] for s in range(count)]
+
+
+def twice_kernel(states, out, done):
+    count = states.shape[0]
+    copies = [pltpu.make_async_copy(states, out.at[pl.ds(k * count, count)], done.at[k]) for k in range(ROUNDS)]
+    for copy in copies:
+        copy.start()
+    for copy in copies:
+        copy.wait()
 
 
 def inner_kernel(center, potential, inside, along_x, out):
@@ -199,16 +208,26 @@
                 pairs.append((b * doms + d, (place // doms * PLANE + b % PLANE) * doms + place % doms))
         return lax.ppermute(values, ("band", "dom"), pairs)
 
-    owner = lax.dynamic_index_in_dim(owners, band % PLANE // count, 0, keepdims=False)
-    twice = jnp.broadcast_to(states[None], (ROUNDS,) + states.shape).reshape((PLANE,) + cells)
+    hbm = pl.BlockSpec(memory_space=pltpu.HBM)
+    twice = pl.pallas_call(
+        twice_kernel,
+        out_shape=jax.ShapeDtypeStruct((ROUNDS * count,) + cells, bf16),
+        in_specs=[hbm],
+        out_specs=hbm,
+        scratch_shapes=[pltpu.SemaphoreType.DMA((ROUNDS,))],
+        compiler_params=params,
+        name="twice",
+    )(states)
     pieces = lax.all_to_all(twice, "band", 0, 0, axis_index_groups=groups)
     before, after = both_ways(states)
     inner = call(inner_kernel, wide, [vmem] * 4, states, potential, inside, along_x, name="first_inner")
+    owner = jnp.where((band >> 3) & 1 == 0, owners[0], owners[1])
+    mine = lax.dynamic_index_in_dim(pieces, owner & (PLANE - 1), 0, keepdims=False)
+    mine = jnp.where(owner >> 4 == band >> 4, mine, jnp.zeros_like(mine))
+    other = lax.ppermute(mine, "band", [(i, (i + PLANE) % bands) for i in range(bands)])
     first = call(first_kernel, block, [vmem] * 4, before, after, inner, beside, name="first")
-    pieces, first = lax.optimization_barrier((pieces, first))
-    mine = lax.dynamic_index_in_dim(pieces, owner % PLANE, 0, keepdims=False)
-    mine = jnp.where(owner // PLANE == band // PLANE, mine, jnp.zeros_like(mine))
-    raw = mine + lax.ppermute(mine, "band", [(i, (i + PLANE) % bands) for i in range(bands)])
+    other, first = lax.optimization_barrier((other, first))
+    raw = mine + other
     near = [along_z(raw, step) for step in (1, -1, 2, -2)]
     pot_before, pot_after = along_z(potential, 1), along_z(potential, -1)
 

time: 69 us -> 67.1 us (0.972)
  starting transfers between devices: 39.3 us -> 37.2 us
  waiting for transfers between devices: 18.9 us -> 20.3 us
  between operations: 2.78 us -> 1.55 us
  local copies, waits for them, and re-layouts: 2.49 us -> 1.59 us
  Pallas kernels: 5.21 us -> 6.07 us
    all_to_all x1, waiting for transfers between devices: 3.24 us -> 6.39 us  [on_device(): pieces = lax.all_to_all(twice, 'band', 0, 0, axis_index_groups=groups)]
    broadcast_in_dim x1 -> x0, local copies, waits for them, and re-layouts: 1.88 us -> none  [on_device(): jnp.broadcast_to(states[None], (ROUNDS,) + states.shape)]
    all_to_all x1, starting transfers between devices: 5.42 us -> 3.58 us  [on_device(): gathered = lax.all_to_all(copies, 'band', 0, 0, axis_index_groups=groups)]
    ppermute x2, starting transfers between devices: 3.16 us -> 1.77 us  [both_ways(): lax.ppermute(values, 'dom', ring)]
    ppermute x2, starting transfers between devices: 1.31 us -> 2.7 us  [both_ways(): lax.ppermute(values, 'dom', [(b, a) for a, b in ring])]
    ppermute x6, starting transfers between devices: 8.89 us -> 7.89 us  [along_z(): return lax.ppermute(values, ('band', 'dom'), pairs)]
    unnamed x12 -> x14, local copies, waits for them, and re-layouts: 0.03 us -> 1 us
    ppermute x2, waiting for transfers between devices: 8.27 us -> 7.39 us  [both_ways(): lax.ppermute(values, 'dom', [(b, a) for a, b in ring])]
  transfers between devices with their start and end apart: 17 -> 17, of which waited for: 10 -> 8; matrix products, arithmetic and copies ran while one was open for 1% -> 1% of each run, Pallas kernels for 3% -> 3%
where the time goes in v3:
time: 67.1 us; the launch traced here: 66.7 us
  starting transfers between devices  37.2 us (55%)
  waiting for transfers between devices  20.3 us (30%)
  Pallas kernels  6.07 us (9%)
  local copies, waits for them, and re-layouts  1.59 us (2%)
  between operations  1.55 us (2%)
    ppermute x6, starting transfers between devices, along_z(): return lax.ppermute(values, ('band', 'dom'), pairs)  7.89 us
    all_to_all x1, starting transfers between devices, on_device(): pieces = lax.all_to_all(twice, 'band', 0, 0, axis_index_groups=groups)  7.73 us
    ppermute x2, waiting for transfers between devices, both_ways(): lax.ppermute(values, 'dom', [(b, a) for a, b in ring])  7.39 us
    ppermute x1, starting transfers between devices, on_device(): lax.ppermute(mine, 'band', [(i, (i + PLANE) % bands) for i in range(bands)])  6.99 us
    all_to_all x1, waiting for transfers between devices, on_device(): pieces = lax.all_to_all(twice, 'band', 0, 0, axis_index_groups=groups)  6.39 us
    pallas_call x7, Pallas kernels, call(): pl.pallas_call(kernel, out_shape=out_shape, in_specs=specs, out_specs=jax...  5.2 us
    ppermute x6, waiting for transfers between devices, along_z(): return lax.ppermute(values, ('band', 'dom'), pairs)  4.27 us
    all_to_all x1, starting transfers between devices, on_device(): gathered = lax.all_to_all(copies, 'band', 0, 0, axis_index_groups=groups)  3.58 us
  transfers between devices with their start and end apart: 17, of which 8 were waited for; matrix products, arithmetic and copies ran while one was open for 1% of the time, Pallas kernels for 3%

profile of v3, /device:TPU:1, one launch (start us, length us, event | category | flops | bytes accessed | tf_op | source)
XLA Modules:
  0.0 66.7 jit_solution(9981278713952946972)
XLA Ops:
  0.0 1.0 %copy-done = bf16[8,6,24,128]{3,2,1,0:T(8,128)(2,1)S(1)} copy-done((bf16[8,6,24,128]{3,2,1,0:T(8,128)(2,1)S(1)}, bf16[8,6,24,128]{3,2,1,0:T(8,128)(2,1)}, u32[]{:S(2)}) %copy-start) | copy-done | bytes 294936
  1.0 0.9 %twice.1 = bf16[16,144,128]{2,1,0:T(8,128)(2,1)} custom-call(bf16[8,144,128]{2,1,0:T(8,128)(2,1)S(1)} %bitcast.9), custom_call_target="tpu_custom_call" | custom-call | tf_op jit(solution)/shard_map/twice/pallas_call | solution.py:212
  1.9 7.7 %all-to-all-start = ((bf16[16,144,128]{2,1,0:T(8,128)(2,1)}), bf16[16,144,128]{2,1,0:T(8,128)(2,1)S(1)}, u32[]{:S(2)}, u32[]{:S(2)}) async-start(bf16[16,144,128]{2,1,0:T(8,128)(2,1)} %twice.1), calls=%async_computation | async-start | bytes 1179648 | tf_op jit(solution)/shard_map/all_to_all | solution.py:221
  9.6 1.0 %collective-permute-start.2 = (bf16[8,144,128]{2,1,0:T(8,128)(2,1)S(1)}, bf16[8,144,128]{2,1,0:T(8,128)(2,1)S(1)}, u32[]{:S(2)}, u32[]{:S(2)}) collective-permute-start(bf16[8,144,128]{2,1,0:T(8,128)(2,1)S(1)} %bitcast.10), channel_id=1, source_target_pairs={{1,0},{2,1},{3,2},{4,3},{5,4},{6,5},{7,6},{0,7},{9,8},{10,9},{11,1... | collective-permute-start | bytes 884744 | tf_op jit(solution)/shard_map/ppermute | solution.py:201
  10.7 1.6 %collective-permute-start.1 = (bf16[8,144,128]{2,1,0:T(8,128)(2,1)S(1)}, bf16[8,144,128]{2,1,0:T(8,128)(2,1)S(1)}, u32[]{:S(2)}, u32[]{:S(2)}) collective-permute-start(bf16[8,144,128]{2,1,0:T(8,128)(2,1)S(1)} %bitcast.11), channel_id=1, source_target_pairs={{0,1},{1,2},{2,3},{3,4},{4,5},{5,6},{6,7},{7,0},{8,9},{9,10},{10,1... | collective-permute-start | bytes 884744 | tf_op jit(solution)/shard_map/ppermute | solution.py:201
  12.3 0.6 fusion
  14.2 6.4 %all-to-all-done = bf16[16,144,128]{2,1,0:T(8,128)(2,1)S(1)} async-done(((bf16[16,144,128]{2,1,0:T(8,128)(2,1)}), bf16[16,144,128]{2,1,0:T(8,128)(2,1)S(1)}, u32[]{:S(2)}, u32[]{:S(2)}) %all-to-all-start) | async-done | bytes 589856 | tf_op jit(solution)/shard_map/all_to_all | solution.py:221
  20.6 7.0 %collective-permute-start = (bf16[144,128]{1,0:T(8,128)(2,1)S(1)}, bf16[144,128]{1,0:T(8,128)(2,1)S(1)}, u32[]{:S(2)}, u32[]{:S(2)}) collective-permute-start(bf16[144,128]{1,0:T(8,128)(2,1)S(1)} %select_bitcast_fusion), channel_id=1, source_target_pairs={{0,128},{8,136},{16,144},{24,152},{32,160},{40,168},{48,176},{56,1... | collective-permute-start | bytes 110600 | tf_op jit(solution)/shard_map/ppermute | solution.py:227
  27.6 2.1 %collective-permute-start.8 = (f32[144,128]{1,0:T(8,128)S(1)}, f32[144,128]{1,0:T(8,128)S(1)}, u32[]{:S(2)}, u32[]{:S(2)}) collective-permute-start(f32[144,128]{1,0:T(8,128)S(1)} %bitcast.14), channel_id=1, source_target_pairs={{0,135},{1,0},{2,1},{3,2},{4,3},{5,4},{6,5},{7,6},{8,143},{9,8},{1... | collective-permute-start | bytes 221192 | tf_op jit(solution)/shard_map/ppermute | solution.py:209
  29.8 0.6 collective-permute-start.7
  30.4 0.5 first_inner.1.inner
  30.9 0.5 first.1.center
  31.4 2.0 %collective-permute-start.6 = (bf16[144,128]{1,0:T(8,128)(2,1)S(1)}, bf16[144,128]{1,0:T(8,128)(2,1)S(1)}, u32[]{:S(2)}, u32[]{:S(2)}) collective-permute-start(bf16[144,128]{1,0:T(8,128)(2,1)S(1)} %fusion.1.slab_c), channel_id=1, source_target_pairs={{0,134},{1,135},{2,0},{3,1},{4,2},{5,3},{6,4},{7,5},{8,142},{9,143... | collective-permute-start | bytes 110600 | tf_op jit(solution)/shard_map/ppermute | solution.py:209
  33.4 3.1 %collective-permute-start.5 = (bf16[144,128]{1,0:T(8,128)(2,1)S(1)}, bf16[144,128]{1,0:T(8,128)(2,1)S(1)}, u32[]{:S(2)}, u32[]{:S(2)}) collective-permute-start(bf16[144,128]{1,0:T(8,128)(2,1)S(1)} %fusion.1.slab_c), channel_id=1, source_target_pairs={{0,135},{1,0},{2,1},{3,2},{4,3},{5,4},{6,5},{7,6},{8,143},{9,8},{1... | collective-permute-start | bytes 110600 | tf_op jit(solution)/shard_map/ppermute | solution.py:209
  36.6 0.8 %collective-permute-done.5.slab_d = bf16[144,128]{1,0:T(8,128)(2,1)S(1)} collective-permute-done((bf16[144,128]{1,0:T(8,128)(2,1)S(1)}, bf16[144,128]{1,0:T(8,128)(2,1)S(1)}, u32[]{:S(2)}, u32[]{:S(2)}) %collective-permute-start.5) | collective-permute-done | bytes 36896 | tf_op jit(solution)/shard_map/ppermute | solution.py:209
  37.4 0.3 collective-permute-done.4.slab_b
  37.7 3.1 %collective-permute-done.3.slab_a = bf16[144,128]{1,0:T(8,128)(2,1)S(1)} collective-permute-done((bf16[144,128]{1,0:T(8,128)(2,1)S(1)}, bf16[144,128]{1,0:T(8,128)(2,1)S(1)}, u32[]{:S(2)}, u32[]{:S(2)}) %collective-permute-start.3) | collective-permute-done | bytes 36896 | tf_op jit(solution)/shard_map/ppermute | solution.py:209
  40.8 1.6 %owner.1 = bf16[16,144,128]{2,1,0:T(8,128)(2,1)} custom-call(bf16[144,128]{1,0:T(8,128)(2,1)S(1)} %collective-permute-done.3.slab_a, bf16[144,128]{1,0:T(8,128)(2,1)S(1)} %collective-permute-done.4.slab_b, bf16[144,128]{1,0:T(8,128)(2,1)S(1)} %fusion.1.slab_c, bf16[144,128]{1,0:T(8,128)(2,1)S(1)} %collective-permute-done.5.slab_d, ...), custom_call_target="tpu_custom_call" | custom-call | tf_op jit(solution)/shard_map/owner/pallas_call | solution.py:175
  42.4 3.6 %all-to-all-start.1 = ((bf16[16,144,128]{2,1,0:T(8,128)(2,1)}), bf16[16,144,128]{2,1,0:T(8,128)(2,1)S(1)}, u32[]{:S(2)}, u32[]{:S(2)}) async-start(bf16[16,144,128]{2,1,0:T(8,128)(2,1)} %owner.1), calls=%async_computation.1 | async-start | bytes 1179648 | tf_op jit(solution)/shard_map/all_to_all | solution.py:243
  46.0 1.7 %collective-permute-start.10 = (bf16[8,144,128]{2,1,0:T(8,128)(2,1)S(1)}, bf16[8,144,128]{2,1,0:T(8,128)(2,1)S(1)}, u32[]{:S(2)}, u32[]{:S(2)}) collective-permute-start(bf16[8,144,128]{2,1,0:T(8,128)(2,1)S(1)} %first.1.center), channel_id=1, source_target_pairs={{1,0},{2,1},{3,2},{4,3},{5,4},{6,5},{7,6},{0,7},{9,8},{10,9},{11,1... | collective-permute-start | bytes 884744 | tf_op jit(solution)/shard_map/ppermute | solution.py:201
  47.8 0.5 second_inner.1.inner
  48.3 7.4 %collective-permute-done.10.after = bf16[8,144,128]{2,1,0:T(8,128)(2,1)S(1)} collective-permute-done((bf16[8,144,128]{2,1,0:T(8,128)(2,1)S(1)}, bf16[8,144,128]{2,1,0:T(8,128)(2,1)S(1)}, u32[]{:S(2)}, u32[]{:S(2)}) %collective-permute-start.10) | collective-permute-done | bytes 294944 | tf_op jit(solution)/shard_map/ppermute | solution.py:201
  55.7 0.5 second.1.resident
  56.2 0.3 gram.1
  56.5 3.0 %collective-permute-start.11 = (f32[16,128]{1,0:T(8,128)S(1)}, f32[16,128]{1,0:T(8,128)S(1)}, u32[]{:S(2)}, u32[]{:S(2)}) collective-permute-start(f32[16,128]{1,0:T(8,128)S(1)} %get-tuple-element.11), channel_id=1, source_target_pairs={{0,1},{1,0},{2,3},{3,2},{4,5},{5,4},{6,7},{7,6},{8,9},{9,8},{10,11... | collective-permute-start | bytes 24584 | tf_op jit(solution)/shard_map/ppermute | solution.py:252
  59.5 0.8 %collective-permute-done.11 = f32[16,128]{1,0:T(8,128)S(1)} collective-permute-done((f32[16,128]{1,0:T(8,128)S(1)}, f32[16,128]{1,0:T(8,128)S(1)}, u32[]{:S(2)}, u32[]{:S(2)}) %collective-permute-start.11) | collective-permute-done | bytes 8224 | tf_op jit(solution)/shard_map/ppermute | solution.py:252
  60.4 0.3 collective-permute-start.14
  60.6 0.3 collective-permute-start.13
  60.9 3.0 %collective-permute-start.12 = (f32[16,128]{1,0:T(8,128)S(1)}, f32[16,128]{1,0:T(8,128)S(1)}, u32[]{:S(2)}, u32[]{:S(2)}) collective-permute-start(f32[16,128]{1,0:T(8,128)S(1)} %add.21), channel_id=1, source_target_pairs={{0,2},{1,3},{2,0},{3,1},{4,6},{5,7},{6,4},{7,5},{8,10},{9,11},{10,... | collective-permute-start | bytes 24584 | tf_op jit(solution)/shard_map/ppermute | solution.py:253
  63.9 0.8 %collective-permute-done.14 = f32[16,128]{1,0:T(8,128)S(1)} collective-permute-done((f32[16,128]{1,0:T(8,128)S(1)}, f32[16,128]{1,0:T(8,128)S(1)}, u32[]{:S(2)}, u32[]{:S(2)}) %collective-permute-start.14) | collective-permute-done | bytes 8224 | tf_op jit(solution)/shard_map/ppermute | solution.py:253
  64.7 0.6 collective-permute-done.12
  65.3 1.4 %project.1 = bf16[8,144,128]{2,1,0:T(8,128)(2,1)} custom-call(f32[16,128]{1,0:T(8,128)S(1)} %add_add_fusion.gram, bf16[128,2304]{1,0:T(8,128)(2,1)S(1)} %get-tuple-element.12.owned, bf16[8,144,128]{2,1,0:T(8,128)(2,1)S(1)} %second.1.resident), custom_call_target="tpu_custom_call" | custom-call | tf_op jit(solution)/shard_map/project/pallas_call | solution.py:175
  (29 shorter events, 0.3 us)
Async XLA Ops:
  0.0 1.0 %copy-start = (bf16[8,6,24,128]{3,2,1,0:T(8,128)(2,1)S(1)}, bf16[8,6,24,128]{3,2,1,0:T(8,128)(2,1)}, u32[]{:S(2)}) copy-start(bf16[8,6,24,128]{3,2,1,0:T(8,128)(2,1)} %param.6) | copy-start | bytes 884740
  1.8 7.8 %copy-start.1 = (bf16[8,6,24,128]{3,2,1,0:T(8,128)(2,1)S(1)}, bf16[8,6,24,128]{3,2,1,0:T(8,128)(2,1)}, u32[]{:S(2)}) copy-start(bf16[8,6,24,128]{3,2,1,0:T(8,128)(2,1)} %param.6) | copy-start | bytes 884740
  1.8 10.4 %copy-start.6 = (s32[2]{0:T(128)S(1)}, s32[2]{0:T(128)}, u32[]{:S(2)}) copy-start(s32[2]{0:T(128)} %param.8) | copy-start | bytes 28
  1.9 28.5 %copy-start.3 = (bf16[288,144]{1,0:T(8,128)(2,1)S(1)}, bf16[288,144]{1,0:T(8,128)(2,1)}, u32[]{:S(2)}) copy-start(bf16[288,144]{1,0:T(8,128)(2,1)} %constant.29.clone.inside) | copy-start | bytes 248836
  1.9 28.5 %copy-start.5 = (bf16[128,256]{1,0:T(8,128)(2,1)S(1)}, bf16[128,256]{1,0:T(8,128)(2,1)}, u32[]{:S(2)}) copy-start(bf16[128,256]{1,0:T(8,128)(2,1)} %constant.31.clone.along_x) | copy-start | bytes 196612
  1.9 18.7 %all-to-all-start = ((bf16[16,144,128]{2,1,0:T(8,128)(2,1)}), bf16[16,144,128]{2,1,0:T(8,128)(2,1)S(1)}, u32[]{:S(2)}, u32[]{:S(2)}) async-start(bf16[16,144,128]{2,1,0:T(8,128)(2,1)} %twice.1), calls=%async_computation | async-start | bytes 1179648 | tf_op jit(solution)/shard_map/all_to_all | solution.py:221
  9.6 18.0 %copy-start.4 = (f32[6,24,128]{2,1,0:T(8,128)S(1)}, f32[6,24,128]{2,1,0:T(8,128)}, u32[]{:S(2)}) copy-start(f32[6,24,128]{2,1,0:T(8,128)} %param.7) | copy-start | bytes 221188
  9.6 21.2 %collective-permute-start.2 = (bf16[8,144,128]{2,1,0:T(8,128)(2,1)S(1)}, bf16[8,144,128]{2,1,0:T(8,128)(2,1)S(1)}, u32[]{:S(2)}, u32[]{:S(2)}) collective-permute-start(bf16[8,144,128]{2,1,0:T(8,128)(2,1)S(1)} %bitcast.10), channel_id=1, source_target_pairs={{1,0},{2,1},{3,2},{4,3},{5,4},{6,5},{7,6},{0,7},{9,8},{10,9},{11,1... | collective-permute-start | bytes 884744 | tf_op jit(solution)/shard_map/ppermute | solution.py:201
  10.7 20.2 %collective-permute-start.1 = (bf16[8,144,128]{2,1,0:T(8,128)(2,1)S(1)}, bf16[8,144,128]{2,1,0:T(8,128)(2,1)S(1)}, u32[]{:S(2)}, u32[]{:S(2)}) collective-permute-start(bf16[8,144,128]{2,1,0:T(8,128)(2,1)S(1)} %bitcast.11), channel_id=1, source_target_pairs={{0,1},{1,2},{2,3},{3,4},{4,5},{5,6},{6,7},{7,0},{8,9},{9,10},{10,1... | collective-permute-start | bytes 884744 | tf_op jit(solution)/shard_map/ppermute | solution.py:201
  20.6 10.7 %collective-permute-start = (bf16[144,128]{1,0:T(8,128)(2,1)S(1)}, bf16[144,128]{1,0:T(8,128)(2,1)S(1)}, u32[]{:S(2)}, u32[]{:S(2)}) collective-permute-start(bf16[144,128]{1,0:T(8,128)(2,1)S(1)} %select_bitcast_fusion), channel_id=1, source_target_pairs={{0,128},{8,136},{16,144},{24,152},{32,160},{40,168},{48,176},{56,1... | collective-permute-start | bytes 110600 | tf_op jit(solution)/shard_map/ppermute | solution.py:227
  27.6 3.3 %copy-start.2 = (bf16[288,288]{1,0:T(8,128)(2,1)S(1)}, bf16[288,288]{1,0:T(8,128)(2,1)}, u32[]{:S(2)}) copy-start(bf16[288,288]{1,0:T(8,128)(2,1)} %constant.30.clone.beside) | copy-start | bytes 497668
  27.6 8.9 %collective-permute-start.8 = (f32[144,128]{1,0:T(8,128)S(1)}, f32[144,128]{1,0:T(8,128)S(1)}, u32[]{:S(2)}, u32[]{:S(2)}) collective-permute-start(f32[144,128]{1,0:T(8,128)S(1)} %bitcast.14), channel_id=1, source_target_pairs={{0,135},{1,0},{2,1},{3,2},{4,3},{5,4},{6,5},{7,6},{8,143},{9,8},{1... | collective-permute-start | bytes 221192 | tf_op jit(solution)/shard_map/ppermute | solution.py:209
  29.8 6.8 %collective-permute-start.7 = (f32[144,128]{1,0:T(8,128)S(1)}, f32[144,128]{1,0:T(8,128)S(1)}, u32[]{:S(2)}, u32[]{:S(2)}) collective-permute-start(f32[144,128]{1,0:T(8,128)S(1)} %bitcast.15), channel_id=1, source_target_pairs={{0,1},{1,2},{2,3},{3,4},{4,5},{5,6},{6,7},{7,128},{8,9},{9,10},{10... | collective-permute-start | bytes 221192 | tf_op jit(solution)/shard_map/ppermute | solution.py:209
  31.4 5.1 %collective-permute-start.6 = (bf16[144,128]{1,0:T(8,128)(2,1)S(1)}, bf16[144,128]{1,0:T(8,128)(2,1)S(1)}, u32[]{:S(2)}, u32[]{:S(2)}) collective-permute-start(bf16[144,128]{1,0:T(8,128)(2,1)S(1)} %fusion.1.slab_c), channel_id=1, source_target_pairs={{0,134},{1,135},{2,0},{3,1},{4,2},{5,3},{6,4},{7,5},{8,142},{9,143... | collective-permute-start | bytes 110600 | tf_op jit(solution)/shard_map/ppermute | solution.py:209
  33.4 4.0 %collective-permute-start.5 = (bf16[144,128]{1,0:T(8,128)(2,1)S(1)}, bf16[144,128]{1,0:T(8,128)(2,1)S(1)}, u32[]{:S(2)}, u32[]{:S(2)}) collective-permute-start(bf16[144,128]{1,0:T(8,128)(2,1)S(1)} %fusion.1.slab_c), channel_id=1, source_target_pairs={{0,135},{1,0},{2,1},{3,2},{4,3},{5,4},{6,5},{7,6},{8,143},{9,8},{1... | collective-permute-start | bytes 110600 | tf_op jit(solution)/shard_map/ppermute | solution.py:209
  36.5 1.2 %collective-permute-start.4 = (bf16[144,128]{1,0:T(8,128)(2,1)S(1)}, bf16[144,128]{1,0:T(8,128)(2,1)S(1)}, u32[]{:S(2)}, u32[]{:S(2)}) collective-permute-start(bf16[144,128]{1,0:T(8,128)(2,1)S(1)} %fusion.1.slab_c), channel_id=1, source_target_pairs={{0,1},{1,2},{2,3},{3,4},{4,5},{5,6},{6,7},{7,128},{8,9},{9,10},{10... | collective-permute-start | bytes 110600 | tf_op jit(solution)/shard_map/ppermute | solution.py:209
  36.5 4.3 %collective-permute-start.3 = (bf16[144,128]{1,0:T(8,128)(2,1)S(1)}, bf16[144,128]{1,0:T(8,128)(2,1)S(1)}, u32[]{:S(2)}, u32[]{:S(2)}) collective-permute-start(bf16[144,128]{1,0:T(8,128)(2,1)S(1)} %fusion.1.slab_c), channel_id=1, source_target_pairs={{0,2},{1,3},{2,4},{3,5},{4,6},{5,7},{6,128},{7,129},{8,10},{9,11},... | collective-permute-start | bytes 110600 | tf_op jit(solution)/shard_map/ppermute | solution.py:209
  42.4 13.8 %all-to-all-start.1 = ((bf16[16,144,128]{2,1,0:T(8,128)(2,1)}), bf16[16,144,128]{2,1,0:T(8,128)(2,1)S(1)}, u32[]{:S(2)}, u32[]{:S(2)}) async-start(bf16[16,144,128]{2,1,0:T(8,128)(2,1)} %owner.1), calls=%async_computation.1 | async-start | bytes 1179648 | tf_op jit(solution)/shard_map/all_to_all | solution.py:243
  46.0 9.7 %collective-permute-start.10 = (bf16[8,144,128]{2,1,0:T(8,128)(2,1)S(1)}, bf16[8,144,128]{2,1,0:T(8,128)(2,1)S(1)}, u32[]{:S(2)}, u32[]{:S(2)}) collective-permute-start(bf16[8,144,128]{2,1,0:T(8,128)(2,1)S(1)} %first.1.center), channel_id=1, source_target_pairs={{1,0},{2,1},{3,2},{4,3},{5,4},{6,5},{7,6},{0,7},{9,8},{10,9},{11,1... | collective-permute-start | bytes 884744 | tf_op jit(solution)/shard_map/ppermute | solution.py:201
  47.7 8.0 %collective-permute-start.9 = (bf16[8,144,128]{2,1,0:T(8,128)(2,1)S(1)}, bf16[8,144,128]{2,1,0:T(8,128)(2,1)S(1)}, u32[]{:S(2)}, u32[]{:S(2)}) collective-permute-start(bf16[8,144,128]{2,1,0:T(8,128)(2,1)S(1)} %first.1.center), channel_id=1, source_target_pairs={{0,1},{1,2},{2,3},{3,4},{4,5},{5,6},{6,7},{7,0},{8,9},{9,10},{10,1... | collective-permute-start | bytes 884744 | tf_op jit(solution)/shard_map/ppermute | solution.py:201
  56.5 3.8 %collective-permute-start.11 = (f32[16,128]{1,0:T(8,128)S(1)}, f32[16,128]{1,0:T(8,128)S(1)}, u32[]{:S(2)}, u32[]{:S(2)}) collective-permute-start(f32[16,128]{1,0:T(8,128)S(1)} %get-tuple-element.11), channel_id=1, source_target_pairs={{0,1},{1,0},{2,3},{3,2},{4,5},{5,4},{6,7},{7,6},{8,9},{9,8},{10,11... | collective-permute-start | bytes 24584 | tf_op jit(solution)/shard_map/ppermute | solution.py:252
  60.4 4.3 %collective-permute-start.14 = (f32[16,128]{1,0:T(8,128)S(1)}, f32[16,128]{1,0:T(8,128)S(1)}, u32[]{:S(2)}, u32[]{:S(2)}) collective-permute-start(f32[16,128]{1,0:T(8,128)S(1)} %add.21), channel_id=1, source_target_pairs={{0,6},{1,7},{2,4},{3,5},{4,2},{5,3},{6,0},{7,1},{8,14},{9,15},{10,... | collective-permute-start | bytes 24584 | tf_op jit(solution)/shard_map/ppermute | solution.py:253
  60.6 4.0 %collective-permute-start.13 = (f32[16,128]{1,0:T(8,128)S(1)}, f32[16,128]{1,0:T(8,128)S(1)}, u32[]{:S(2)}, u32[]{:S(2)}) collective-permute-start(f32[16,128]{1,0:T(8,128)S(1)} %add.21), channel_id=1, source_target_pairs={{0,4},{1,5},{2,6},{3,7},{4,0},{5,1},{6,2},{7,3},{8,12},{9,13},{10,... | collective-permute-start | bytes 24584 | tf_op jit(solution)/shard_map/ppermute | solution.py:253
  60.9 4.4 %collective-permute-start.12 = (f32[16,128]{1,0:T(8,128)S(1)}, f32[16,128]{1,0:T(8,128)S(1)}, u32[]{:S(2)}, u32[]{:S(2)}) collective-permute-start(f32[16,128]{1,0:T(8,128)S(1)} %add.21), channel_id=1, source_target_pairs={{0,2},{1,3},{2,0},{3,1},{4,6},{5,7},{6,4},{7,5},{8,10},{9,11},{10,... | collective-permute-start | bytes 24584 | tf_op jit(solution)/shard_map/ppermute | solution.py:253

commit v4 on v3

--- a/solution.py
+++ b/solution.py
@@ -84,8 +84,18 @@
         copy.wait()
 
 
-def inner_kernel(center, potential, inside, along_x, out):
-    for s, value in enumerate(inner_part(center[...], [diagonal_of(potential[...])] * center.shape[0], inside[...], along_x[...])):
+def first_inner_kernel(center, potential, inside, along_x, out, diagonal_out, terms_out):
+    diagonal = diagonal_of(potential[...])
+    diagonal_out[...] = diagonal
+    high = potential[...].astype(bf16)
+    terms_out[0] = high
+    terms_out[1] = (potential[...] - high.astype(f32)).astype(bf16)
+    for s, value in enumerate(inner_part(center[...], [diagonal] * center.shape[0], inside[...], along_x[...])):
+        out[s] = value
+
+
+def second_inner_kernel(center, diagonal, inside, along_x, out):
+    for s, value in enumerate(inner_part(center[...], [diagonal[...]] * center.shape[0], inside[...], along_x[...])):
         out[s] = value
 
 
@@ -99,14 +109,14 @@
         out[s] = (2.0 * (inner[s] + value) - states[s].astype(f32)).astype(bf16)
 
 
-def owner_kernel(slab_a, slab_b, slab_c, slab_d, slab_e, pot_b, pot_c, pot_d, inside, beside, along_x, out):
+def owner_kernel(slab_a, near_b, slab_c, near_d, slab_e, diagonal, inside, beside, along_x, out):
     inside, beside, along_x = inside[...], beside[...], along_x[...]
-    middle = jnp.stack([slab_b[...], slab_c[...], slab_d[...]])
-    first = []
-    before = jnp.stack([slab_a[...], slab_b[...], slab_c[...]])
-    after = jnp.stack([slab_c[...], slab_d[...], slab_e[...]])
+    middle = jnp.stack([near_b[0], slab_c[...], near_d[0]])
+    before = jnp.stack([slab_a[...], near_b[0], slab_c[...]])
+    after = jnp.stack([slab_c[...], near_d[0], slab_e[...]])
     outer = outer_part(before, after, beside)
-    diagonals = [diagonal_of(p[...]) for p in (pot_b, pot_c, pot_d)]
+    beside_diagonals = [diagonal_of(n[1].astype(f32) + n[2].astype(f32)) for n in (near_b, near_d)]
+    diagonals = [beside_diagonals[0], diagonal[...], beside_diagonals[1]]
     inner = inner_part(middle, diagonals, inside, along_x)
     first = [(i + o).astype(bf16)[None] for i, o in zip(inner, outer)]
     value = inner_part(first[1], diagonals[1:2], inside, along_x)[0] + outer_part(first[0], first[2], beside)[0]
@@ -147,7 +157,12 @@
     lanes = gram.shape[1]
     group = lax.broadcasted_iota(jnp.int32, (lanes, lanes), 0) // GROUP
     same_group = jnp.where(group == lax.broadcasted_iota(jnp.int32, (lanes, lanes), 1) // GROUP, 1.0, 0.0)
-    sums = jnp.dot(gram[...], same_group, precision=lax.Precision.HIGHEST, preferred_element_type=f32)
+    left, terms = gram[...], []
+    for _ in range(3):
+        terms.append(left.astype(bf16))
+        left = left - terms[-1].astype(f32)
+    sums = jnp.dot(jnp.concatenate(terms, axis=0), same_group.astype(bf16), preferred_element_type=f32)
+    sums = sums[: 2 * count] + (sums[2 * count : 4 * count] + sums[4 * count :])
     one = sums[:count] * weight
     two = sums[count:]
     for k in range(count):
@@ -220,25 +235,30 @@
     )(states)
     pieces = lax.all_to_all(twice, "band", 0, 0, axis_index_groups=groups)
     before, after = both_ways(states)
-    inner = call(inner_kernel, wide, [vmem] * 4, states, potential, inside, along_x, name="first_inner")
+    flat = jax.ShapeDtypeStruct(cells, f32)
+    terms = jax.ShapeDtypeStruct((2,) + cells, bf16)
+    inner, diagonal, terms = call(
+        first_inner_kernel, (wide, flat, terms), [vmem] * 4, states, potential, inside, along_x, name="first_inner"
+    )
     owner = jnp.where((band >> 3) & 1 == 0, owners[0], owners[1])
     mine = lax.dynamic_index_in_dim(pieces, owner & (PLANE - 1), 0, keepdims=False)
     mine = jnp.where(owner >> 4 == band >> 4, mine, jnp.zeros_like(mine))
     other = lax.ppermute(mine, "band", [(i, (i + PLANE) % bands) for i in range(bands)])
     first = call(first_kernel, block, [vmem] * 4, before, after, inner, beside, name="first")
-    other, first = lax.optimization_barrier((other, first))
+    other, first, terms = lax.optimization_barrier((other, first, terms))
     raw = mine + other
-    near = [along_z(raw, step) for step in (1, -1, 2, -2)]
-    pot_before, pot_after = along_z(potential, 1), along_z(potential, -1)
-
+    bundle = jnp.concatenate([raw[None], terms], axis=0)
     before, after = both_ways(first)
-    inner = call(inner_kernel, wide, [vmem] * 4, first, potential, inside, along_x, name="second_inner")
+    inner = call(second_inner_kernel, wide, [vmem] * 4, first, diagonal, inside, along_x, name="second_inner")
+    near_before, near_after = along_z(bundle, 1), along_z(bundle, -1)
+    next_before, next_after = along_z(raw, 2), along_z(raw, -2)
+    next_after, inner = lax.optimization_barrier((next_after, inner))
+
     resident = call(second_kernel, block, [vmem] * 5, before, after, inner, states, beside, name="second")
 
     copies = call(
-        owner_kernel, jax.ShapeDtypeStruct((PLANE,) + cells, bf16), [vmem] * 11,
-        near[2], near[0], raw, near[1], near[3], pot_before, potential, pot_after, inside, beside, along_x,
-        name="owner",
+        owner_kernel, jax.ShapeDtypeStruct((PLANE,) + cells, bf16), [vmem] * 9,
+        next_before, near_before, raw, near_after, next_after, diagonal, inside, beside, along_x, name="owner",
     )
     gathered = lax.all_to_all(copies, "band", 0, 0, axis_index_groups=groups)
     gram, owned = call(

time: 67.1 us -> 66.6 us (level)
  waiting for transfers between devices: 20.3 us -> 19.5 us
    ppermute x2, waiting for transfers between devices: 7.39 us -> 4.29 us  [both_ways(): lax.ppermute(values, 'dom', [(b, a) for a, b in ring])]
    ppermute x2, waiting for transfers between devices: 0.01 us -> 2.36 us  [both_ways(): lax.ppermute(values, 'dom', ring)]
    ppermute x6 -> x4, starting transfers between devices: 7.89 us -> 6.96 us  [along_z(): return lax.ppermute(values, ('band', 'dom'), pairs)]
    ppermute x6 -> x4, waiting for transfers between devices: 4.27 us -> 3.55 us  [along_z(): return lax.ppermute(values, ('band', 'dom'), pairs)]
  transfers between devices with their start and end apart: 17 -> 15, of which waited for: 8 -> 9; matrix products, arithmetic and copies ran while one was open for 1% -> 1% of each run, Pallas kernels for 3% -> 3%
where the time goes in v4:
time: 66.6 us; the launch traced here: 66.2 us
  starting transfers between devices  37.1 us (56%)
  waiting for transfers between devices  19.5 us (29%)
  Pallas kernels  5.97 us (9%)
  local copies, waits for them, and re-layouts  2.02 us (3%)
  between operations  1.52 us (2%)
    all_to_all x1, starting transfers between devices, on_device(): pieces = lax.all_to_all(twice, 'band', 0, 0, axis_index_groups=groups)  7.73 us
    ppermute x1, starting transfers between devices, on_device(): lax.ppermute(mine, 'band', [(i, (i + PLANE) % bands) for i in range(bands)])  6.99 us
    ppermute x4, starting transfers between devices, along_z(): return lax.ppermute(values, ('band', 'dom'), pairs)  6.96 us
    all_to_all x1, waiting for transfers between devices, on_device(): pieces = lax.all_to_all(twice, 'band', 0, 0, axis_index_groups=groups)  6.39 us
    pallas_call x7, Pallas kernels, call(): pl.pallas_call(kernel, out_shape=out_shape, in_specs=specs, out_specs=jax...  5.11 us
    ppermute x2, waiting for transfers between devices, both_ways(): lax.ppermute(values, 'dom', [(b, a) for a, b in ring])  4.29 us
    all_to_all x1, starting transfers between devices, on_device(): gathered = lax.all_to_all(copies, 'band', 0, 0, axis_index_groups=groups)  3.58 us
    ppermute x4, waiting for transfers between devices, along_z(): return lax.ppermute(values, ('band', 'dom'), pairs)  3.55 us
  transfers between devices with their start and end apart: 15, of which 9 were waited for; matrix products, arithmetic and copies ran while one was open for 1% of the time, Pallas kernels for 3%

profile of v4, /device:TPU:1, one launch (start us, length us, event | category | flops | bytes accessed | tf_op | source)
XLA Modules:
  0.0 66.2 jit_solution(5022640672991177883)
XLA Ops:
  0.0 1.0 %copy-done = bf16[8,6,24,128]{3,2,1,0:T(8,128)(2,1)S(1)} copy-done((bf16[8,6,24,128]{3,2,1,0:T(8,128)(2,1)S(1)}, bf16[8,6,24,128]{3,2,1,0:T(8,128)(2,1)}, u32[]{:S(2)}) %copy-start) | copy-done | bytes 294936
  1.0 0.9 %twice.1 = bf16[16,144,128]{2,1,0:T(8,128)(2,1)} custom-call(bf16[8,144,128]{2,1,0:T(8,128)(2,1)S(1)} %bitcast.10), custom_call_target="tpu_custom_call" | custom-call | tf_op jit(solution)/shard_map/twice/pallas_call | solution.py:227
  1.9 7.7 %all-to-all-start = ((bf16[16,144,128]{2,1,0:T(8,128)(2,1)}), bf16[16,144,128]{2,1,0:T(8,128)(2,1)S(1)}, u32[]{:S(2)}, u32[]{:S(2)}) async-start(bf16[16,144,128]{2,1,0:T(8,128)(2,1)} %twice.1), calls=%async_computation | async-start | bytes 1179648 | tf_op jit(solution)/shard_map/all_to_all | solution.py:236
  9.6 1.0 %collective-permute-start.2 = (bf16[8,144,128]{2,1,0:T(8,128)(2,1)S(1)}, bf16[8,144,128]{2,1,0:T(8,128)(2,1)S(1)}, u32[]{:S(2)}, u32[]{:S(2)}) collective-permute-start(bf16[8,144,128]{2,1,0:T(8,128)(2,1)S(1)} %bitcast.11), channel_id=1, source_target_pairs={{1,0},{2,1},{3,2},{4,3},{5,4},{6,5},{7,6},{0,7},{9,8},{10,9},{11,1... | collective-permute-start | bytes 884744 | tf_op jit(solution)/shard_map/ppermute | solution.py:216
  10.7 1.6 %collective-permute-start.1 = (bf16[8,144,128]{2,1,0:T(8,128)(2,1)S(1)}, bf16[8,144,128]{2,1,0:T(8,128)(2,1)S(1)}, u32[]{:S(2)}, u32[]{:S(2)}) collective-permute-start(bf16[8,144,128]{2,1,0:T(8,128)(2,1)S(1)} %bitcast.12), channel_id=1, source_target_pairs={{0,1},{1,2},{2,3},{3,4},{4,5},{5,6},{6,7},{7,0},{8,9},{9,10},{10,1... | collective-permute-start | bytes 884744 | tf_op jit(solution)/shard_map/ppermute | solution.py:216
  12.3 0.6 fusion
  14.2 6.4 %all-to-all-done = bf16[16,144,128]{2,1,0:T(8,128)(2,1)S(1)} async-done(((bf16[16,144,128]{2,1,0:T(8,128)(2,1)}), bf16[16,144,128]{2,1,0:T(8,128)(2,1)S(1)}, u32[]{:S(2)}, u32[]{:S(2)}) %all-to-all-start) | async-done | bytes 589856 | tf_op jit(solution)/shard_map/all_to_all | solution.py:236
  20.6 7.0 %collective-permute-start = (bf16[144,128]{1,0:T(8,128)(2,1)S(1)}, bf16[144,128]{1,0:T(8,128)(2,1)S(1)}, u32[]{:S(2)}, u32[]{:S(2)}) collective-permute-start(bf16[144,128]{1,0:T(8,128)(2,1)S(1)} %select_bitcast_fusion), channel_id=1, source_target_pairs={{0,128},{8,136},{16,144},{24,152},{32,160},{40,168},{48,176},{56,1... | collective-permute-start | bytes 110600 | tf_op jit(solution)/shard_map/ppermute | solution.py:246
  27.6 0.5 first_inner.1
  28.1 0.4 copy-done.2
  28.6 0.5 first.1.center
  29.1 2.7 %collective-permute-start.5 = (bf16[3,144,128]{2,1,0:T(8,128)(2,1)S(1)}, bf16[3,144,128]{2,1,0:T(8,128)(2,1)S(1)}, u32[]{:S(2)}, u32[]{:S(2)}) collective-permute-start(bf16[3,144,128]{2,1,0:T(8,128)(2,1)S(1)} %pad_maximum_fusion), channel_id=1, source_target_pairs={{0,135},{1,0},{2,1},{3,2},{4,3},{5,4},{6,5},{7,6},{8,143},{9,8},{1... | collective-permute-start | bytes 331784 | tf_op jit(solution)/shard_map/ppermute | solution.py:224
  31.8 1.0 %collective-permute-start.4 = (bf16[3,144,128]{2,1,0:T(8,128)(2,1)S(1)}, bf16[3,144,128]{2,1,0:T(8,128)(2,1)S(1)}, u32[]{:S(2)}, u32[]{:S(2)}) collective-permute-start(bf16[3,144,128]{2,1,0:T(8,128)(2,1)S(1)} %pad_maximum_fusion), channel_id=1, source_target_pairs={{0,1},{1,2},{2,3},{3,4},{4,5},{5,6},{6,7},{7,128},{8,9},{9,10},{10... | collective-permute-start | bytes 331784 | tf_op jit(solution)/shard_map/ppermute | solution.py:224
  32.8 3.3 %collective-permute-start.6 = (bf16[144,128]{1,0:T(8,128)(2,1)S(1)}, bf16[144,128]{1,0:T(8,128)(2,1)S(1)}, u32[]{:S(2)}, u32[]{:S(2)}) collective-permute-start(bf16[144,128]{1,0:T(8,128)(2,1)S(1)} %fusion.1.slab_c), channel_id=1, source_target_pairs={{0,134},{1,135},{2,0},{3,1},{4,2},{5,3},{6,4},{7,5},{8,142},{9,143... | collective-permute-start | bytes 110600 | tf_op jit(solution)/shard_map/ppermute | solution.py:224
  36.1 0.5 second_inner.1.inner
  36.5 0.6 collective-permute-done.6.slab_e
  37.1 3.0 %collective-permute-done.3.slab_a = bf16[144,128]{1,0:T(8,128)(2,1)S(1)} collective-permute-done((bf16[144,128]{1,0:T(8,128)(2,1)S(1)}, bf16[144,128]{1,0:T(8,128)(2,1)S(1)}, u32[]{:S(2)}, u32[]{:S(2)}) %collective-permute-start.3) | collective-permute-done | bytes 36896 | tf_op jit(solution)/shard_map/ppermute | solution.py:224
  40.1 1.6 %owner.1 = bf16[16,144,128]{2,1,0:T(8,128)(2,1)} custom-call(bf16[144,128]{1,0:T(8,128)(2,1)S(1)} %collective-permute-done.3.slab_a, bf16[3,144,128]{2,1,0:T(8,128)(2,1)S(1)} %collective-permute-done.4.near_b, bf16[144,128]{1,0:T(8,128)(2,1)S(1)} %fusion.1.slab_c, bf16[3,144,128]{2,1,0:T(8,128)(2,1)S(1)} %collective-permute-done.5.near_d, ...), custom_call_target="tpu_custom_call" | custom-call | tf_op jit(solution)/shard_map/owner/pallas_call | solution.py:190
  41.7 3.6 %all-to-all-start.1 = ((bf16[16,144,128]{2,1,0:T(8,128)(2,1)}), bf16[16,144,128]{2,1,0:T(8,128)(2,1)S(1)}, u32[]{:S(2)}, u32[]{:S(2)}) async-start(bf16[16,144,128]{2,1,0:T(8,128)(2,1)} %owner.1), calls=%async_computation.1 | async-start | bytes 1179648 | tf_op jit(solution)/shard_map/all_to_all | solution.py:263
  45.3 2.2 %collective-permute-start.8 = (bf16[8,144,128]{2,1,0:T(8,128)(2,1)S(1)}, bf16[8,144,128]{2,1,0:T(8,128)(2,1)S(1)}, u32[]{:S(2)}, u32[]{:S(2)}) collective-permute-start(bf16[8,144,128]{2,1,0:T(8,128)(2,1)S(1)} %first.1.center), channel_id=1, source_target_pairs={{1,0},{2,1},{3,2},{4,3},{5,4},{6,5},{7,6},{0,7},{9,8},{10,9},{11,1... | collective-permute-start | bytes 884744 | tf_op jit(solution)/shard_map/ppermute | solution.py:216
  47.5 4.3 %collective-permute-done.8.after = bf16[8,144,128]{2,1,0:T(8,128)(2,1)S(1)} collective-permute-done((bf16[8,144,128]{2,1,0:T(8,128)(2,1)S(1)}, bf16[8,144,128]{2,1,0:T(8,128)(2,1)S(1)}, u32[]{:S(2)}, u32[]{:S(2)}) %collective-permute-start.8) | collective-permute-done | bytes 294944 | tf_op jit(solution)/shard_map/ppermute | solution.py:216
  51.8 2.4 %collective-permute-done.7.before = bf16[8,144,128]{2,1,0:T(8,128)(2,1)S(1)} collective-permute-done((bf16[8,144,128]{2,1,0:T(8,128)(2,1)S(1)}, bf16[8,144,128]{2,1,0:T(8,128)(2,1)S(1)}, u32[]{:S(2)}, u32[]{:S(2)}) %collective-permute-start.7) | collective-permute-done | bytes 294944 | tf_op jit(solution)/shard_map/ppermute | solution.py:216
  54.1 0.5 second.1.resident
  54.6 0.4 all-to-all-done.1.gathered
  55.0 0.3 gram.1
  55.4 3.5 %collective-permute-start.9 = (f32[16,128]{1,0:T(8,128)S(1)}, f32[16,128]{1,0:T(8,128)S(1)}, u32[]{:S(2)}, u32[]{:S(2)}) collective-permute-start(f32[16,128]{1,0:T(8,128)S(1)} %get-tuple-element.23), channel_id=1, source_target_pairs={{0,1},{1,0},{2,3},{3,2},{4,5},{5,4},{6,7},{7,6},{8,9},{9,8},{10,11... | collective-permute-start | bytes 24584 | tf_op jit(solution)/shard_map/ppermute | solution.py:272
  58.8 0.8 %collective-permute-done.9 = f32[16,128]{1,0:T(8,128)S(1)} collective-permute-done((f32[16,128]{1,0:T(8,128)S(1)}, f32[16,128]{1,0:T(8,128)S(1)}, u32[]{:S(2)}, u32[]{:S(2)}) %collective-permute-start.9) | collective-permute-done | bytes 8224 | tf_op jit(solution)/shard_map/ppermute | solution.py:272
  59.7 1.6 %collective-permute-start.12 = (f32[16,128]{1,0:T(8,128)S(1)}, f32[16,128]{1,0:T(8,128)S(1)}, u32[]{:S(2)}, u32[]{:S(2)}) collective-permute-start(f32[16,128]{1,0:T(8,128)S(1)} %add.21), channel_id=1, source_target_pairs={{0,6},{1,7},{2,4},{3,5},{4,2},{5,3},{6,0},{7,1},{8,14},{9,15},{10,... | collective-permute-start | bytes 24584 | tf_op jit(solution)/shard_map/ppermute | solution.py:273
  61.2 2.0 %collective-permute-start.10 = (f32[16,128]{1,0:T(8,128)S(1)}, f32[16,128]{1,0:T(8,128)S(1)}, u32[]{:S(2)}, u32[]{:S(2)}) collective-permute-start(f32[16,128]{1,0:T(8,128)S(1)} %add.21), channel_id=1, source_target_pairs={{0,2},{1,3},{2,0},{3,1},{4,6},{5,7},{6,4},{7,5},{8,10},{9,11},{10,... | collective-permute-start | bytes 24584 | tf_op jit(solution)/shard_map/ppermute | solution.py:273
  63.2 0.8 %collective-permute-done.12 = f32[16,128]{1,0:T(8,128)S(1)} collective-permute-done((f32[16,128]{1,0:T(8,128)S(1)}, f32[16,128]{1,0:T(8,128)S(1)}, u32[]{:S(2)}, u32[]{:S(2)}) %collective-permute-start.12) | collective-permute-done | bytes 8224 | tf_op jit(solution)/shard_map/ppermute | solution.py:273
  64.0 1.0 %collective-permute-done.11 = f32[16,128]{1,0:T(8,128)S(1)} collective-permute-done((f32[16,128]{1,0:T(8,128)S(1)}, f32[16,128]{1,0:T(8,128)S(1)}, u32[]{:S(2)}, u32[]{:S(2)}) %collective-permute-start.11) | collective-permute-done | bytes 8224 | tf_op jit(solution)/shard_map/ppermute | solution.py:273
  64.9 1.3 %project.1 = bf16[8,144,128]{2,1,0:T(8,128)(2,1)} custom-call(f32[16,128]{1,0:T(8,128)S(1)} %add_add_fusion.gram, bf16[128,2304]{1,0:T(8,128)(2,1)S(1)} %get-tuple-element.24.owned, bf16[8,144,128]{2,1,0:T(8,128)(2,1)S(1)} %second.1.resident), custom_call_target="tpu_custom_call" | custom-call | tf_op jit(solution)/shard_map/project/pallas_call | solution.py:190
  (26 shorter events, 0.1 us)
Async XLA Ops:
  0.0 1.0 %copy-start = (bf16[8,6,24,128]{3,2,1,0:T(8,128)(2,1)S(1)}, bf16[8,6,24,128]{3,2,1,0:T(8,128)(2,1)}, u32[]{:S(2)}) copy-start(bf16[8,6,24,128]{3,2,1,0:T(8,128)(2,1)} %param.6) | copy-start | bytes 884740
  1.8 7.8 %copy-start.1 = (bf16[8,6,24,128]{3,2,1,0:T(8,128)(2,1)S(1)}, bf16[8,6,24,128]{3,2,1,0:T(8,128)(2,1)}, u32[]{:S(2)}) copy-start(bf16[8,6,24,128]{3,2,1,0:T(8,128)(2,1)} %param.6) | copy-start | bytes 884740
  1.9 10.4 %copy-start.6 = (s32[2]{0:T(128)S(1)}, s32[2]{0:T(128)}, u32[]{:S(2)}) copy-start(s32[2]{0:T(128)} %param.8) | copy-start | bytes 28
  1.9 25.8 %copy-start.3 = (bf16[288,144]{1,0:T(8,128)(2,1)S(1)}, bf16[288,144]{1,0:T(8,128)(2,1)}, u32[]{:S(2)}) copy-start(bf16[288,144]{1,0:T(8,128)(2,1)} %constant.29.clone.inside) | copy-start | bytes 248836
  1.9 25.8 %copy-start.5 = (f32[6,24,128]{2,1,0:T(8,128)S(1)}, f32[6,24,128]{2,1,0:T(8,128)}, u32[]{:S(2)}) copy-start(f32[6,24,128]{2,1,0:T(8,128)} %param.7) | copy-start | bytes 221188
  1.9 18.7 %all-to-all-start = ((bf16[16,144,128]{2,1,0:T(8,128)(2,1)}), bf16[16,144,128]{2,1,0:T(8,128)(2,1)S(1)}, u32[]{:S(2)}, u32[]{:S(2)}) async-start(bf16[16,144,128]{2,1,0:T(8,128)(2,1)} %twice.1), calls=%async_computation | async-start | bytes 1179648 | tf_op jit(solution)/shard_map/all_to_all | solution.py:236
  9.6 18.0 %copy-start.4 = (bf16[128,256]{1,0:T(8,128)(2,1)S(1)}, bf16[128,256]{1,0:T(8,128)(2,1)}, u32[]{:S(2)}) copy-start(bf16[128,256]{1,0:T(8,128)(2,1)} %constant.31.clone.along_x) | copy-start | bytes 196612
  9.6 18.5 %collective-permute-start.2 = (bf16[8,144,128]{2,1,0:T(8,128)(2,1)S(1)}, bf16[8,144,128]{2,1,0:T(8,128)(2,1)S(1)}, u32[]{:S(2)}, u32[]{:S(2)}) collective-permute-start(bf16[8,144,128]{2,1,0:T(8,128)(2,1)S(1)} %bitcast.11), channel_id=1, source_target_pairs={{1,0},{2,1},{3,2},{4,3},{5,4},{6,5},{7,6},{0,7},{9,8},{10,9},{11,1... | collective-permute-start | bytes 884744 | tf_op jit(solution)/shard_map/ppermute | solution.py:216
  10.7 17.4 %collective-permute-start.1 = (bf16[8,144,128]{2,1,0:T(8,128)(2,1)S(1)}, bf16[8,144,128]{2,1,0:T(8,128)(2,1)S(1)}, u32[]{:S(2)}, u32[]{:S(2)}) collective-permute-start(bf16[8,144,128]{2,1,0:T(8,128)(2,1)S(1)} %bitcast.12), channel_id=1, source_target_pairs={{0,1},{1,2},{2,3},{3,4},{4,5},{5,6},{6,7},{7,0},{8,9},{9,10},{10,1... | collective-permute-start | bytes 884744 | tf_op jit(solution)/shard_map/ppermute | solution.py:216
  20.6 8.4 %collective-permute-start = (bf16[144,128]{1,0:T(8,128)(2,1)S(1)}, bf16[144,128]{1,0:T(8,128)(2,1)S(1)}, u32[]{:S(2)}, u32[]{:S(2)}) collective-permute-start(bf16[144,128]{1,0:T(8,128)(2,1)S(1)} %select_bitcast_fusion), channel_id=1, source_target_pairs={{0,128},{8,136},{16,144},{24,152},{32,160},{40,168},{48,176},{56,1... | collective-permute-start | bytes 110600 | tf_op jit(solution)/shard_map/ppermute | solution.py:246
  27.6 0.9 %copy-start.2 = (bf16[288,288]{1,0:T(8,128)(2,1)S(1)}, bf16[288,288]{1,0:T(8,128)(2,1)}, u32[]{:S(2)}) copy-start(bf16[288,288]{1,0:T(8,128)(2,1)} %constant.30.clone.beside) | copy-start | bytes 497668
  29.1 11.0 %collective-permute-start.5 = (bf16[3,144,128]{2,1,0:T(8,128)(2,1)S(1)}, bf16[3,144,128]{2,1,0:T(8,128)(2,1)S(1)}, u32[]{:S(2)}, u32[]{:S(2)}) collective-permute-start(bf16[3,144,128]{2,1,0:T(8,128)(2,1)S(1)} %pad_maximum_fusion), channel_id=1, source_target_pairs={{0,135},{1,0},{2,1},{3,2},{4,3},{5,4},{6,5},{7,6},{8,143},{9,8},{1... | collective-permute-start | bytes 331784 | tf_op jit(solution)/shard_map/ppermute | solution.py:224
  31.8 8.3 %collective-permute-start.4 = (bf16[3,144,128]{2,1,0:T(8,128)(2,1)S(1)}, bf16[3,144,128]{2,1,0:T(8,128)(2,1)S(1)}, u32[]{:S(2)}, u32[]{:S(2)}) collective-permute-start(bf16[3,144,128]{2,1,0:T(8,128)(2,1)S(1)} %pad_maximum_fusion), channel_id=1, source_target_pairs={{0,1},{1,2},{2,3},{3,4},{4,5},{5,6},{6,7},{7,128},{8,9},{9,10},{10... | collective-permute-start | bytes 331784 | tf_op jit(solution)/shard_map/ppermute | solution.py:224
  32.8 4.3 %collective-permute-start.6 = (bf16[144,128]{1,0:T(8,128)(2,1)S(1)}, bf16[144,128]{1,0:T(8,128)(2,1)S(1)}, u32[]{:S(2)}, u32[]{:S(2)}) collective-permute-start(bf16[144,128]{1,0:T(8,128)(2,1)S(1)} %fusion.1.slab_c), channel_id=1, source_target_pairs={{0,134},{1,135},{2,0},{3,1},{4,2},{5,3},{6,4},{7,5},{8,142},{9,143... | collective-permute-start | bytes 110600 | tf_op jit(solution)/shard_map/ppermute | solution.py:224
  36.1 4.0 %collective-permute-start.3 = (bf16[144,128]{1,0:T(8,128)(2,1)S(1)}, bf16[144,128]{1,0:T(8,128)(2,1)S(1)}, u32[]{:S(2)}, u32[]{:S(2)}) collective-permute-start(bf16[144,128]{1,0:T(8,128)(2,1)S(1)} %fusion.1.slab_c), channel_id=1, source_target_pairs={{0,2},{1,3},{2,4},{3,5},{4,6},{5,7},{6,128},{7,129},{8,10},{9,11},... | collective-permute-start | bytes 110600 | tf_op jit(solution)/shard_map/ppermute | solution.py:224
  41.7 13.3 %all-to-all-start.1 = ((bf16[16,144,128]{2,1,0:T(8,128)(2,1)}), bf16[16,144,128]{2,1,0:T(8,128)(2,1)S(1)}, u32[]{:S(2)}, u32[]{:S(2)}) async-start(bf16[16,144,128]{2,1,0:T(8,128)(2,1)} %owner.1), calls=%async_computation.1 | async-start | bytes 1179648 | tf_op jit(solution)/shard_map/all_to_all | solution.py:263
  45.3 6.5 %collective-permute-start.8 = (bf16[8,144,128]{2,1,0:T(8,128)(2,1)S(1)}, bf16[8,144,128]{2,1,0:T(8,128)(2,1)S(1)}, u32[]{:S(2)}, u32[]{:S(2)}) collective-permute-start(bf16[8,144,128]{2,1,0:T(8,128)(2,1)S(1)} %first.1.center), channel_id=1, source_target_pairs={{1,0},{2,1},{3,2},{4,3},{5,4},{6,5},{7,6},{0,7},{9,8},{10,9},{11,1... | collective-permute-start | bytes 884744 | tf_op jit(solution)/shard_map/ppermute | solution.py:216
  47.5 6.6 %collective-permute-start.7 = (bf16[8,144,128]{2,1,0:T(8,128)(2,1)S(1)}, bf16[8,144,128]{2,1,0:T(8,128)(2,1)S(1)}, u32[]{:S(2)}, u32[]{:S(2)}) collective-permute-start(bf16[8,144,128]{2,1,0:T(8,128)(2,1)S(1)} %first.1.center), channel_id=1, source_target_pairs={{0,1},{1,2},{2,3},{3,4},{4,5},{5,6},{6,7},{7,0},{8,9},{9,10},{10,1... | collective-permute-start | bytes 884744 | tf_op jit(solution)/shard_map/ppermute | solution.py:216
  55.4 4.3 %collective-permute-start.9 = (f32[16,128]{1,0:T(8,128)S(1)}, f32[16,128]{1,0:T(8,128)S(1)}, u32[]{:S(2)}, u32[]{:S(2)}) collective-permute-start(f32[16,128]{1,0:T(8,128)S(1)} %get-tuple-element.23), channel_id=1, source_target_pairs={{0,1},{1,0},{2,3},{3,2},{4,5},{5,4},{6,7},{7,6},{8,9},{9,8},{10,11... | collective-permute-start | bytes 24584 | tf_op jit(solution)/shard_map/ppermute | solution.py:272
  59.7 4.3 %collective-permute-start.12 = (f32[16,128]{1,0:T(8,128)S(1)}, f32[16,128]{1,0:T(8,128)S(1)}, u32[]{:S(2)}, u32[]{:S(2)}) collective-permute-start(f32[16,128]{1,0:T(8,128)S(1)} %add.21), channel_id=1, source_target_pairs={{0,6},{1,7},{2,4},{3,5},{4,2},{5,3},{6,0},{7,1},{8,14},{9,15},{10,... | collective-permute-start | bytes 24584 | tf_op jit(solution)/shard_map/ppermute | solution.py:273
  61.2 3.7 %collective-permute-start.11 = (f32[16,128]{1,0:T(8,128)S(1)}, f32[16,128]{1,0:T(8,128)S(1)}, u32[]{:S(2)}, u32[]{:S(2)}) collective-permute-start(f32[16,128]{1,0:T(8,128)S(1)} %add.21), channel_id=1, source_target_pairs={{0,4},{1,5},{2,6},{3,7},{4,0},{5,1},{6,2},{7,3},{8,12},{9,13},{10,... | collective-permute-start | bytes 24584 | tf_op jit(solution)/shard_map/ppermute | solution.py:273
  61.2 3.7 %collective-permute-start.10 = (f32[16,128]{1,0:T(8,128)S(1)}, f32[16,128]{1,0:T(8,128)S(1)}, u32[]{:S(2)}, u32[]{:S(2)}) collective-permute-start(f32[16,128]{1,0:T(8,128)S(1)} %add.21), channel_id=1, source_target_pairs={{0,2},{1,3},{2,0},{3,1},{4,6},{5,7},{6,4},{7,5},{8,10},{9,11},{10,... | collective-permute-start | bytes 24584 | tf_op jit(solution)/shard_map/ppermute | solution.py:273

commit v5 on v4

--- a/solution.py
+++ b/solution.py
@@ -75,15 +75,6 @@
     return [zy[:, s * nx : (s + 1) * nx] for s in range(count)]
 
 
-def twice_kernel(states, out, done):
-    count = states.shape[0]
-    copies = [pltpu.make_async_copy(states, out.at[pl.ds(k * count, count)], done.at[k]) for k in range(ROUNDS)]
-    for copy in copies:
-        copy.start()
-    for copy in copies:
-        copy.wait()
-
-
 def first_inner_kernel(center, potential, inside, along_x, out, diagonal_out, terms_out):
     diagonal = diagonal_of(potential[...])
     diagonal_out[...] = diagonal
@@ -99,17 +90,17 @@
         out[s] = value
 
 
-def first_kernel(before, after, inner, beside, out):
+def first_kernel(after, before, inner, beside, out):
     for s, value in enumerate(outer_part(before[...], after[...], beside[...])):
         out[s] = (inner[s] + value).astype(bf16)
 
 
-def second_kernel(before, after, inner, states, beside, out):
+def second_kernel(after, before, inner, states, beside, out):
     for s, value in enumerate(outer_part(before[...], after[...], beside[...])):
         out[s] = (2.0 * (inner[s] + value) - states[s].astype(f32)).astype(bf16)
 
 
-def owner_kernel(slab_a, near_b, slab_c, near_d, slab_e, diagonal, inside, beside, along_x, out):
+def owner_kernel(near_d, near_b, slab_e, slab_a, slab_c, diagonal, inside, beside, along_x, out):
     inside, beside, along_x = inside[...], beside[...], along_x[...]
     middle = jnp.stack([near_b[0], slab_c[...], near_d[0]])
     before = jnp.stack([slab_a[...], near_b[0], slab_c[...]])
@@ -141,7 +132,7 @@
     blocks = []
     for turn in range(ROUNDS):
         for s in range(count):
-            blocks.append(gathered[turn * count + s].astype(f32))
+            blocks.append(gathered[(2 * (s // 4) + turn) * 4 + s % 4].astype(f32))
     owned = by_rows(blocks)
     against = jnp.concatenate(
         [by_rows([resident[j].astype(f32) for j in range(count)]), owned[: count * GROUP]], axis=0
@@ -186,13 +177,14 @@
 params = pltpu.CompilerParams(vmem_limit_bytes=40 * 1024 * 1024)
 
 
-def call(kernel, out_shape, specs, *operands, name):
+def call(kernel, out_shape, specs, *operands, name, cost=None):
     return pl.pallas_call(
         kernel,
         out_shape=out_shape,
         in_specs=specs,
         out_specs=jax.tree.map(lambda _: vmem, out_shape),
         compiler_params=params,
+        cost_estimate=cost and pl.CostEstimate(flops=cost, bytes_accessed=1 << 20, transcendentals=0),
         name=name,
     )(*operands)
 
@@ -223,42 +215,41 @@
                 pairs.append((b * doms + d, (place // doms * PLANE + b % PLANE) * doms + place % doms))
         return lax.ppermute(values, ("band", "dom"), pairs)
 
-    hbm = pl.BlockSpec(memory_space=pltpu.HBM)
-    twice = pl.pallas_call(
-        twice_kernel,
-        out_shape=jax.ShapeDtypeStruct((ROUNDS * count,) + cells, bf16),
-        in_specs=[hbm],
-        out_specs=hbm,
-        scratch_shapes=[pltpu.SemaphoreType.DMA((ROUNDS,))],
-        compiler_params=params,
-        name="twice",
-    )(states)
-    pieces = lax.all_to_all(twice, "band", 0, 0, axis_index_groups=groups)
+    x_odd, z_hi = (band >> 2) & 1, band >> 4
+    spread_groups = [
+        [z * PLANE + x * 4 + y for x in (odd, odd + 2) for y in range(4)] for z in range(2) for odd in range(2)
+    ]
+    pieces = lax.all_to_all(states, "band", 0, 0, axis_index_groups=spread_groups)
     before, after = both_ways(states)
     flat = jax.ShapeDtypeStruct(cells, f32)
     terms = jax.ShapeDtypeStruct((2,) + cells, bf16)
     inner, diagonal, terms = call(
         first_inner_kernel, (wide, flat, terms), [vmem] * 4, states, potential, inside, along_x, name="first_inner"
     )
-    owner = jnp.where((band >> 3) & 1 == 0, owners[0], owners[1])
-    mine = lax.dynamic_index_in_dim(pieces, owner & (PLANE - 1), 0, keepdims=False)
-    mine = jnp.where(owner >> 4 == band >> 4, mine, jnp.zeros_like(mine))
-    other = lax.ppermute(mine, "band", [(i, (i + PLANE) % bands) for i in range(bands)])
-    first = call(first_kernel, block, [vmem] * 4, before, after, inner, beside, name="first")
+    def piece_of(owner):
+        piece = lax.dynamic_index_in_dim(pieces, ((owner >> 3) & 1) * 4 + (owner & 3), 0, keepdims=False)
+        here = jnp.logical_and(owner >> 4 == z_hi, (owner >> 2) & 1 == x_odd)
+        return jnp.where(here, piece, jnp.zeros_like(piece))
+
+    kept = piece_of(jnp.where(x_odd == 0, owners[0], owners[1]))
+    sent = piece_of(jnp.where(x_odd == 0, owners[1], owners[0]))
+    mine = kept + lax.ppermute(sent, "band", [(i, i ^ 4) for i in range(bands)])
+    other = lax.ppermute(mine, "band", [(i, i ^ PLANE) for i in range(bands)])
+    first = call(first_kernel, block, [vmem] * 4, after, before, inner, beside, name="first", cost=2*10**10)
     other, first, terms = lax.optimization_barrier((other, first, terms))
     raw = mine + other
     bundle = jnp.concatenate([raw[None], terms], axis=0)
     before, after = both_ways(first)
-    inner = call(second_inner_kernel, wide, [vmem] * 4, first, diagonal, inside, along_x, name="second_inner")
+    inner = call(second_inner_kernel, wide, [vmem] * 4, first, diagonal, inside, along_x, name="second_inner", cost=None)
     near_before, near_after = along_z(bundle, 1), along_z(bundle, -1)
     next_before, next_after = along_z(raw, 2), along_z(raw, -2)
     next_after, inner = lax.optimization_barrier((next_after, inner))
 
-    resident = call(second_kernel, block, [vmem] * 5, before, after, inner, states, beside, name="second")
+    resident = call(second_kernel, block, [vmem] * 5, after, before, inner, states, beside, name="second")
 
     copies = call(
         owner_kernel, jax.ShapeDtypeStruct((PLANE,) + cells, bf16), [vmem] * 9,
-        next_before, near_before, raw, near_after, next_after, diagonal, inside, beside, along_x, name="owner",
+        near_after, near_before, next_after, next_before, raw, diagonal, inside, beside, along_x, name="owner",
     )
     gathered = lax.all_to_all(copies, "band", 0, 0, axis_index_groups=groups)
     gram, owned = call(
@@ -270,7 +261,7 @@
         [vmem] * 2, gathered, resident, name="gram",
     )
     gram = gram + lax.ppermute(gram, "dom", [(i, i ^ 1) for i in range(doms)])
-    gram = gram + sum(lax.ppermute(gram, "dom", [(i, i ^ s) for i in range(doms)]) for s in range(2, doms, 2))
+    gram = gram + sum(lax.ppermute(gram, "dom", [(i, i ^ s) for i in range(doms)]) for s in range(doms - 2, 0, -2))
     result = call(
         functools.partial(project_kernel, weight), block, [vmem] * 3, gram, owned, resident, name="project"
     )

time: 66.6 us -> 66.1 us (level)
  local copies, waits for them, and re-layouts: 2.02 us -> 0.61 us
  between operations: 1.52 us -> 2.62 us
  Pallas kernels: 5.97 us -> 5.1 us
  starting transfers between devices: 37.1 us -> 37.9 us
    ppermute x2, waiting for transfers between devices: 4.29 us -> 7.86 us  [both_ways(): lax.ppermute(values, 'dom', [(b, a) for a, b in ring])]
    all_to_all x1, waiting for transfers between devices: 6.39 us -> 3.22 us  [on_device(): lax.all_to_all(states, 'band', 0, 0, axis_index_groups=spread_groups)]
    ppermute x2, waiting for transfers between devices: 2.36 us -> 0.01 us  [both_ways(): lax.ppermute(values, 'dom', ring)]
    ppermute x1 -> x2, waiting for transfers between devices: 0.01 us -> 1.9 us  [the longest x1 1.04 us: on_device(): mine = kept + lax.ppermute(sent, 'band', [(i, i ^ 4) for i in range(bands)])]
    ppermute x4, starting transfers between devices: 6.96 us -> 8.62 us  [along_z(): return lax.ppermute(values, ('band', 'dom'), pairs)]
    unnamed x14 -> x12, local copies, waits for them, and re-layouts: 1.43 us -> 0.03 us
    ppermute x1, starting transfers between devices: 3.46 us -> 2.37 us  [on_device(): gram = gram + lax.ppermute(gram, 'dom', [(i, i ^ 1) for i in range(doms)])]
    pallas_call x1 -> x0, Pallas kernels: 0.87 us -> none  [on_device(): pl.pallas_call(twice_kernel, out_shape=jax.ShapeDtypeStruct((ROUNDS * cou...]
  transfers between devices with their start and end apart: 15 -> 16, of which waited for: 9 -> 10; matrix products, arithmetic and copies ran while one was open for 1% -> 1% of each run, Pallas kernels for 3% -> 3%
where the time goes in v5:
time: 66.1 us; the launch traced here: 65.6 us
  starting transfers between devices  37.9 us (57%)
  waiting for transfers between devices  19.4 us (29%)
  Pallas kernels  5.1 us (8%)
  between operations  2.62 us (4%)
    ppermute x4, starting transfers between devices, along_z(): return lax.ppermute(values, ('band', 'dom'), pairs)  8.62 us
    ppermute x2, waiting for transfers between devices, both_ways(): lax.ppermute(values, 'dom', [(b, a) for a, b in ring])  7.86 us
    all_to_all x1, starting transfers between devices, on_device(): lax.all_to_all(states, 'band', 0, 0, axis_index_groups=spread_groups)  7.62 us
    ppermute x1, starting transfers between devices, on_device(): other = lax.ppermute(mine, 'band', [(i, i ^ PLANE) for i in range(bands)])  6.7 us
    pallas_call x7, Pallas kernels, call(): pl.pallas_call(kernel, out_shape=out_shape, in_specs=specs, out_specs=jax...  5.1 us
    all_to_all x1, starting transfers between devices, on_device(): gathered = lax.all_to_all(copies, 'band', 0, 0, axis_index_groups=groups)  4.14 us
    ppermute x4, waiting for transfers between devices, along_z(): return lax.ppermute(values, ('band', 'dom'), pairs)  3.55 us
    ppermute x3, starting transfers between devices, on_device(): lax.ppermute(gram, 'dom', [(i, i ^ s) for i in range(doms)])  3.55 us
  transfers between devices with their start and end apart: 16, of which 10 were waited for; matrix products, arithmetic and copies ran while one was open for 1% of the time, Pallas kernels for 3%

profile of v5, /device:TPU:1, one launch (start us, length us, event | category | flops | bytes accessed | tf_op | source)
XLA Modules:
  0.0 65.6 jit_solution(1623965114071942927)
XLA Ops:
  0.0 7.6 %all-to-all-start = ((bf16[8,144,128]{2,1,0:T(8,128)(2,1)}), bf16[8,144,128]{2,1,0:T(8,128)(2,1)S(1)}, u32[]{:S(2)}, u32[]{:S(2)}) async-start(bf16[8,144,128]{2,1,0:T(8,128)(2,1)} %bitcast.10), calls=%async_computation | async-start | bytes 589824 | tf_op jit(solution)/shard_map/all_to_all | solution.py:222
  7.7 1.0 %collective-permute-start.2 = (bf16[8,144,128]{2,1,0:T(8,128)(2,1)S(1)}, bf16[8,144,128]{2,1,0:T(8,128)(2,1)S(1)}, u32[]{:S(2)}, u32[]{:S(2)}) collective-permute-start(bf16[8,144,128]{2,1,0:T(8,128)(2,1)S(1)} %bitcast.11), channel_id=1, source_target_pairs={{1,0},{2,1},{3,2},{4,3},{5,4},{6,5},{7,6},{0,7},{9,8},{10,9},{11,1... | collective-permute-start | bytes 884744 | tf_op jit(solution)/shard_map/ppermute | solution.py:208
  8.7 1.6 %collective-permute-start.3 = (bf16[8,144,128]{2,1,0:T(8,128)(2,1)S(1)}, bf16[8,144,128]{2,1,0:T(8,128)(2,1)S(1)}, u32[]{:S(2)}, u32[]{:S(2)}) collective-permute-start(bf16[8,144,128]{2,1,0:T(8,128)(2,1)S(1)} %bitcast.12), channel_id=1, source_target_pairs={{0,1},{1,2},{2,3},{3,4},{4,5},{5,6},{6,7},{7,0},{8,9},{9,10},{10,1... | collective-permute-start | bytes 884744 | tf_op jit(solution)/shard_map/ppermute | solution.py:208
  10.3 0.6 fusion
  12.1 3.2 %all-to-all-done = bf16[8,144,128]{2,1,0:T(8,128)(2,1)S(1)} async-done(((bf16[8,144,128]{2,1,0:T(8,128)(2,1)}), bf16[8,144,128]{2,1,0:T(8,128)(2,1)S(1)}, u32[]{:S(2)}, u32[]{:S(2)}) %all-to-all-start) | async-done | bytes 294944 | tf_op jit(solution)/shard_map/all_to_all | solution.py:222
  15.4 0.4 collective-permute-start
  17.0 0.5 first_inner.1
  17.5 1.0 %collective-permute-done = bf16[144,128]{1,0:T(8,128)(2,1)S(1)} collective-permute-done((bf16[144,128]{1,0:T(8,128)(2,1)S(1)}, bf16[144,128]{1,0:T(8,128)(2,1)S(1)}, u32[]{:S(2)}, u32[]{:S(2)}) %collective-permute-start) | collective-permute-done | bytes 36896 | tf_op jit(solution)/shard_map/ppermute | solution.py:236
  18.6 6.7 %collective-permute-start.1 = (bf16[144,128]{1,0:T(8,128)(2,1)S(1)}, bf16[144,128]{1,0:T(8,128)(2,1)S(1)}, u32[]{:S(2)}, u32[]{:S(2)}) collective-permute-start(bf16[144,128]{1,0:T(8,128)(2,1)S(1)} %bitcast_add_fusion), channel_id=1, source_target_pairs={{0,128},{8,136},{16,144},{24,152},{32,160},{40,168},{48,176},{56,1... | collective-permute-start | bytes 110600 | tf_op jit(solution)/shard_map/ppermute | solution.py:237
  25.3 0.5 first.1.center
  25.7 0.9 %collective-permute-done.1 = bf16[144,128]{1,0:T(8,128)(2,1)S(1)} collective-permute-done((bf16[144,128]{1,0:T(8,128)(2,1)S(1)}, bf16[144,128]{1,0:T(8,128)(2,1)S(1)}, u32[]{:S(2)}, u32[]{:S(2)}) %collective-permute-start.1) | collective-permute-done | bytes 36896 | tf_op jit(solution)/shard_map/ppermute | solution.py:237
  26.7 4.3 %collective-permute-start.4 = (bf16[3,144,128]{2,1,0:T(8,128)(2,1)S(1)}, bf16[3,144,128]{2,1,0:T(8,128)(2,1)S(1)}, u32[]{:S(2)}, u32[]{:S(2)}) collective-permute-start(bf16[3,144,128]{2,1,0:T(8,128)(2,1)S(1)} %pad_maximum_fusion), channel_id=1, source_target_pairs={{0,135},{1,0},{2,1},{3,2},{4,3},{5,4},{6,5},{7,6},{8,143},{9,8},{1... | collective-permute-start | bytes 331784 | tf_op jit(solution)/shard_map/ppermute | solution.py:216
  31.0 0.6 collective-permute-start.5
  31.6 3.7 %collective-permute-start.6 = (bf16[144,128]{1,0:T(8,128)(2,1)S(1)}, bf16[144,128]{1,0:T(8,128)(2,1)S(1)}, u32[]{:S(2)}, u32[]{:S(2)}) collective-permute-start(bf16[144,128]{1,0:T(8,128)(2,1)S(1)} %add.36.slab_c), channel_id=1, source_target_pairs={{0,134},{1,135},{2,0},{3,1},{4,2},{5,3},{6,4},{7,5},{8,142},{9,143... | collective-permute-start | bytes 110600 | tf_op jit(solution)/shard_map/ppermute | solution.py:216
  35.3 0.5 second_inner.1.inner
  35.7 0.6 collective-permute-done.6.slab_e
  36.3 3.0 %collective-permute-done.7.slab_a = bf16[144,128]{1,0:T(8,128)(2,1)S(1)} collective-permute-done((bf16[144,128]{1,0:T(8,128)(2,1)S(1)}, bf16[144,128]{1,0:T(8,128)(2,1)S(1)}, u32[]{:S(2)}, u32[]{:S(2)}) %collective-permute-start.7) | collective-permute-done | bytes 36896 | tf_op jit(solution)/shard_map/ppermute | solution.py:216
  39.3 1.6 %owner.1 = bf16[16,144,128]{2,1,0:T(8,128)(2,1)} custom-call(bf16[3,144,128]{2,1,0:T(8,128)(2,1)S(1)} %collective-permute-done.4.near_d, bf16[3,144,128]{2,1,0:T(8,128)(2,1)S(1)} %collective-permute-done.5.near_b, bf16[144,128]{1,0:T(8,128)(2,1)S(1)} %collective-permute-done.6.slab_e, bf16[144,128]{1,0:T(8,128)(2,1)S(1)} %collective-permute-done.7.slab_a, ...), custom_call_target="tpu_custom_call" | custom-call | tf_op jit(solution)/shard_map/owner/pallas_call | solution.py:181
  40.9 4.1 %all-to-all-start.1 = ((bf16[16,144,128]{2,1,0:T(8,128)(2,1)}), bf16[16,144,128]{2,1,0:T(8,128)(2,1)S(1)}, u32[]{:S(2)}, u32[]{:S(2)}) async-start(bf16[16,144,128]{2,1,0:T(8,128)(2,1)} %owner.1), calls=%async_computation.1 | async-start | bytes 1179648 | tf_op jit(solution)/shard_map/all_to_all | solution.py:254
  45.0 1.5 %collective-permute-start.8 = (bf16[8,144,128]{2,1,0:T(8,128)(2,1)S(1)}, bf16[8,144,128]{2,1,0:T(8,128)(2,1)S(1)}, u32[]{:S(2)}, u32[]{:S(2)}) collective-permute-start(bf16[8,144,128]{2,1,0:T(8,128)(2,1)S(1)} %first.1.center), channel_id=1, source_target_pairs={{1,0},{2,1},{3,2},{4,3},{5,4},{6,5},{7,6},{0,7},{9,8},{10,9},{11,1... | collective-permute-start | bytes 884744 | tf_op jit(solution)/shard_map/ppermute | solution.py:208
  46.5 0.4 collective-permute-start.9
  46.9 7.9 %collective-permute-done.8.after = bf16[8,144,128]{2,1,0:T(8,128)(2,1)S(1)} collective-permute-done((bf16[8,144,128]{2,1,0:T(8,128)(2,1)S(1)}, bf16[8,144,128]{2,1,0:T(8,128)(2,1)S(1)}, u32[]{:S(2)}, u32[]{:S(2)}) %collective-permute-start.8) | collective-permute-done | bytes 294944 | tf_op jit(solution)/shard_map/ppermute | solution.py:208
  54.7 0.5 second.1.resident
  55.2 0.7 %all-to-all-done.1.gathered = bf16[16,144,128]{2,1,0:T(8,128)(2,1)S(1)} async-done(((bf16[16,144,128]{2,1,0:T(8,128)(2,1)}), bf16[16,144,128]{2,1,0:T(8,128)(2,1)S(1)}, u32[]{:S(2)}, u32[]{:S(2)}) %all-to-all-start.1) | async-done | bytes 589856 | tf_op jit(solution)/shard_map/all_to_all | solution.py:254
  55.9 0.3 gram.1
  56.3 2.4 %collective-permute-start.10 = (f32[16,128]{1,0:T(8,128)S(1)}, f32[16,128]{1,0:T(8,128)S(1)}, u32[]{:S(2)}, u32[]{:S(2)}) collective-permute-start(f32[16,128]{1,0:T(8,128)S(1)} %get-tuple-element.23), channel_id=1, source_target_pairs={{0,1},{1,0},{2,3},{3,2},{4,5},{5,4},{6,7},{7,6},{8,9},{9,8},{10,11... | collective-permute-start | bytes 24584 | tf_op jit(solution)/shard_map/ppermute | solution.py:263
  58.6 0.8 %collective-permute-done.10 = f32[16,128]{1,0:T(8,128)S(1)} collective-permute-done((f32[16,128]{1,0:T(8,128)S(1)}, f32[16,128]{1,0:T(8,128)S(1)}, u32[]{:S(2)}, u32[]{:S(2)}) %collective-permute-start.10) | collective-permute-done | bytes 8224 | tf_op jit(solution)/shard_map/ppermute | solution.py:263
  59.5 0.9 %collective-permute-start.11 = (f32[16,128]{1,0:T(8,128)S(1)}, f32[16,128]{1,0:T(8,128)S(1)}, u32[]{:S(2)}, u32[]{:S(2)}) collective-permute-start(f32[16,128]{1,0:T(8,128)S(1)} %add.37), channel_id=1, source_target_pairs={{0,6},{1,7},{2,4},{3,5},{4,2},{5,3},{6,0},{7,1},{8,14},{9,15},{10,... | collective-permute-start | bytes 24584 | tf_op jit(solution)/shard_map/ppermute | solution.py:264
  60.3 2.7 %collective-permute-start.13 = (f32[16,128]{1,0:T(8,128)S(1)}, f32[16,128]{1,0:T(8,128)S(1)}, u32[]{:S(2)}, u32[]{:S(2)}) collective-permute-start(f32[16,128]{1,0:T(8,128)S(1)} %add.37), channel_id=1, source_target_pairs={{0,2},{1,3},{2,0},{3,1},{4,6},{5,7},{6,4},{7,5},{8,10},{9,11},{10,... | collective-permute-start | bytes 24584 | tf_op jit(solution)/shard_map/ppermute | solution.py:264
  63.0 0.8 %collective-permute-done.11 = f32[16,128]{1,0:T(8,128)S(1)} collective-permute-done((f32[16,128]{1,0:T(8,128)S(1)}, f32[16,128]{1,0:T(8,128)S(1)}, u32[]{:S(2)}, u32[]{:S(2)}) %collective-permute-start.11) | collective-permute-done | bytes 8224 | tf_op jit(solution)/shard_map/ppermute | solution.py:264
  63.8 0.5 collective-permute-done.13
  64.3 1.3 %project.1 = bf16[8,144,128]{2,1,0:T(8,128)(2,1)} custom-call(f32[16,128]{1,0:T(8,128)S(1)} %add_add_fusion.gram, bf16[128,2304]{1,0:T(8,128)(2,1)S(1)} %get-tuple-element.24.owned, bf16[8,144,128]{2,1,0:T(8,128)(2,1)S(1)} %second.1.resident), custom_call_target="tpu_custom_call" | custom-call | tf_op jit(solution)/shard_map/project/pallas_call | solution.py:181
  (26 shorter events, 0.1 us)
Async XLA Ops:
  0.0 7.6 %copy-start = (bf16[8,6,24,128]{3,2,1,0:T(8,128)(2,1)S(1)}, bf16[8,6,24,128]{3,2,1,0:T(8,128)(2,1)}, u32[]{:S(2)}) copy-start(bf16[8,6,24,128]{3,2,1,0:T(8,128)(2,1)} %param.6) | copy-start | bytes 884740
  0.0 10.3 %copy-start.5 = (s32[2]{0:T(128)S(1)}, s32[2]{0:T(128)}, u32[]{:S(2)}) copy-start(s32[2]{0:T(128)} %param.8) | copy-start | bytes 28
  0.0 17.0 %copy-start.3 = (bf16[128,256]{1,0:T(8,128)(2,1)S(1)}, bf16[128,256]{1,0:T(8,128)(2,1)}, u32[]{:S(2)}) copy-start(bf16[128,256]{1,0:T(8,128)(2,1)} %constant.33.clone.along_x) | copy-start | bytes 196612
  0.0 17.0 %copy-start.4 = (f32[6,24,128]{2,1,0:T(8,128)S(1)}, f32[6,24,128]{2,1,0:T(8,128)}, u32[]{:S(2)}) copy-start(f32[6,24,128]{2,1,0:T(8,128)} %param.7) | copy-start | bytes 221188
  0.0 15.3 %all-to-all-start = ((bf16[8,144,128]{2,1,0:T(8,128)(2,1)}), bf16[8,144,128]{2,1,0:T(8,128)(2,1)S(1)}, u32[]{:S(2)}, u32[]{:S(2)}) async-start(bf16[8,144,128]{2,1,0:T(8,128)(2,1)} %bitcast.10), calls=%async_computation | async-start | bytes 589824 | tf_op jit(solution)/shard_map/all_to_all | solution.py:222
  7.6 9.4 %copy-start.1 = (bf16[288,144]{1,0:T(8,128)(2,1)S(1)}, bf16[288,144]{1,0:T(8,128)(2,1)}, u32[]{:S(2)}) copy-start(bf16[288,144]{1,0:T(8,128)(2,1)} %constant.31.clone.inside) | copy-start | bytes 248836
  7.7 17.6 %collective-permute-start.2 = (bf16[8,144,128]{2,1,0:T(8,128)(2,1)S(1)}, bf16[8,144,128]{2,1,0:T(8,128)(2,1)S(1)}, u32[]{:S(2)}, u32[]{:S(2)}) collective-permute-start(bf16[8,144,128]{2,1,0:T(8,128)(2,1)S(1)} %bitcast.11), channel_id=1, source_target_pairs={{1,0},{2,1},{3,2},{4,3},{5,4},{6,5},{7,6},{0,7},{9,8},{10,9},{11,1... | collective-permute-start | bytes 884744 | tf_op jit(solution)/shard_map/ppermute | solution.py:208
  8.7 16.6 %collective-permute-start.3 = (bf16[8,144,128]{2,1,0:T(8,128)(2,1)S(1)}, bf16[8,144,128]{2,1,0:T(8,128)(2,1)S(1)}, u32[]{:S(2)}, u32[]{:S(2)}) collective-permute-start(bf16[8,144,128]{2,1,0:T(8,128)(2,1)S(1)} %bitcast.12), channel_id=1, source_target_pairs={{0,1},{1,2},{2,3},{3,4},{4,5},{5,6},{6,7},{7,0},{8,9},{9,10},{10,1... | collective-permute-start | bytes 884744 | tf_op jit(solution)/shard_map/ppermute | solution.py:208
  15.4 3.2 %collective-permute-start = (bf16[144,128]{1,0:T(8,128)(2,1)S(1)}, bf16[144,128]{1,0:T(8,128)(2,1)S(1)}, u32[]{:S(2)}, u32[]{:S(2)}) collective-permute-start(bf16[144,128]{1,0:T(8,128)(2,1)S(1)} %select_bitcast_fusion), channel_id=1, source_target_pairs={{0,32},{8,40},{16,48},{24,56},{32,0},{40,8},{48,16},{56,24},{64,96... | collective-permute-start | bytes 110600 | tf_op jit(solution)/shard_map/ppermute | solution.py:236
  17.0 8.2 %copy-start.2 = (bf16[288,288]{1,0:T(8,128)(2,1)S(1)}, bf16[288,288]{1,0:T(8,128)(2,1)}, u32[]{:S(2)}) copy-start(bf16[288,288]{1,0:T(8,128)(2,1)} %constant.32.clone.beside) | copy-start | bytes 497668
  18.6 8.1 %collective-permute-start.1 = (bf16[144,128]{1,0:T(8,128)(2,1)S(1)}, bf16[144,128]{1,0:T(8,128)(2,1)S(1)}, u32[]{:S(2)}, u32[]{:S(2)}) collective-permute-start(bf16[144,128]{1,0:T(8,128)(2,1)S(1)} %bitcast_add_fusion), channel_id=1, source_target_pairs={{0,128},{8,136},{16,144},{24,152},{32,160},{40,168},{48,176},{56,1... | collective-permute-start | bytes 110600 | tf_op jit(solution)/shard_map/ppermute | solution.py:237
  26.7 12.6 %collective-permute-start.4 = (bf16[3,144,128]{2,1,0:T(8,128)(2,1)S(1)}, bf16[3,144,128]{2,1,0:T(8,128)(2,1)S(1)}, u32[]{:S(2)}, u32[]{:S(2)}) collective-permute-start(bf16[3,144,128]{2,1,0:T(8,128)(2,1)S(1)} %pad_maximum_fusion), channel_id=1, source_target_pairs={{0,135},{1,0},{2,1},{3,2},{4,3},{5,4},{6,5},{7,6},{8,143},{9,8},{1... | collective-permute-start | bytes 331784 | tf_op jit(solution)/shard_map/ppermute | solution.py:216
  31.0 8.3 %collective-permute-start.5 = (bf16[3,144,128]{2,1,0:T(8,128)(2,1)S(1)}, bf16[3,144,128]{2,1,0:T(8,128)(2,1)S(1)}, u32[]{:S(2)}, u32[]{:S(2)}) collective-permute-start(bf16[3,144,128]{2,1,0:T(8,128)(2,1)S(1)} %pad_maximum_fusion), channel_id=1, source_target_pairs={{0,1},{1,2},{2,3},{3,4},{4,5},{5,6},{6,7},{7,128},{8,9},{9,10},{10... | collective-permute-start | bytes 331784 | tf_op jit(solution)/shard_map/ppermute | solution.py:216
  31.6 4.7 %collective-permute-start.6 = (bf16[144,128]{1,0:T(8,128)(2,1)S(1)}, bf16[144,128]{1,0:T(8,128)(2,1)S(1)}, u32[]{:S(2)}, u32[]{:S(2)}) collective-permute-start(bf16[144,128]{1,0:T(8,128)(2,1)S(1)} %add.36.slab_c), channel_id=1, source_target_pairs={{0,134},{1,135},{2,0},{3,1},{4,2},{5,3},{6,4},{7,5},{8,142},{9,143... | collective-permute-start | bytes 110600 | tf_op jit(solution)/shard_map/ppermute | solution.py:216
  35.3 4.0 %collective-permute-start.7 = (bf16[144,128]{1,0:T(8,128)(2,1)S(1)}, bf16[144,128]{1,0:T(8,128)(2,1)S(1)}, u32[]{:S(2)}, u32[]{:S(2)}) collective-permute-start(bf16[144,128]{1,0:T(8,128)(2,1)S(1)} %add.36.slab_c), channel_id=1, source_target_pairs={{0,2},{1,3},{2,4},{3,5},{4,6},{5,7},{6,128},{7,129},{8,10},{9,11},... | collective-permute-start | bytes 110600 | tf_op jit(solution)/shard_map/ppermute | solution.py:216
  40.9 15.0 %all-to-all-start.1 = ((bf16[16,144,128]{2,1,0:T(8,128)(2,1)}), bf16[16,144,128]{2,1,0:T(8,128)(2,1)S(1)}, u32[]{:S(2)}, u32[]{:S(2)}) async-start(bf16[16,144,128]{2,1,0:T(8,128)(2,1)} %owner.1), calls=%async_computation.1 | async-start | bytes 1179648 | tf_op jit(solution)/shard_map/all_to_all | solution.py:254
  45.0 9.7 %collective-permute-start.8 = (bf16[8,144,128]{2,1,0:T(8,128)(2,1)S(1)}, bf16[8,144,128]{2,1,0:T(8,128)(2,1)S(1)}, u32[]{:S(2)}, u32[]{:S(2)}) collective-permute-start(bf16[8,144,128]{2,1,0:T(8,128)(2,1)S(1)} %first.1.center), channel_id=1, source_target_pairs={{1,0},{2,1},{3,2},{4,3},{5,4},{6,5},{7,6},{0,7},{9,8},{10,9},{11,1... | collective-permute-start | bytes 884744 | tf_op jit(solution)/shard_map/ppermute | solution.py:208
  46.5 8.2 %collective-permute-start.9 = (bf16[8,144,128]{2,1,0:T(8,128)(2,1)S(1)}, bf16[8,144,128]{2,1,0:T(8,128)(2,1)S(1)}, u32[]{:S(2)}, u32[]{:S(2)}) collective-permute-start(bf16[8,144,128]{2,1,0:T(8,128)(2,1)S(1)} %first.1.center), channel_id=1, source_target_pairs={{0,1},{1,2},{2,3},{3,4},{4,5},{5,6},{6,7},{7,0},{8,9},{9,10},{10,1... | collective-permute-start | bytes 884744 | tf_op jit(solution)/shard_map/ppermute | solution.py:208
  56.3 3.2 %collective-permute-start.10 = (f32[16,128]{1,0:T(8,128)S(1)}, f32[16,128]{1,0:T(8,128)S(1)}, u32[]{:S(2)}, u32[]{:S(2)}) collective-permute-start(f32[16,128]{1,0:T(8,128)S(1)} %get-tuple-element.23), channel_id=1, source_target_pairs={{0,1},{1,0},{2,3},{3,2},{4,5},{5,4},{6,7},{7,6},{8,9},{9,8},{10,11... | collective-permute-start | bytes 24584 | tf_op jit(solution)/shard_map/ppermute | solution.py:263
  59.5 4.3 %collective-permute-start.11 = (f32[16,128]{1,0:T(8,128)S(1)}, f32[16,128]{1,0:T(8,128)S(1)}, u32[]{:S(2)}, u32[]{:S(2)}) collective-permute-start(f32[16,128]{1,0:T(8,128)S(1)} %add.37), channel_id=1, source_target_pairs={{0,6},{1,7},{2,4},{3,5},{4,2},{5,3},{6,0},{7,1},{8,14},{9,15},{10,... | collective-permute-start | bytes 24584 | tf_op jit(solution)/shard_map/ppermute | solution.py:264
  60.3 3.5 %collective-permute-start.12 = (f32[16,128]{1,0:T(8,128)S(1)}, f32[16,128]{1,0:T(8,128)S(1)}, u32[]{:S(2)}, u32[]{:S(2)}) collective-permute-start(f32[16,128]{1,0:T(8,128)S(1)} %add.37), channel_id=1, source_target_pairs={{0,4},{1,5},{2,6},{3,7},{4,0},{5,1},{6,2},{7,3},{8,12},{9,13},{10,... | collective-permute-start | bytes 24584 | tf_op jit(solution)/shard_map/ppermute | solution.py:264
  60.3 4.0 %collective-permute-start.13 = (f32[16,128]{1,0:T(8,128)S(1)}, f32[16,128]{1,0:T(8,128)S(1)}, u32[]{:S(2)}, u32[]{:S(2)}) collective-permute-start(f32[16,128]{1,0:T(8,128)S(1)} %add.37), channel_id=1, source_target_pairs={{0,2},{1,3},{2,0},{3,1},{4,6},{5,7},{6,4},{7,5},{8,10},{9,11},{10,... | collective-permute-start | bytes 24584 | tf_op jit(solution)/shard_map/ppermute | solution.py:264

commit v6 on v5

--- a/solution.py
+++ b/solution.py
@@ -143,12 +143,12 @@
     rows_out[...] = owned
 
 
-def project_kernel(weight, gram, owned, resident, out):
+def project_kernel(weight, part_a, part_b, part_c, gram, owned, resident, out):
     count, rows, nx = resident.shape
     lanes = gram.shape[1]
     group = lax.broadcasted_iota(jnp.int32, (lanes, lanes), 0) // GROUP
     same_group = jnp.where(group == lax.broadcasted_iota(jnp.int32, (lanes, lanes), 1) // GROUP, 1.0, 0.0)
-    left, terms = gram[...], []
+    left, terms = (gram[...] + part_a[...]) + (part_b[...] + part_c[...]), []
     for _ in range(3):
         terms.append(left.astype(bf16))
         left = left - terms[-1].astype(f32)
@@ -261,9 +261,9 @@
         [vmem] * 2, gathered, resident, name="gram",
     )
     gram = gram + lax.ppermute(gram, "dom", [(i, i ^ 1) for i in range(doms)])
-    gram = gram + sum(lax.ppermute(gram, "dom", [(i, i ^ s) for i in range(doms)]) for s in range(doms - 2, 0, -2))
+    parts = [lax.ppermute(gram, "dom", [(i, i ^ s) for i in range(doms)]) for s in (6, 2, 4)]
     result = call(
-        functools.partial(project_kernel, weight), block, [vmem] * 3, gram, owned, resident, name="project"
+        functools.partial(project_kernel, weight), block, [vmem] * 6, *parts, gram, owned, resident, name="project"
     )
     return result.reshape(count, planes, ny, nx)
 

time: 66.1 us -> 65.7 us (level)
  no operation moved by 1% of the time
where the time goes in v6:
time: 65.7 us; the launch traced here: 65.4 us
  starting transfers between devices  37.9 us (58%)
  waiting for transfers between devices  19.1 us (29%)
  Pallas kernels  5.11 us (8%)
  between operations  2.62 us (4%)
    ppermute x4, starting transfers between devices, along_z(): return lax.ppermute(values, ('band', 'dom'), pairs)  8.62 us
    ppermute x2, waiting for transfers between devices, both_ways(): lax.ppermute(values, 'dom', [(b, a) for a, b in ring])  7.86 us
    all_to_all x1, starting transfers between devices, on_device(): lax.all_to_all(states, 'band', 0, 0, axis_index_groups=spread_groups)  7.62 us
    ppermute x1, starting transfers between devices, on_device(): other = lax.ppermute(mine, 'band', [(i, i ^ PLANE) for i in range(bands)])  6.7 us
    pallas_call x7, Pallas kernels, call(): pl.pallas_call(kernel, out_shape=out_shape, in_specs=specs, out_specs=jax...  5.11 us
    all_to_all x1, starting transfers between devices, on_device(): gathered = lax.all_to_all(copies, 'band', 0, 0, axis_index_groups=groups)  4.14 us
    ppermute x4, waiting for transfers between devices, along_z(): return lax.ppermute(values, ('band', 'dom'), pairs)  3.55 us
    ppermute x3, starting transfers between devices, on_device(): lax.ppermute(gram, 'dom', [(i, i ^ s) for i in range(doms)])  3.55 us
  transfers between devices with their start and end apart: 16, of which 10 were waited for; matrix products, arithmetic and copies ran while one was open for 1% of the time, Pallas kernels for 3%

profile of v6, /device:TPU:1, one launch (start us, length us, event | category | flops | bytes accessed | tf_op | source)
XLA Modules:
  0.0 65.4 jit_solution(13382694121264093565)
XLA Ops:
  0.0 7.6 %all-to-all-start = ((bf16[8,144,128]{2,1,0:T(8,128)(2,1)}), bf16[8,144,128]{2,1,0:T(8,128)(2,1)S(1)}, u32[]{:S(2)}, u32[]{:S(2)}) async-start(bf16[8,144,128]{2,1,0:T(8,128)(2,1)} %bitcast.10), calls=%async_computation | async-start | bytes 589824 | tf_op jit(solution)/shard_map/all_to_all | solution.py:222
  7.7 1.0 %collective-permute-start.2 = (bf16[8,144,128]{2,1,0:T(8,128)(2,1)S(1)}, bf16[8,144,128]{2,1,0:T(8,128)(2,1)S(1)}, u32[]{:S(2)}, u32[]{:S(2)}) collective-permute-start(bf16[8,144,128]{2,1,0:T(8,128)(2,1)S(1)} %bitcast.11), channel_id=1, source_target_pairs={{1,0},{2,1},{3,2},{4,3},{5,4},{6,5},{7,6},{0,7},{9,8},{10,9},{11,1... | collective-permute-start | bytes 884744 | tf_op jit(solution)/shard_map/ppermute | solution.py:208
  8.7 1.6 %collective-permute-start.3 = (bf16[8,144,128]{2,1,0:T(8,128)(2,1)S(1)}, bf16[8,144,128]{2,1,0:T(8,128)(2,1)S(1)}, u32[]{:S(2)}, u32[]{:S(2)}) collective-permute-start(bf16[8,144,128]{2,1,0:T(8,128)(2,1)S(1)} %bitcast.12), channel_id=1, source_target_pairs={{0,1},{1,2},{2,3},{3,4},{4,5},{5,6},{6,7},{7,0},{8,9},{9,10},{10,1... | collective-permute-start | bytes 884744 | tf_op jit(solution)/shard_map/ppermute | solution.py:208
  10.3 0.6 fusion
  12.1 3.2 %all-to-all-done = bf16[8,144,128]{2,1,0:T(8,128)(2,1)S(1)} async-done(((bf16[8,144,128]{2,1,0:T(8,128)(2,1)}), bf16[8,144,128]{2,1,0:T(8,128)(2,1)S(1)}, u32[]{:S(2)}, u32[]{:S(2)}) %all-to-all-start) | async-done | bytes 294944 | tf_op jit(solution)/shard_map/all_to_all | solution.py:222
  15.4 0.4 collective-permute-start
  17.0 0.5 first_inner.1
  17.5 1.0 %collective-permute-done = bf16[144,128]{1,0:T(8,128)(2,1)S(1)} collective-permute-done((bf16[144,128]{1,0:T(8,128)(2,1)S(1)}, bf16[144,128]{1,0:T(8,128)(2,1)S(1)}, u32[]{:S(2)}, u32[]{:S(2)}) %collective-permute-start) | collective-permute-done | bytes 36896 | tf_op jit(solution)/shard_map/ppermute | solution.py:236
  18.6 6.7 %collective-permute-start.1 = (bf16[144,128]{1,0:T(8,128)(2,1)S(1)}, bf16[144,128]{1,0:T(8,128)(2,1)S(1)}, u32[]{:S(2)}, u32[]{:S(2)}) collective-permute-start(bf16[144,128]{1,0:T(8,128)(2,1)S(1)} %bitcast_add_fusion), channel_id=1, source_target_pairs={{0,128},{8,136},{16,144},{24,152},{32,160},{40,168},{48,176},{56,1... | collective-permute-start | bytes 110600 | tf_op jit(solution)/shard_map/ppermute | solution.py:237
  25.3 0.5 first.1.center
  25.7 0.9 %collective-permute-done.1 = bf16[144,128]{1,0:T(8,128)(2,1)S(1)} collective-permute-done((bf16[144,128]{1,0:T(8,128)(2,1)S(1)}, bf16[144,128]{1,0:T(8,128)(2,1)S(1)}, u32[]{:S(2)}, u32[]{:S(2)}) %collective-permute-start.1) | collective-permute-done | bytes 36896 | tf_op jit(solution)/shard_map/ppermute | solution.py:237
  26.7 4.3 %collective-permute-start.4 = (bf16[3,144,128]{2,1,0:T(8,128)(2,1)S(1)}, bf16[3,144,128]{2,1,0:T(8,128)(2,1)S(1)}, u32[]{:S(2)}, u32[]{:S(2)}) collective-permute-start(bf16[3,144,128]{2,1,0:T(8,128)(2,1)S(1)} %pad_maximum_fusion), channel_id=1, source_target_pairs={{0,135},{1,0},{2,1},{3,2},{4,3},{5,4},{6,5},{7,6},{8,143},{9,8},{1... | collective-permute-start | bytes 331784 | tf_op jit(solution)/shard_map/ppermute | solution.py:216
  31.0 0.6 collective-permute-start.5
  31.6 3.7 %collective-permute-start.6 = (bf16[144,128]{1,0:T(8,128)(2,1)S(1)}, bf16[144,128]{1,0:T(8,128)(2,1)S(1)}, u32[]{:S(2)}, u32[]{:S(2)}) collective-permute-start(bf16[144,128]{1,0:T(8,128)(2,1)S(1)} %add.27.slab_c), channel_id=1, source_target_pairs={{0,134},{1,135},{2,0},{3,1},{4,2},{5,3},{6,4},{7,5},{8,142},{9,143... | collective-permute-start | bytes 110600 | tf_op jit(solution)/shard_map/ppermute | solution.py:216
  35.3 0.5 second_inner.1.inner
  35.7 0.6 collective-permute-done.6.slab_e
  36.3 3.0 %collective-permute-done.7.slab_a = bf16[144,128]{1,0:T(8,128)(2,1)S(1)} collective-permute-done((bf16[144,128]{1,0:T(8,128)(2,1)S(1)}, bf16[144,128]{1,0:T(8,128)(2,1)S(1)}, u32[]{:S(2)}, u32[]{:S(2)}) %collective-permute-start.7) | collective-permute-done | bytes 36896 | tf_op jit(solution)/shard_map/ppermute | solution.py:216
  39.3 1.6 %owner.1 = bf16[16,144,128]{2,1,0:T(8,128)(2,1)} custom-call(bf16[3,144,128]{2,1,0:T(8,128)(2,1)S(1)} %collective-permute-done.4.near_d, bf16[3,144,128]{2,1,0:T(8,128)(2,1)S(1)} %collective-permute-done.5.near_b, bf16[144,128]{1,0:T(8,128)(2,1)S(1)} %collective-permute-done.6.slab_e, bf16[144,128]{1,0:T(8,128)(2,1)S(1)} %collective-permute-done.7.slab_a, ...), custom_call_target="tpu_custom_call" | custom-call | tf_op jit(solution)/shard_map/owner/pallas_call | solution.py:181
  40.9 4.1 %all-to-all-start.1 = ((bf16[16,144,128]{2,1,0:T(8,128)(2,1)}), bf16[16,144,128]{2,1,0:T(8,128)(2,1)S(1)}, u32[]{:S(2)}, u32[]{:S(2)}) async-start(bf16[16,144,128]{2,1,0:T(8,128)(2,1)} %owner.1), calls=%async_computation.1 | async-start | bytes 1179648 | tf_op jit(solution)/shard_map/all_to_all | solution.py:254
  45.0 1.5 %collective-permute-start.8 = (bf16[8,144,128]{2,1,0:T(8,128)(2,1)S(1)}, bf16[8,144,128]{2,1,0:T(8,128)(2,1)S(1)}, u32[]{:S(2)}, u32[]{:S(2)}) collective-permute-start(bf16[8,144,128]{2,1,0:T(8,128)(2,1)S(1)} %first.1.center), channel_id=1, source_target_pairs={{1,0},{2,1},{3,2},{4,3},{5,4},{6,5},{7,6},{0,7},{9,8},{10,9},{11,1... | collective-permute-start | bytes 884744 | tf_op jit(solution)/shard_map/ppermute | solution.py:208
  46.5 0.4 collective-permute-start.9
  46.9 7.9 %collective-permute-done.8.after = bf16[8,144,128]{2,1,0:T(8,128)(2,1)S(1)} collective-permute-done((bf16[8,144,128]{2,1,0:T(8,128)(2,1)S(1)}, bf16[8,144,128]{2,1,0:T(8,128)(2,1)S(1)}, u32[]{:S(2)}, u32[]{:S(2)}) %collective-permute-start.8) | collective-permute-done | bytes 294944 | tf_op jit(solution)/shard_map/ppermute | solution.py:208
  54.7 0.5 second.1.resident
  55.2 0.7 %all-to-all-done.1.gathered = bf16[16,144,128]{2,1,0:T(8,128)(2,1)S(1)} async-done(((bf16[16,144,128]{2,1,0:T(8,128)(2,1)}), bf16[16,144,128]{2,1,0:T(8,128)(2,1)S(1)}, u32[]{:S(2)}, u32[]{:S(2)}) %all-to-all-start.1) | async-done | bytes 589856 | tf_op jit(solution)/shard_map/all_to_all | solution.py:254
  55.9 0.3 gram.1
  56.3 2.4 %collective-permute-start.10 = (f32[16,128]{1,0:T(8,128)S(1)}, f32[16,128]{1,0:T(8,128)S(1)}, u32[]{:S(2)}, u32[]{:S(2)}) collective-permute-start(f32[16,128]{1,0:T(8,128)S(1)} %get-tuple-element.23), channel_id=1, source_target_pairs={{0,1},{1,0},{2,3},{3,2},{4,5},{5,4},{6,7},{7,6},{8,9},{9,8},{10,11... | collective-permute-start | bytes 24584 | tf_op jit(solution)/shard_map/ppermute | solution.py:263
  58.6 0.8 %collective-permute-done.10 = f32[16,128]{1,0:T(8,128)S(1)} collective-permute-done((f32[16,128]{1,0:T(8,128)S(1)}, f32[16,128]{1,0:T(8,128)S(1)}, u32[]{:S(2)}, u32[]{:S(2)}) %collective-permute-start.10) | collective-permute-done | bytes 8224 | tf_op jit(solution)/shard_map/ppermute | solution.py:263
  59.5 0.9 %collective-permute-start.11 = (f32[16,128]{1,0:T(8,128)S(1)}, f32[16,128]{1,0:T(8,128)S(1)}, u32[]{:S(2)}, u32[]{:S(2)}) collective-permute-start(f32[16,128]{1,0:T(8,128)S(1)} %add.28.gram), channel_id=1, source_target_pairs={{0,6},{1,7},{2,4},{3,5},{4,2},{5,3},{6,0},{7,1},{8,14},{9,15},{10,... | collective-permute-start | bytes 24584 | tf_op jit(solution)/shard_map/ppermute | solution.py:264
  60.3 2.7 %collective-permute-start.13 = (f32[16,128]{1,0:T(8,128)S(1)}, f32[16,128]{1,0:T(8,128)S(1)}, u32[]{:S(2)}, u32[]{:S(2)}) collective-permute-start(f32[16,128]{1,0:T(8,128)S(1)} %add.28.gram), channel_id=1, source_target_pairs={{0,4},{1,5},{2,6},{3,7},{4,0},{5,1},{6,2},{7,3},{8,12},{9,13},{10,... | collective-permute-start | bytes 24584 | tf_op jit(solution)/shard_map/ppermute | solution.py:264
  63.0 0.8 %collective-permute-done.11.part_a = f32[16,128]{1,0:T(8,128)S(1)} collective-permute-done((f32[16,128]{1,0:T(8,128)S(1)}, f32[16,128]{1,0:T(8,128)S(1)}, u32[]{:S(2)}, u32[]{:S(2)}) %collective-permute-start.11) | collective-permute-done | bytes 8224 | tf_op jit(solution)/shard_map/ppermute | solution.py:264
  63.8 0.3 collective-permute-done.13.part_c
  64.0 1.3 %project.1 = bf16[8,144,128]{2,1,0:T(8,128)(2,1)} custom-call(f32[16,128]{1,0:T(8,128)S(1)} %collective-permute-done.11.part_a, f32[16,128]{1,0:T(8,128)S(1)} %collective-permute-done.12.part_b, f32[16,128]{1,0:T(8,128)S(1)} %collective-permute-done.13.part_c, f32[16,128]{1,0:T(8,128)S(1)} %add.28.gram, bf16[128,2304]{1,0:T(8,128)(2,1)S(1)} %get-tuple-element.24.owned, ...), custom_call_target="tpu_custom_call" | custom-call | tf_op jit(solution)/shard_map/project/pallas_call | solution.py:181
  (25 shorter events, 0.1 us)
Async XLA Ops:
  0.0 7.6 %copy-start = (bf16[8,6,24,128]{3,2,1,0:T(8,128)(2,1)S(1)}, bf16[8,6,24,128]{3,2,1,0:T(8,128)(2,1)}, u32[]{:S(2)}) copy-start(bf16[8,6,24,128]{3,2,1,0:T(8,128)(2,1)} %param.6) | copy-start | bytes 884740
  0.0 10.3 %copy-start.5 = (s32[2]{0:T(128)S(1)}, s32[2]{0:T(128)}, u32[]{:S(2)}) copy-start(s32[2]{0:T(128)} %param.8) | copy-start | bytes 28
  0.0 17.0 %copy-start.3 = (bf16[128,256]{1,0:T(8,128)(2,1)S(1)}, bf16[128,256]{1,0:T(8,128)(2,1)}, u32[]{:S(2)}) copy-start(bf16[128,256]{1,0:T(8,128)(2,1)} %constant.33.clone.along_x) | copy-start | bytes 196612
  0.0 17.0 %copy-start.4 = (f32[6,24,128]{2,1,0:T(8,128)S(1)}, f32[6,24,128]{2,1,0:T(8,128)}, u32[]{:S(2)}) copy-start(f32[6,24,128]{2,1,0:T(8,128)} %param.7) | copy-start | bytes 221188
  0.0 15.3 %all-to-all-start = ((bf16[8,144,128]{2,1,0:T(8,128)(2,1)}), bf16[8,144,128]{2,1,0:T(8,128)(2,1)S(1)}, u32[]{:S(2)}, u32[]{:S(2)}) async-start(bf16[8,144,128]{2,1,0:T(8,128)(2,1)} %bitcast.10), calls=%async_computation | async-start | bytes 589824 | tf_op jit(solution)/shard_map/all_to_all | solution.py:222
  7.6 9.4 %copy-start.1 = (bf16[288,144]{1,0:T(8,128)(2,1)S(1)}, bf16[288,144]{1,0:T(8,128)(2,1)}, u32[]{:S(2)}) copy-start(bf16[288,144]{1,0:T(8,128)(2,1)} %constant.31.clone.inside) | copy-start | bytes 248836
  7.7 17.6 %collective-permute-start.2 = (bf16[8,144,128]{2,1,0:T(8,128)(2,1)S(1)}, bf16[8,144,128]{2,1,0:T(8,128)(2,1)S(1)}, u32[]{:S(2)}, u32[]{:S(2)}) collective-permute-start(bf16[8,144,128]{2,1,0:T(8,128)(2,1)S(1)} %bitcast.11), channel_id=1, source_target_pairs={{1,0},{2,1},{3,2},{4,3},{5,4},{6,5},{7,6},{0,7},{9,8},{10,9},{11,1... | collective-permute-start | bytes 884744 | tf_op jit(solution)/shard_map/ppermute | solution.py:208
  8.7 16.6 %collective-permute-start.3 = (bf16[8,144,128]{2,1,0:T(8,128)(2,1)S(1)}, bf16[8,144,128]{2,1,0:T(8,128)(2,1)S(1)}, u32[]{:S(2)}, u32[]{:S(2)}) collective-permute-start(bf16[8,144,128]{2,1,0:T(8,128)(2,1)S(1)} %bitcast.12), channel_id=1, source_target_pairs={{0,1},{1,2},{2,3},{3,4},{4,5},{5,6},{6,7},{7,0},{8,9},{9,10},{10,1... | collective-permute-start | bytes 884744 | tf_op jit(solution)/shard_map/ppermute | solution.py:208
  15.4 3.2 %collective-permute-start = (bf16[144,128]{1,0:T(8,128)(2,1)S(1)}, bf16[144,128]{1,0:T(8,128)(2,1)S(1)}, u32[]{:S(2)}, u32[]{:S(2)}) collective-permute-start(bf16[144,128]{1,0:T(8,128)(2,1)S(1)} %select_bitcast_fusion), channel_id=1, source_target_pairs={{0,32},{8,40},{16,48},{24,56},{32,0},{40,8},{48,16},{56,24},{64,96... | collective-permute-start | bytes 110600 | tf_op jit(solution)/shard_map/ppermute | solution.py:236
  17.0 8.2 %copy-start.2 = (bf16[288,288]{1,0:T(8,128)(2,1)S(1)}, bf16[288,288]{1,0:T(8,128)(2,1)}, u32[]{:S(2)}) copy-start(bf16[288,288]{1,0:T(8,128)(2,1)} %constant.32.clone.beside) | copy-start | bytes 497668
  18.6 8.1 %collective-permute-start.1 = (bf16[144,128]{1,0:T(8,128)(2,1)S(1)}, bf16[144,128]{1,0:T(8,128)(2,1)S(1)}, u32[]{:S(2)}, u32[]{:S(2)}) collective-permute-start(bf16[144,128]{1,0:T(8,128)(2,1)S(1)} %bitcast_add_fusion), channel_id=1, source_target_pairs={{0,128},{8,136},{16,144},{24,152},{32,160},{40,168},{48,176},{56,1... | collective-permute-start | bytes 110600 | tf_op jit(solution)/shard_map/ppermute | solution.py:237
  26.7 12.6 %collective-permute-start.4 = (bf16[3,144,128]{2,1,0:T(8,128)(2,1)S(1)}, bf16[3,144,128]{2,1,0:T(8,128)(2,1)S(1)}, u32[]{:S(2)}, u32[]{:S(2)}) collective-permute-start(bf16[3,144,128]{2,1,0:T(8,128)(2,1)S(1)} %pad_maximum_fusion), channel_id=1, source_target_pairs={{0,135},{1,0},{2,1},{3,2},{4,3},{5,4},{6,5},{7,6},{8,143},{9,8},{1... | collective-permute-start | bytes 331784 | tf_op jit(solution)/shard_map/ppermute | solution.py:216
  31.0 8.3 %collective-permute-start.5 = (bf16[3,144,128]{2,1,0:T(8,128)(2,1)S(1)}, bf16[3,144,128]{2,1,0:T(8,128)(2,1)S(1)}, u32[]{:S(2)}, u32[]{:S(2)}) collective-permute-start(bf16[3,144,128]{2,1,0:T(8,128)(2,1)S(1)} %pad_maximum_fusion), channel_id=1, source_target_pairs={{0,1},{1,2},{2,3},{3,4},{4,5},{5,6},{6,7},{7,128},{8,9},{9,10},{10... | collective-permute-start | bytes 331784 | tf_op jit(solution)/shard_map/ppermute | solution.py:216
  31.6 4.7 %collective-permute-start.6 = (bf16[144,128]{1,0:T(8,128)(2,1)S(1)}, bf16[144,128]{1,0:T(8,128)(2,1)S(1)}, u32[]{:S(2)}, u32[]{:S(2)}) collective-permute-start(bf16[144,128]{1,0:T(8,128)(2,1)S(1)} %add.27.slab_c), channel_id=1, source_target_pairs={{0,134},{1,135},{2,0},{3,1},{4,2},{5,3},{6,4},{7,5},{8,142},{9,143... | collective-permute-start | bytes 110600 | tf_op jit(solution)/shard_map/ppermute | solution.py:216
  35.3 4.0 %collective-permute-start.7 = (bf16[144,128]{1,0:T(8,128)(2,1)S(1)}, bf16[144,128]{1,0:T(8,128)(2,1)S(1)}, u32[]{:S(2)}, u32[]{:S(2)}) collective-permute-start(bf16[144,128]{1,0:T(8,128)(2,1)S(1)} %add.27.slab_c), channel_id=1, source_target_pairs={{0,2},{1,3},{2,4},{3,5},{4,6},{5,7},{6,128},{7,129},{8,10},{9,11},... | collective-permute-start | bytes 110600 | tf_op jit(solution)/shard_map/ppermute | solution.py:216
  40.9 15.0 %all-to-all-start.1 = ((bf16[16,144,128]{2,1,0:T(8,128)(2,1)}), bf16[16,144,128]{2,1,0:T(8,128)(2,1)S(1)}, u32[]{:S(2)}, u32[]{:S(2)}) async-start(bf16[16,144,128]{2,1,0:T(8,128)(2,1)} %owner.1), calls=%async_computation.1 | async-start | bytes 1179648 | tf_op jit(solution)/shard_map/all_to_all | solution.py:254
  45.0 9.7 %collective-permute-start.8 = (bf16[8,144,128]{2,1,0:T(8,128)(2,1)S(1)}, bf16[8,144,128]{2,1,0:T(8,128)(2,1)S(1)}, u32[]{:S(2)}, u32[]{:S(2)}) collective-permute-start(bf16[8,144,128]{2,1,0:T(8,128)(2,1)S(1)} %first.1.center), channel_id=1, source_target_pairs={{1,0},{2,1},{3,2},{4,3},{5,4},{6,5},{7,6},{0,7},{9,8},{10,9},{11,1... | collective-permute-start | bytes 884744 | tf_op jit(solution)/shard_map/ppermute | solution.py:208
  46.5 8.2 %collective-permute-start.9 = (bf16[8,144,128]{2,1,0:T(8,128)(2,1)S(1)}, bf16[8,144,128]{2,1,0:T(8,128)(2,1)S(1)}, u32[]{:S(2)}, u32[]{:S(2)}) collective-permute-start(bf16[8,144,128]{2,1,0:T(8,128)(2,1)S(1)} %first.1.center), channel_id=1, source_target_pairs={{0,1},{1,2},{2,3},{3,4},{4,5},{5,6},{6,7},{7,0},{8,9},{9,10},{10,1... | collective-permute-start | bytes 884744 | tf_op jit(solution)/shard_map/ppermute | solution.py:208
  56.3 3.2 %collective-permute-start.10 = (f32[16,128]{1,0:T(8,128)S(1)}, f32[16,128]{1,0:T(8,128)S(1)}, u32[]{:S(2)}, u32[]{:S(2)}) collective-permute-start(f32[16,128]{1,0:T(8,128)S(1)} %get-tuple-element.23), channel_id=1, source_target_pairs={{0,1},{1,0},{2,3},{3,2},{4,5},{5,4},{6,7},{7,6},{8,9},{9,8},{10,11... | collective-permute-start | bytes 24584 | tf_op jit(solution)/shard_map/ppermute | solution.py:263
  59.5 4.3 %collective-permute-start.11 = (f32[16,128]{1,0:T(8,128)S(1)}, f32[16,128]{1,0:T(8,128)S(1)}, u32[]{:S(2)}, u32[]{:S(2)}) collective-permute-start(f32[16,128]{1,0:T(8,128)S(1)} %add.28.gram), channel_id=1, source_target_pairs={{0,6},{1,7},{2,4},{3,5},{4,2},{5,3},{6,0},{7,1},{8,14},{9,15},{10,... | collective-permute-start | bytes 24584 | tf_op jit(solution)/shard_map/ppermute | solution.py:264
  60.3 3.4 %collective-permute-start.12 = (f32[16,128]{1,0:T(8,128)S(1)}, f32[16,128]{1,0:T(8,128)S(1)}, u32[]{:S(2)}, u32[]{:S(2)}) collective-permute-start(f32[16,128]{1,0:T(8,128)S(1)} %add.28.gram), channel_id=1, source_target_pairs={{0,2},{1,3},{2,0},{3,1},{4,6},{5,7},{6,4},{7,5},{8,10},{9,11},{10,... | collective-permute-start | bytes 24584 | tf_op jit(solution)/shard_map/ppermute | solution.py:264
  60.3 3.7 %collective-permute-start.13 = (f32[16,128]{1,0:T(8,128)S(1)}, f32[16,128]{1,0:T(8,128)S(1)}, u32[]{:S(2)}, u32[]{:S(2)}) collective-permute-start(f32[16,128]{1,0:T(8,128)S(1)} %add.28.gram), channel_id=1, source_target_pairs={{0,4},{1,5},{2,6},{3,7},{4,0},{5,1},{6,2},{7,3},{8,12},{9,13},{10,... | collective-permute-start | bytes 24584 | tf_op jit(solution)/shard_map/ppermute | solution.py:264

commit v7 on v6

--- a/solution.py
+++ b/solution.py
@@ -100,17 +100,17 @@
         out[s] = (2.0 * (inner[s] + value) - states[s].astype(f32)).astype(bf16)
 
 
-def owner_kernel(near_d, near_b, slab_e, slab_a, slab_c, diagonal, inside, beside, along_x, out):
+def owner_kernel(near_d, near_b, slab_e, slab_a, slab_c, raw_inner, diagonal, inside, beside, along_x, out):
     inside, beside, along_x = inside[...], beside[...], along_x[...]
-    middle = jnp.stack([near_b[0], slab_c[...], near_d[0]])
+    middle = jnp.stack([near_b[0], near_d[0]])
     before = jnp.stack([slab_a[...], near_b[0], slab_c[...]])
     after = jnp.stack([slab_c[...], near_d[0], slab_e[...]])
     outer = outer_part(before, after, beside)
     beside_diagonals = [diagonal_of(n[1].astype(f32) + n[2].astype(f32)) for n in (near_b, near_d)]
-    diagonals = [beside_diagonals[0], diagonal[...], beside_diagonals[1]]
-    inner = inner_part(middle, diagonals, inside, along_x)
+    inner = inner_part(middle, beside_diagonals, inside, along_x)
+    inner = [inner[0], raw_inner[0], inner[1]]
     first = [(i + o).astype(bf16)[None] for i, o in zip(inner, outer)]
-    value = inner_part(first[1], diagonals[1:2], inside, along_x)[0] + outer_part(first[0], first[2], beside)[0]
+    value = inner_part(first[1], [diagonal[...]], inside, along_x)[0] + outer_part(first[0], first[2], beside)[0]
     block = (2.0 * value - slab_c[...].astype(f32)).astype(bf16)
     for target in range(PLANE):
         out[target] = block
@@ -247,9 +247,13 @@
 
     resident = call(second_kernel, block, [vmem] * 5, after, before, inner, states, beside, name="second")
 
+    raw_inner = call(
+        second_inner_kernel, jax.ShapeDtypeStruct((1,) + cells, f32), [vmem] * 4, raw[None], diagonal, inside, along_x,
+        name="raw_inner",
+    )
     copies = call(
-        owner_kernel, jax.ShapeDtypeStruct((PLANE,) + cells, bf16), [vmem] * 9,
-        near_after, near_before, next_after, next_before, raw, diagonal, inside, beside, along_x, name="owner",
+        owner_kernel, jax.ShapeDtypeStruct((PLANE,) + cells, bf16), [vmem] * 10,
+        near_after, near_before, next_after, next_before, raw, raw_inner, diagonal, inside, beside, along_x, name="owner",
     )
     gathered = lax.all_to_all(copies, "band", 0, 0, axis_index_groups=groups)
     gram, owned = call(

time: 65.7 us -> 65.6 us (level)
    pallas_call x7 -> x8, Pallas kernels: 5.11 us -> 5.14 us  [call(): pl.pallas_call(kernel, out_shape=out_shape, in_specs=specs, out_specs=jax...]
where the time goes in v7:
time: 65.6 us; the launch traced here: 65.2 us
  starting transfers between devices  37.9 us (58%)
  waiting for transfers between devices  18.9 us (29%)
  Pallas kernels  5.14 us (8%)
  between operations  2.62 us (4%)
    ppermute x4, starting transfers between devices, along_z(): return lax.ppermute(values, ('band', 'dom'), pairs)  8.62 us
    ppermute x2, waiting for transfers between devices, both_ways(): lax.ppermute(values, 'dom', [(b, a) for a, b in ring])  7.86 us
    all_to_all x1, starting transfers between devices, on_device(): lax.all_to_all(states, 'band', 0, 0, axis_index_groups=spread_groups)  7.62 us
    ppermute x1, starting transfers between devices, on_device(): other = lax.ppermute(mine, 'band', [(i, i ^ PLANE) for i in range(bands)])  6.7 us
    pallas_call x8, Pallas kernels, call(): pl.pallas_call(kernel, out_shape=out_shape, in_specs=specs, out_specs=jax...  5.14 us
    all_to_all x1, starting transfers between devices, on_device(): gathered = lax.all_to_all(copies, 'band', 0, 0, axis_index_groups=groups)  4.14 us
    ppermute x3, starting transfers between devices, on_device(): lax.ppermute(gram, 'dom', [(i, i ^ s) for i in range(doms)])  3.55 us
    ppermute x4, waiting for transfers between devices, along_z(): return lax.ppermute(values, ('band', 'dom'), pairs)  3.34 us
  transfers between devices with their start and end apart: 16, of which 10 were waited for; matrix products, arithmetic and copies ran while one was open for 1% of the time, Pallas kernels for 3%

profile of v7, /device:TPU:1, one launch (start us, length us, event | category | flops | bytes accessed | tf_op | source)
XLA Modules:
  0.0 65.2 jit_solution(11132430123762403639)
XLA Ops:
  0.0 7.6 %all-to-all-start = ((bf16[8,144,128]{2,1,0:T(8,128)(2,1)}), bf16[8,144,128]{2,1,0:T(8,128)(2,1)S(1)}, u32[]{:S(2)}, u32[]{:S(2)}) async-start(bf16[8,144,128]{2,1,0:T(8,128)(2,1)} %bitcast.10), calls=%async_computation | async-start | bytes 589824 | tf_op jit(solution)/shard_map/all_to_all | solution.py:222
  7.7 1.0 %collective-permute-start.2 = (bf16[8,144,128]{2,1,0:T(8,128)(2,1)S(1)}, bf16[8,144,128]{2,1,0:T(8,128)(2,1)S(1)}, u32[]{:S(2)}, u32[]{:S(2)}) collective-permute-start(bf16[8,144,128]{2,1,0:T(8,128)(2,1)S(1)} %bitcast.11), channel_id=1, source_target_pairs={{1,0},{2,1},{3,2},{4,3},{5,4},{6,5},{7,6},{0,7},{9,8},{10,9},{11,1... | collective-permute-start | bytes 884744 | tf_op jit(solution)/shard_map/ppermute | solution.py:208
  8.7 1.6 %collective-permute-start.3 = (bf16[8,144,128]{2,1,0:T(8,128)(2,1)S(1)}, bf16[8,144,128]{2,1,0:T(8,128)(2,1)S(1)}, u32[]{:S(2)}, u32[]{:S(2)}) collective-permute-start(bf16[8,144,128]{2,1,0:T(8,128)(2,1)S(1)} %bitcast.12), channel_id=1, source_target_pairs={{0,1},{1,2},{2,3},{3,4},{4,5},{5,6},{6,7},{7,0},{8,9},{9,10},{10,1... | collective-permute-start | bytes 884744 | tf_op jit(solution)/shard_map/ppermute | solution.py:208
  10.3 0.6 fusion
  12.1 3.2 %all-to-all-done = bf16[8,144,128]{2,1,0:T(8,128)(2,1)S(1)} async-done(((bf16[8,144,128]{2,1,0:T(8,128)(2,1)}), bf16[8,144,128]{2,1,0:T(8,128)(2,1)S(1)}, u32[]{:S(2)}, u32[]{:S(2)}) %all-to-all-start) | async-done | bytes 294944 | tf_op jit(solution)/shard_map/all_to_all | solution.py:222
  15.4 0.4 collective-permute-start
  17.0 0.5 first_inner.1
  17.5 1.0 %collective-permute-done = bf16[144,128]{1,0:T(8,128)(2,1)S(1)} collective-permute-done((bf16[144,128]{1,0:T(8,128)(2,1)S(1)}, bf16[144,128]{1,0:T(8,128)(2,1)S(1)}, u32[]{:S(2)}, u32[]{:S(2)}) %collective-permute-start) | collective-permute-done | bytes 36896 | tf_op jit(solution)/shard_map/ppermute | solution.py:236
  18.6 6.7 %collective-permute-start.1 = (bf16[144,128]{1,0:T(8,128)(2,1)S(1)}, bf16[144,128]{1,0:T(8,128)(2,1)S(1)}, u32[]{:S(2)}, u32[]{:S(2)}) collective-permute-start(bf16[144,128]{1,0:T(8,128)(2,1)S(1)} %bitcast_add_fusion), channel_id=1, source_target_pairs={{0,128},{8,136},{16,144},{24,152},{32,160},{40,168},{48,176},{56,1... | collective-permute-start | bytes 110600 | tf_op jit(solution)/shard_map/ppermute | solution.py:237
  25.3 0.5 first.1.center
  25.7 0.9 %collective-permute-done.1 = bf16[144,128]{1,0:T(8,128)(2,1)S(1)} collective-permute-done((bf16[144,128]{1,0:T(8,128)(2,1)S(1)}, bf16[144,128]{1,0:T(8,128)(2,1)S(1)}, u32[]{:S(2)}, u32[]{:S(2)}) %collective-permute-start.1) | collective-permute-done | bytes 36896 | tf_op jit(solution)/shard_map/ppermute | solution.py:237
  26.7 4.3 %collective-permute-start.4 = (bf16[3,144,128]{2,1,0:T(8,128)(2,1)S(1)}, bf16[3,144,128]{2,1,0:T(8,128)(2,1)S(1)}, u32[]{:S(2)}, u32[]{:S(2)}) collective-permute-start(bf16[3,144,128]{2,1,0:T(8,128)(2,1)S(1)} %pad_maximum_fusion), channel_id=1, source_target_pairs={{0,135},{1,0},{2,1},{3,2},{4,3},{5,4},{6,5},{7,6},{8,143},{9,8},{1... | collective-permute-start | bytes 331784 | tf_op jit(solution)/shard_map/ppermute | solution.py:216
  31.0 0.6 collective-permute-start.5
  31.6 3.7 %collective-permute-start.6 = (bf16[144,128]{1,0:T(8,128)(2,1)S(1)}, bf16[144,128]{1,0:T(8,128)(2,1)S(1)}, u32[]{:S(2)}, u32[]{:S(2)}) collective-permute-start(bf16[144,128]{1,0:T(8,128)(2,1)S(1)} %add.27.slab_c), channel_id=1, source_target_pairs={{0,134},{1,135},{2,0},{3,1},{4,2},{5,3},{6,4},{7,5},{8,142},{9,143... | collective-permute-start | bytes 110600 | tf_op jit(solution)/shard_map/ppermute | solution.py:216
  35.5 0.5 second_inner.1.inner
  36.0 0.4 collective-permute-done.6.slab_e
  36.3 3.0 %collective-permute-done.7.slab_a = bf16[144,128]{1,0:T(8,128)(2,1)S(1)} collective-permute-done((bf16[144,128]{1,0:T(8,128)(2,1)S(1)}, bf16[144,128]{1,0:T(8,128)(2,1)S(1)}, u32[]{:S(2)}, u32[]{:S(2)}) %collective-permute-start.7) | collective-permute-done | bytes 36896 | tf_op jit(solution)/shard_map/ppermute | solution.py:216
  39.3 1.4 %owner.1 = bf16[16,144,128]{2,1,0:T(8,128)(2,1)} custom-call(bf16[3,144,128]{2,1,0:T(8,128)(2,1)S(1)} %collective-permute-done.4.near_d, bf16[3,144,128]{2,1,0:T(8,128)(2,1)S(1)} %collective-permute-done.5.near_b, bf16[144,128]{1,0:T(8,128)(2,1)S(1)} %collective-permute-done.6.slab_e, bf16[144,128]{1,0:T(8,128)(2,1)S(1)} %collective-permute-done.7.slab_a, ...), custom_call_target="tpu_custom_call" | custom-call | tf_op jit(solution)/shard_map/owner/pallas_call | solution.py:181
  40.7 4.1 %all-to-all-start.1 = ((bf16[16,144,128]{2,1,0:T(8,128)(2,1)}), bf16[16,144,128]{2,1,0:T(8,128)(2,1)S(1)}, u32[]{:S(2)}, u32[]{:S(2)}) async-start(bf16[16,144,128]{2,1,0:T(8,128)(2,1)} %owner.1), calls=%async_computation.1 | async-start | bytes 1179648 | tf_op jit(solution)/shard_map/all_to_all | solution.py:258
  44.9 1.5 %collective-permute-start.8 = (bf16[8,144,128]{2,1,0:T(8,128)(2,1)S(1)}, bf16[8,144,128]{2,1,0:T(8,128)(2,1)S(1)}, u32[]{:S(2)}, u32[]{:S(2)}) collective-permute-start(bf16[8,144,128]{2,1,0:T(8,128)(2,1)S(1)} %first.1.center), channel_id=1, source_target_pairs={{1,0},{2,1},{3,2},{4,3},{5,4},{6,5},{7,6},{0,7},{9,8},{10,9},{11,1... | collective-permute-start | bytes 884744 | tf_op jit(solution)/shard_map/ppermute | solution.py:208
  46.3 0.4 collective-permute-start.9
  46.7 7.9 %collective-permute-done.8.after = bf16[8,144,128]{2,1,0:T(8,128)(2,1)S(1)} collective-permute-done((bf16[8,144,128]{2,1,0:T(8,128)(2,1)S(1)}, bf16[8,144,128]{2,1,0:T(8,128)(2,1)S(1)}, u32[]{:S(2)}, u32[]{:S(2)}) %collective-permute-start.8) | collective-permute-done | bytes 294944 | tf_op jit(solution)/shard_map/ppermute | solution.py:208
  54.6 0.5 second.1.resident
  55.0 0.7 %all-to-all-done.1.gathered = bf16[16,144,128]{2,1,0:T(8,128)(2,1)S(1)} async-done(((bf16[16,144,128]{2,1,0:T(8,128)(2,1)}), bf16[16,144,128]{2,1,0:T(8,128)(2,1)S(1)}, u32[]{:S(2)}, u32[]{:S(2)}) %all-to-all-start.1) | async-done | bytes 589856 | tf_op jit(solution)/shard_map/all_to_all | solution.py:258
  55.7 0.3 gram.1
  56.1 2.4 %collective-permute-start.10 = (f32[16,128]{1,0:T(8,128)S(1)}, f32[16,128]{1,0:T(8,128)S(1)}, u32[]{:S(2)}, u32[]{:S(2)}) collective-permute-start(f32[16,128]{1,0:T(8,128)S(1)} %get-tuple-element.23), channel_id=1, source_target_pairs={{0,1},{1,0},{2,3},{3,2},{4,5},{5,4},{6,7},{7,6},{8,9},{9,8},{10,11... | collective-permute-start | bytes 24584 | tf_op jit(solution)/shard_map/ppermute | solution.py:267
  58.5 0.8 %collective-permute-done.10 = f32[16,128]{1,0:T(8,128)S(1)} collective-permute-done((f32[16,128]{1,0:T(8,128)S(1)}, f32[16,128]{1,0:T(8,128)S(1)}, u32[]{:S(2)}, u32[]{:S(2)}) %collective-permute-start.10) | collective-permute-done | bytes 8224 | tf_op jit(solution)/shard_map/ppermute | solution.py:267
  59.3 0.8 %collective-permute-start.11 = (f32[16,128]{1,0:T(8,128)S(1)}, f32[16,128]{1,0:T(8,128)S(1)}, u32[]{:S(2)}, u32[]{:S(2)}) collective-permute-start(f32[16,128]{1,0:T(8,128)S(1)} %add.28.gram), channel_id=1, source_target_pairs={{0,6},{1,7},{2,4},{3,5},{4,2},{5,3},{6,0},{7,1},{8,14},{9,15},{10,... | collective-permute-start | bytes 24584 | tf_op jit(solution)/shard_map/ppermute | solution.py:268
  60.1 2.7 %collective-permute-start.13 = (f32[16,128]{1,0:T(8,128)S(1)}, f32[16,128]{1,0:T(8,128)S(1)}, u32[]{:S(2)}, u32[]{:S(2)}) collective-permute-start(f32[16,128]{1,0:T(8,128)S(1)} %add.28.gram), channel_id=1, source_target_pairs={{0,4},{1,5},{2,6},{3,7},{4,0},{5,1},{6,2},{7,3},{8,12},{9,13},{10,... | collective-permute-start | bytes 24584 | tf_op jit(solution)/shard_map/ppermute | solution.py:268
  62.8 0.8 %collective-permute-done.11.part_a = f32[16,128]{1,0:T(8,128)S(1)} collective-permute-done((f32[16,128]{1,0:T(8,128)S(1)}, f32[16,128]{1,0:T(8,128)S(1)}, u32[]{:S(2)}, u32[]{:S(2)}) %collective-permute-start.11) | collective-permute-done | bytes 8224 | tf_op jit(solution)/shard_map/ppermute | solution.py:268
  63.6 0.3 collective-permute-done.13.part_c
  63.9 1.3 %project.1 = bf16[8,144,128]{2,1,0:T(8,128)(2,1)} custom-call(f32[16,128]{1,0:T(8,128)S(1)} %collective-permute-done.11.part_a, f32[16,128]{1,0:T(8,128)S(1)} %collective-permute-done.12.part_b, f32[16,128]{1,0:T(8,128)S(1)} %collective-permute-done.13.part_c, f32[16,128]{1,0:T(8,128)S(1)} %add.28.gram, bf16[128,2304]{1,0:T(8,128)(2,1)S(1)} %get-tuple-element.24.owned, ...), custom_call_target="tpu_custom_call" | custom-call | tf_op jit(solution)/shard_map/project/pallas_call | solution.py:181
  (26 shorter events, 0.3 us)
Async XLA Ops:
  0.0 7.6 %copy-start = (bf16[8,6,24,128]{3,2,1,0:T(8,128)(2,1)S(1)}, bf16[8,6,24,128]{3,2,1,0:T(8,128)(2,1)}, u32[]{:S(2)}) copy-start(bf16[8,6,24,128]{3,2,1,0:T(8,128)(2,1)} %param.6) | copy-start | bytes 884740
  0.0 10.3 %copy-start.5 = (s32[2]{0:T(128)S(1)}, s32[2]{0:T(128)}, u32[]{:S(2)}) copy-start(s32[2]{0:T(128)} %param.8) | copy-start | bytes 28
  0.0 17.0 %copy-start.2 = (bf16[128,256]{1,0:T(8,128)(2,1)S(1)}, bf16[128,256]{1,0:T(8,128)(2,1)}, u32[]{:S(2)}) copy-start(bf16[128,256]{1,0:T(8,128)(2,1)} %constant.33.clone.along_x) | copy-start | bytes 196612
  0.0 17.0 %copy-start.4 = (f32[6,24,128]{2,1,0:T(8,128)S(1)}, f32[6,24,128]{2,1,0:T(8,128)}, u32[]{:S(2)}) copy-start(f32[6,24,128]{2,1,0:T(8,128)} %param.7) | copy-start | bytes 221188
  0.0 15.3 %all-to-all-start = ((bf16[8,144,128]{2,1,0:T(8,128)(2,1)}), bf16[8,144,128]{2,1,0:T(8,128)(2,1)S(1)}, u32[]{:S(2)}, u32[]{:S(2)}) async-start(bf16[8,144,128]{2,1,0:T(8,128)(2,1)} %bitcast.10), calls=%async_computation | async-start | bytes 589824 | tf_op jit(solution)/shard_map/all_to_all | solution.py:222
  7.6 9.4 %copy-start.1 = (bf16[288,144]{1,0:T(8,128)(2,1)S(1)}, bf16[288,144]{1,0:T(8,128)(2,1)}, u32[]{:S(2)}) copy-start(bf16[288,144]{1,0:T(8,128)(2,1)} %constant.31.clone.inside) | copy-start | bytes 248836
  7.7 17.6 %collective-permute-start.2 = (bf16[8,144,128]{2,1,0:T(8,128)(2,1)S(1)}, bf16[8,144,128]{2,1,0:T(8,128)(2,1)S(1)}, u32[]{:S(2)}, u32[]{:S(2)}) collective-permute-start(bf16[8,144,128]{2,1,0:T(8,128)(2,1)S(1)} %bitcast.11), channel_id=1, source_target_pairs={{1,0},{2,1},{3,2},{4,3},{5,4},{6,5},{7,6},{0,7},{9,8},{10,9},{11,1... | collective-permute-start | bytes 884744 | tf_op jit(solution)/shard_map/ppermute | solution.py:208
  8.7 16.6 %collective-permute-start.3 = (bf16[8,144,128]{2,1,0:T(8,128)(2,1)S(1)}, bf16[8,144,128]{2,1,0:T(8,128)(2,1)S(1)}, u32[]{:S(2)}, u32[]{:S(2)}) collective-permute-start(bf16[8,144,128]{2,1,0:T(8,128)(2,1)S(1)} %bitcast.12), channel_id=1, source_target_pairs={{0,1},{1,2},{2,3},{3,4},{4,5},{5,6},{6,7},{7,0},{8,9},{9,10},{10,1... | collective-permute-start | bytes 884744 | tf_op jit(solution)/shard_map/ppermute | solution.py:208
  15.4 3.2 %collective-permute-start = (bf16[144,128]{1,0:T(8,128)(2,1)S(1)}, bf16[144,128]{1,0:T(8,128)(2,1)S(1)}, u32[]{:S(2)}, u32[]{:S(2)}) collective-permute-start(bf16[144,128]{1,0:T(8,128)(2,1)S(1)} %select_bitcast_fusion), channel_id=1, source_target_pairs={{0,32},{8,40},{16,48},{24,56},{32,0},{40,8},{48,16},{56,24},{64,96... | collective-permute-start | bytes 110600 | tf_op jit(solution)/shard_map/ppermute | solution.py:236
  17.0 8.2 %copy-start.3 = (bf16[288,288]{1,0:T(8,128)(2,1)S(1)}, bf16[288,288]{1,0:T(8,128)(2,1)}, u32[]{:S(2)}) copy-start(bf16[288,288]{1,0:T(8,128)(2,1)} %constant.32.clone.beside) | copy-start | bytes 497668
  18.6 8.1 %collective-permute-start.1 = (bf16[144,128]{1,0:T(8,128)(2,1)S(1)}, bf16[144,128]{1,0:T(8,128)(2,1)S(1)}, u32[]{:S(2)}, u32[]{:S(2)}) collective-permute-start(bf16[144,128]{1,0:T(8,128)(2,1)S(1)} %bitcast_add_fusion), channel_id=1, source_target_pairs={{0,128},{8,136},{16,144},{24,152},{32,160},{40,168},{48,176},{56,1... | collective-permute-start | bytes 110600 | tf_op jit(solution)/shard_map/ppermute | solution.py:237
  26.7 12.6 %collective-permute-start.4 = (bf16[3,144,128]{2,1,0:T(8,128)(2,1)S(1)}, bf16[3,144,128]{2,1,0:T(8,128)(2,1)S(1)}, u32[]{:S(2)}, u32[]{:S(2)}) collective-permute-start(bf16[3,144,128]{2,1,0:T(8,128)(2,1)S(1)} %pad_maximum_fusion), channel_id=1, source_target_pairs={{0,135},{1,0},{2,1},{3,2},{4,3},{5,4},{6,5},{7,6},{8,143},{9,8},{1... | collective-permute-start | bytes 331784 | tf_op jit(solution)/shard_map/ppermute | solution.py:216
  31.0 8.3 %collective-permute-start.5 = (bf16[3,144,128]{2,1,0:T(8,128)(2,1)S(1)}, bf16[3,144,128]{2,1,0:T(8,128)(2,1)S(1)}, u32[]{:S(2)}, u32[]{:S(2)}) collective-permute-start(bf16[3,144,128]{2,1,0:T(8,128)(2,1)S(1)} %pad_maximum_fusion), channel_id=1, source_target_pairs={{0,1},{1,2},{2,3},{3,4},{4,5},{5,6},{6,7},{7,128},{8,9},{9,10},{10... | collective-permute-start | bytes 331784 | tf_op jit(solution)/shard_map/ppermute | solution.py:216
  31.6 4.7 %collective-permute-start.6 = (bf16[144,128]{1,0:T(8,128)(2,1)S(1)}, bf16[144,128]{1,0:T(8,128)(2,1)S(1)}, u32[]{:S(2)}, u32[]{:S(2)}) collective-permute-start(bf16[144,128]{1,0:T(8,128)(2,1)S(1)} %add.27.slab_c), channel_id=1, source_target_pairs={{0,134},{1,135},{2,0},{3,1},{4,2},{5,3},{6,4},{7,5},{8,142},{9,143... | collective-permute-start | bytes 110600 | tf_op jit(solution)/shard_map/ppermute | solution.py:216
  35.3 4.0 %collective-permute-start.7 = (bf16[144,128]{1,0:T(8,128)(2,1)S(1)}, bf16[144,128]{1,0:T(8,128)(2,1)S(1)}, u32[]{:S(2)}, u32[]{:S(2)}) collective-permute-start(bf16[144,128]{1,0:T(8,128)(2,1)S(1)} %add.27.slab_c), channel_id=1, source_target_pairs={{0,2},{1,3},{2,4},{3,5},{4,6},{5,7},{6,128},{7,129},{8,10},{9,11},... | collective-permute-start | bytes 110600 | tf_op jit(solution)/shard_map/ppermute | solution.py:216
  40.7 15.0 %all-to-all-start.1 = ((bf16[16,144,128]{2,1,0:T(8,128)(2,1)}), bf16[16,144,128]{2,1,0:T(8,128)(2,1)S(1)}, u32[]{:S(2)}, u32[]{:S(2)}) async-start(bf16[16,144,128]{2,1,0:T(8,128)(2,1)} %owner.1), calls=%async_computation.1 | async-start | bytes 1179648 | tf_op jit(solution)/shard_map/all_to_all | solution.py:258
  44.9 9.7 %collective-permute-start.8 = (bf16[8,144,128]{2,1,0:T(8,128)(2,1)S(1)}, bf16[8,144,128]{2,1,0:T(8,128)(2,1)S(1)}, u32[]{:S(2)}, u32[]{:S(2)}) collective-permute-start(bf16[8,144,128]{2,1,0:T(8,128)(2,1)S(1)} %first.1.center), channel_id=1, source_target_pairs={{1,0},{2,1},{3,2},{4,3},{5,4},{6,5},{7,6},{0,7},{9,8},{10,9},{11,1... | collective-permute-start | bytes 884744 | tf_op jit(solution)/shard_map/ppermute | solution.py:208
  46.3 8.2 %collective-permute-start.9 = (bf16[8,144,128]{2,1,0:T(8,128)(2,1)S(1)}, bf16[8,144,128]{2,1,0:T(8,128)(2,1)S(1)}, u32[]{:S(2)}, u32[]{:S(2)}) collective-permute-start(bf16[8,144,128]{2,1,0:T(8,128)(2,1)S(1)} %first.1.center), channel_id=1, source_target_pairs={{0,1},{1,2},{2,3},{3,4},{4,5},{5,6},{6,7},{7,0},{8,9},{9,10},{10,1... | collective-permute-start | bytes 884744 | tf_op jit(solution)/shard_map/ppermute | solution.py:208
  56.1 3.2 %collective-permute-start.10 = (f32[16,128]{1,0:T(8,128)S(1)}, f32[16,128]{1,0:T(8,128)S(1)}, u32[]{:S(2)}, u32[]{:S(2)}) collective-permute-start(f32[16,128]{1,0:T(8,128)S(1)} %get-tuple-element.23), channel_id=1, source_target_pairs={{0,1},{1,0},{2,3},{3,2},{4,5},{5,4},{6,7},{7,6},{8,9},{9,8},{10,11... | collective-permute-start | bytes 24584 | tf_op jit(solution)/shard_map/ppermute | solution.py:267
  59.3 4.3 %collective-permute-start.11 = (f32[16,128]{1,0:T(8,128)S(1)}, f32[16,128]{1,0:T(8,128)S(1)}, u32[]{:S(2)}, u32[]{:S(2)}) collective-permute-start(f32[16,128]{1,0:T(8,128)S(1)} %add.28.gram), channel_id=1, source_target_pairs={{0,6},{1,7},{2,4},{3,5},{4,2},{5,3},{6,0},{7,1},{8,14},{9,15},{10,... | collective-permute-start | bytes 24584 | tf_op jit(solution)/shard_map/ppermute | solution.py:268
  60.1 3.5 %collective-permute-start.12 = (f32[16,128]{1,0:T(8,128)S(1)}, f32[16,128]{1,0:T(8,128)S(1)}, u32[]{:S(2)}, u32[]{:S(2)}) collective-permute-start(f32[16,128]{1,0:T(8,128)S(1)} %add.28.gram), channel_id=1, source_target_pairs={{0,2},{1,3},{2,0},{3,1},{4,6},{5,7},{6,4},{7,5},{8,10},{9,11},{10,... | collective-permute-start | bytes 24584 | tf_op jit(solution)/shard_map/ppermute | solution.py:268
  60.1 3.7 %collective-permute-start.13 = (f32[16,128]{1,0:T(8,128)S(1)}, f32[16,128]{1,0:T(8,128)S(1)}, u32[]{:S(2)}, u32[]{:S(2)}) collective-permute-start(f32[16,128]{1,0:T(8,128)S(1)} %add.28.gram), channel_id=1, source_target_pairs={{0,4},{1,5},{2,6},{3,7},{4,0},{5,1},{6,2},{7,3},{8,12},{9,13},{10,... | collective-permute-start | bytes 24584 | tf_op jit(solution)/shard_map/ppermute | solution.py:268
